TPU v7x, 128 devices: a whole 4x4x4 slice. The times are simulated.
128 devices in a mesh: branch: 8 (over x, core), wide: 16 (over y, z).
Axes of the slice: x: 4, y: 4, z: 4, core: 2. Of those that a mesh axis runs over, the one named last changes fastest.
Arguments:
- x_tokens: bfloat16 [1024, 4096], P(('branch', 'wide')), may hold values from -6 to 6
- out_grad: bfloat16 [1024, 4096], P(('branch', 'wide')), may hold values from -6 to 6
- expert_ids: int32 [1024, 2], P(('branch', 'wide')), may hold values from 0 to 7, all different within a row; in each aligned block of 8 rows (0 to 7, 8 to 15, ...) at most 3 rows name the same one
- gate_probs: float32 [1024, 2], P(('branch', 'wide')), may hold values from 0.2 to 1
- w_gate: bfloat16 [8, 6144, 4096], P('branch', 'wide'), may hold values from -0.09375 to 0.09375
- w_up: bfloat16 [8, 6144, 4096], P('branch', 'wide'), may hold values from -0.09375 to 0.09375
- w_down: bfloat16 [8, 6144, 4096], P('branch', 'wide'), may hold values from -0.078125 to 0.078125
- attn_out: bfloat16 [8, 4096, 4096], P('branch', None, 'wide'), may hold values from -6 to 6
Outputs:
- mixed: bfloat16 [1024, 4096], P(('branch', 'wide'))
- token_grad: bfloat16 [1024, 4096], P(('branch', 'wide'))
- merged_attn: bfloat16 [4096, 4096], P('branch', 'wide')
- grad_gate: bfloat16 [16, 8, 16, 24, 4096], P('wide', 'branch')
- grad_up: bfloat16 [16, 8, 16, 24, 4096], P('wide', 'branch')
- grad_down: bfloat16 [16, 8, 16, 24, 4096], P('wide', 'branch')
Inputs may be any that keep to these rules, and one draw needn't show every extreme that they name: `expert_ids`: each row names two different experts. In each aligned block of 8 rows (the tokens of one device) no expert is named by more than 3 routes.
All inputs are finite; a program needn't handle non-finite values.
Results may differ from a plain program's by a relative error of at most 0.017.
Values may be sent and summed in bfloat16 or wider, within the bound.
No kernel may reach another device: no remote copies, remote signals or barrier semaphores. Data moves between devices by JAX's collectives and lax.ppermute only.
A program may use at most 128 MiB of HBM per device.

v0:
```python
import jax
import jax.numpy as jnp
from jax import lax
from jax.sharding import PartitionSpec as P


def expert_pass(tokens_in, grads_in, gate_w, up_w, down_w):
    contract = (((1,), (1,)), ((), ()))
    over_rows = (((0,), (0,)), ((), ()))
    gate_val = lax.dot_general(tokens_in, gate_w, contract, preferred_element_type=jnp.float32)
    up_val = lax.dot_general(tokens_in, up_w, contract, preferred_element_type=jnp.float32)
    sigmoid_gate = jax.nn.sigmoid(gate_val)
    hidden = (gate_val * sigmoid_gate * up_val).astype(jnp.bfloat16)
    partial_out = jnp.dot(hidden, down_w, preferred_element_type=jnp.float32)
    hidden_grad = lax.dot_general(grads_in, down_w, contract, preferred_element_type=jnp.float32)
    gate_grad = (
        hidden_grad * up_val * sigmoid_gate * (1.0 + gate_val * (1.0 - sigmoid_gate))
    ).astype(jnp.bfloat16)
    up_grad = (hidden_grad * gate_val * sigmoid_gate).astype(jnp.bfloat16)
    partial_in = jnp.dot(gate_grad, gate_w, preferred_element_type=jnp.float32) + jnp.dot(
        up_grad, up_w, preferred_element_type=jnp.float32
    )
    grad_gate = lax.dot_general(
        gate_grad, tokens_in, over_rows, preferred_element_type=jnp.float32
    ).astype(jnp.bfloat16)
    grad_up = lax.dot_general(
        up_grad, tokens_in, over_rows, preferred_element_type=jnp.float32
    ).astype(jnp.bfloat16)
    grad_down = lax.dot_general(
        hidden, grads_in, over_rows, preferred_element_type=jnp.float32
    ).astype(jnp.bfloat16)
    return (partial_out, partial_in, grad_gate, grad_up, grad_down)


def attn_term(attn_local, factor):
    return attn_local.astype(jnp.float32) * factor


def route_tables(expert_ids, gate_probs, experts, capacity):
    token_total = expert_ids.shape[0]
    flat_ids = expert_ids.reshape(-1)
    marked = (flat_ids[:, None] == jnp.arange(experts, dtype=jnp.int32)[None, :]).astype(jnp.int32)
    before = jnp.cumsum(marked, axis=0) - marked
    slot_index = jnp.sum(before * marked, axis=1)
    target = flat_ids * capacity + slot_index
    chosen = (target[:, None] == jnp.arange(experts * capacity, dtype=jnp.int32)[None, :]).astype(
        jnp.float32
    )
    chosen = chosen.reshape(token_total, 2, experts * capacity)
    select_map = jnp.sum(chosen, axis=1)
    weighted = jnp.sum(chosen * gate_probs[:, :, None], axis=1)
    return (select_map, weighted)


def relay_pieces(first, second, third):
    return (
        lax.all_to_all(
            lax.all_to_all(first, "branch", split_axis=0, concat_axis=0, tiled=True),
            "wide",
            split_axis=0,
            concat_axis=0,
            tiled=True,
        ),
        lax.all_to_all(
            lax.all_to_all(second, "branch", split_axis=0, concat_axis=0, tiled=True),
            "wide",
            split_axis=0,
            concat_axis=0,
            tiled=True,
        ),
        lax.all_to_all(
            lax.all_to_all(third, "branch", split_axis=0, concat_axis=0, tiled=True),
            "wide",
            split_axis=0,
            concat_axis=0,
            tiled=True,
        ),
    )


def duplicate(buffer, copies):
    experts, capacity, features = buffer.shape
    spread = jnp.broadcast_to(buffer[:, None], (experts, copies, capacity, features))
    return spread.reshape(experts * copies, capacity, features)


def on_device(x_tokens, out_grad, expert_ids, gate_probs, w_gate, w_up, w_down, attn_out):
    experts = lax.axis_size("branch")
    wide_count = lax.axis_size("wide")
    copies = wide_count // experts
    features = x_tokens.shape[1]
    capacity = 3 * x_tokens.shape[0] // experts
    attn_local = attn_out[0]
    merged_attn = lax.psum_scatter(
        attn_term(attn_local, 1.0 / experts).astype(jnp.bfloat16),
        "branch",
        scatter_dimension=0,
        tiled=True,
    )
    select_map, weighted = route_tables(expert_ids, gate_probs, experts, capacity)
    over_tokens = (((0,), (0,)), ((), ()))
    send_tokens = lax.dot_general(
        select_map.astype(jnp.bfloat16), x_tokens, over_tokens, preferred_element_type=jnp.float32
    )
    send_tokens = send_tokens.astype(jnp.bfloat16).reshape(experts, capacity, features)
    send_grads = lax.dot_general(
        weighted,
        out_grad.astype(jnp.float32),
        over_tokens,
        precision=lax.Precision.HIGHEST,
        preferred_element_type=jnp.float32,
    )
    send_grads = send_grads.astype(jnp.bfloat16).reshape(experts, capacity, features)
    piece_rows = w_gate.shape[1] // wide_count
    piece_shape = (wide_count, piece_rows, features)
    gate_local, up_local, down_local = relay_pieces(
        w_gate[0].reshape(piece_shape), w_up[0].reshape(piece_shape), w_down[0].reshape(piece_shape)
    )
    arrived_tokens, arrived_grads = (
        lax.all_to_all(
            duplicate(send_tokens, copies), "wide", split_axis=0, concat_axis=0, tiled=True
        ),
        lax.all_to_all(
            duplicate(send_grads, copies), "wide", split_axis=0, concat_axis=0, tiled=True
        ),
    )
    all_tokens, all_grads = (
        lax.all_gather(arrived_tokens, "branch", axis=0, tiled=True),
        lax.all_gather(arrived_grads, "branch", axis=0, tiled=True),
    )
    partial_out, partial_in, grad_gate, grad_up, grad_down = expert_pass(
        all_tokens.reshape(-1, features),
        all_grads.reshape(-1, features),
        gate_local.reshape(-1, features),
        up_local.reshape(-1, features),
        down_local.reshape(-1, features),
    )
    shape_back = (experts * wide_count, capacity, features)
    summed_out, summed_in = (
        lax.psum_scatter(
            partial_out.reshape(shape_back), "branch", scatter_dimension=0, tiled=True
        ),
        lax.psum_scatter(partial_in.reshape(shape_back), "branch", scatter_dimension=0, tiled=True),
    )
    back_out, back_in = (
        lax.all_to_all(summed_out, "wide", split_axis=0, concat_axis=0, tiled=True),
        lax.all_to_all(summed_in, "wide", split_axis=0, concat_axis=0, tiled=True),
    )
    expert_out = jnp.sum(back_out.reshape(experts, copies, capacity, features), axis=1)
    expert_in = jnp.sum(back_in.reshape(experts, copies, capacity, features), axis=1)
    mixed = jnp.dot(
        weighted,
        expert_out.reshape(-1, features),
        precision=lax.Precision.HIGHEST,
        preferred_element_type=jnp.float32,
    ).astype(jnp.bfloat16)
    token_grad = jnp.dot(
        select_map,
        expert_in.reshape(-1, features),
        precision=lax.Precision.HIGHEST,
        preferred_element_type=jnp.float32,
    ).astype(jnp.bfloat16)
    layout = (1, 1, wide_count, piece_rows, features)
    return (
        mixed,
        token_grad,
        merged_attn,
        grad_gate.reshape(layout),
        grad_up.reshape(layout),
        grad_down.reshape(layout),
    )


def solution(mesh):
    in_specs = (
        P(("branch", "wide"), None),
        P(("branch", "wide"), None),
        P(("branch", "wide"), None),
        P(("branch", "wide"), None),
        P("branch", "wide", None),
        P("branch", "wide", None),
        P("branch", "wide", None),
        P("branch", None, "wide"),
    )
    out_specs = (
        P(("branch", "wide"), None),
        P(("branch", "wide"), None),
        P("branch", "wide"),
        P("wide", "branch", None, None, None),
        P("wide", "branch", None, None, None),
        P("wide", "branch", None, None, None),
    )
    return jax.shard_map(
        on_device, mesh=mesh, in_specs=in_specs, out_specs=out_specs, check_vma=False
    )
```

profile of v0, /device:TPU:1, one launch (start us, length us, event | category | flops | bytes accessed | tf_op | source)
XLA Modules:
  0.0 537.4 jit_solution(737816255367363912)
XLA Ops:
  7.2 0.9 copy.44
  9.4 0.9 convolution_convert_fusion.4
  10.3 1.1 broadcast_in_dim.8
  11.4 1.0 broadcast_in_dim.9
  12.4 8.6 %all-to-all-start = ((bf16[16,3,4096]{2,1,0:T(4,128)(2,1)}), bf16[16,3,4096]{2,1,0:T(4,128)(2,1)}, u32[]{:S(2)}, u32[]{:S(2)}) async-start(bf16[16,3,4096]{2,1,0:T(4,128)(2,1)} %bitcast.52), calls=%async_computation | async-start | bytes 1048576 | tf_op jit(solution)/shard_map/all_to_all | solution.py:120
  21.1 1.9 convolution_convert_fusion.3
  22.9 1.1 broadcast_in_dim.20
  24.0 7.4 %all-to-all-done = bf16[16,3,4096]{2,1,0:T(4,128)(2,1)} async-done(((bf16[16,3,4096]{2,1,0:T(4,128)(2,1)}), bf16[16,3,4096]{2,1,0:T(4,128)(2,1)}, u32[]{:S(2)}, u32[]{:S(2)}) %all-to-all-start) | async-done | bytes 393248 | tf_op jit(solution)/shard_map/all_to_all | solution.py:120
  31.6 12.6 %all_to_all.50 = bf16[16,3,4096]{2,1,0:T(4,128)(2,1)} all-to-all(bf16[16,3,4096]{2,1,0:T(4,128)(2,1)S(1)} %bitcast.53), channel_id=1, replica_groups=mesh['branch'=8,'wide'=16] {'wide'}, dimensions={0} | all-to-all | bytes 786432 | tf_op jit(solution)/shard_map/all_to_all | solution.py:123
  44.2 45.3 %all_to_all.51 = bf16[16,24,4096]{2,1,0:T(8,128)(2,1)} all-to-all(bf16[16,24,4096]{2,1,0:T(8,128)(2,1)S(1)} %bitcast.46), channel_id=1, replica_groups=mesh['branch'=8,'wide'=16] {'branch'}, dimensions={0} | all-to-all | bytes 6291456 | tf_op jit(solution)/shard_map/all_to_all | solution.py:72
  89.5 5.4 all-to-all-start.1
  94.9 2.1 copy.47
  97.0 48.2 %all-to-all-done.1 = bf16[16,24,4096]{2,1,0:T(8,128)(2,1)} async-done(((bf16[16,24,4096]{2,1,0:T(8,128)(2,1)}), bf16[16,24,4096]{2,1,0:T(8,128)(2,1)}, u32[]{:S(2)}, u32[]{:S(2)}) %all-to-all-start.1) | async-done | bytes 3145760 | tf_op jit(solution)/shard_map/all_to_all | solution.py:58
  145.3 42.3 %all_to_all.52 = bf16[16,24,4096]{2,1,0:T(8,128)(2,1)S(1)} all-to-all(bf16[16,24,4096]{2,1,0:T(8,128)(2,1)} %bitcast.48), channel_id=1, replica_groups=mesh['branch'=8,'wide'=16] {'branch'}, dimensions={0} | all-to-all | bytes 6291456 | tf_op jit(solution)/shard_map/all_to_all | solution.py:65
  187.6 4.5 all-to-all-start.2
  192.1 2.1 copy.53
  194.2 38.2 %all-to-all-done.2 = bf16[16,24,4096]{2,1,0:T(8,128)(2,1)} async-done(((bf16[16,24,4096]{2,1,0:T(8,128)(2,1)}), bf16[16,24,4096]{2,1,0:T(8,128)(2,1)}, u32[]{:S(2)}, u32[]{:S(2)}) %all-to-all-start.2) | async-done | bytes 3145760 | tf_op jit(solution)/shard_map/all_to_all | solution.py:57
  232.4 44.8 %all_to_all.53 = bf16[16,24,4096]{2,1,0:T(8,128)(2,1)} all-to-all(bf16[16,24,4096]{2,1,0:T(8,128)(2,1)S(1)} %all_to_all.52), channel_id=1, replica_groups=mesh['branch'=8,'wide'=16] {'wide'}, dimensions={0} | all-to-all | bytes 6291456 | tf_op jit(solution)/shard_map/all_to_all | solution.py:64
  277.2 4.5 all-to-all-start.6
  281.8 6.5 %copy.48 = bf16[128,3,4096]{2,1,0:T(4,128)(2,1)} copy(bf16[128,3,4096]{2,0,1:T(8,128)(2,1)} %all-gather.3.cloned.1.call-done) | data formatting | bytes 6291456 | tf_op jit(solution)/shard_map/all_gather | solution.py:128
  288.3 6.0 %reshape.86 = bf16[384,4096]{1,0:T(8,128)(2,1)S(1)} reshape(bf16[128,3,4096]{2,1,0:T(4,128)(2,1)} %copy.48) | data formatting | bytes 6291456 | tf_op jit(solution)/shard_map/reshape | solution.py:132
  294.3 6.5 %copy.54 = bf16[128,3,4096]{2,1,0:T(4,128)(2,1)} copy(bf16[128,3,4096]{2,0,1:T(8,128)(2,1)} %all-gather.5.cloned.1.call-done) | data formatting | bytes 6291456 | tf_op jit(solution)/shard_map/all_gather | solution.py:129
  300.9 7.4 %reshape.93 = bf16[384,4096]{1,0:T(8,128)(2,1)} reshape(bf16[128,3,4096]{2,1,0:T(4,128)(2,1)} %copy.54) | data formatting | bytes 6291456 | tf_op jit(solution)/shard_map/reshape | solution.py:133
  308.3 4.7 fusion.5
  312.9 2.6 fusion.6
  315.6 1.6 all-to-all-done.6
  317.2 5.7 %multiply_convert_fusion.1 = (bf16[384,384]{1,0:T(8,128)(2,1)S(1)}, bf16[384,384]{1,0:T(8,128)(2,1)S(1)}, bf16[384,384]{1,0:T(8,128)(2,1)}) fusion(f32[384,384]{1,0:T(8,128)} %fusion.5, f32[384,384]{1,0:T(8,128)} %fusion.6, bf16[384,4096]{1,0:T(8,128)(2,1)} %reshape.93, bf16[384,4096]{1,0:T(8,128)(2,1)} %bitcast.6), kind=kOutput, calls=%fused_computation.12 | convolution fusion | flops 1210318848 | bytes 8355840 | tf_op jit(solution)/shard_map/dot_general | solution.py:15
  322.9 3.8 fusion.7
  326.8 4.5 convolution_add_fusion
  331.2 9.1 %reshape.94 = f32[128,3,4096]{2,1,0:T(4,128)} reshape(f32[384,4096]{1,0:T(8,128)} %convolution_add_fusion) | data formatting | bytes 12582912 | tf_op jit(solution)/shard_map/reshape | solution.py:143
  340.7 1.8 dot_general.44
  342.5 6.5 %fusion.1 = f32[128,3,4096]{2,0,1:T(8,128)} fusion(bf16[384,4096,1]{1,0,2:T(8,128)(2,1)} %bitcast.7, bf16[128,3,384]{2,1,0:T(4,128)(2,1)} %dot_general.44), kind=kOutput, calls=%fused_computation.16 | convolution fusion | flops 1207959552 | bytes 9732096 | tf_op jit(solution)/shard_map/dot_general | solution.py:14
  349.1 3.3 fusion
  353.7 98.4 %all-reduce.3.cloned.1.call-done = f32[128,3,4096]{2,1,0:T(4,128)} async-done(((f32[128,3,4096]{2,1,0:T(4,128)}), f32[128,3,4096]{2,1,0:T(4,128)}) %all-reduce.3.cloned.1.call-update) | async-done | bytes 6291472
  452.0 2.5 constant_dynamic-slice_fusion
  454.6 6.8 %all-to-all-start.9 = ((f32[16,3,4096]{2,1,0:T(4,128)}), f32[16,3,4096]{2,1,0:T(4,128)}, u32[]{:S(2)}, u32[]{:S(2)}) async-start(f32[16,3,4096]{2,1,0:T(4,128)} %constant_dynamic-slice_fusion), calls=%async_computation.10 | async-start | bytes 2097152 | tf_op jit(solution)/shard_map/all_to_all | solution.py:147
  461.3 3.5 convolution_convert_fusion.2
  464.8 3.5 convolution_convert_fusion.1
  468.4 28.1 %reduce-scatter.3.cloned.1.call-done = f32[16,3,4096]{2,0,1:T(8,128)} async-done(((f32[128,3,4096]{2,0,1:T(8,128)}), f32[16,3,4096]{2,0,1:T(8,128)}) %reduce-scatter.3.cloned.1.call-update) | async-done | bytes 786448 | tf_op jit(solution)/shard_map/reduce_scatter | solution.py:140
  496.4 2.7 copy.50
  499.1 6.8 %all-to-all-start.7 = ((f32[16,3,4096]{2,1,0:T(4,128)}), f32[16,3,4096]{2,1,0:T(4,128)}, u32[]{:S(2)}, u32[]{:S(2)}) async-start(f32[16,3,4096]{2,1,0:T(4,128)} %copy.50), calls=%async_computation.8 | async-start | bytes 2097152 | tf_op jit(solution)/shard_map/all_to_all | solution.py:146
  505.9 3.5 convolution_convert_fusion
  509.4 1.6 bitcast_reduce_fusion
  511.1 1.0 convolution_convert_fusion.5
  512.1 9.0 %all-to-all-done.7 = f32[16,3,4096]{2,1,0:T(4,128)} async-done(((f32[16,3,4096]{2,1,0:T(4,128)}), f32[16,3,4096]{2,1,0:T(4,128)}, u32[]{:S(2)}, u32[]{:S(2)}) %all-to-all-start.7) | async-done | bytes 786464 | tf_op jit(solution)/shard_map/all_to_all | solution.py:146
  521.1 1.6 bitcast_reduce_fusion.1
  522.9 1.0 convolution_convert_fusion.6
  523.9 7.0 %reduce-scatter.5.cloned.1.call-done = bf16[512,256]{1,0:T(8,128)(2,1)} async-done(((bf16[4096,256]{1,0:T(8,128)(2,1)}), bf16[512,256]{1,0:T(8,128)(2,1)}) %reduce-scatter.5.cloned.1.call-update) | async-done | bytes 262160 | tf_op jit(solution)/shard_map/reduce_scatter | solution.py:94
  (45 shorter events, 3.1 us)
Async XLA Ops:
  7.2 2.3 copy-start
  7.2 37.1 %copy-start.5 = (bf16[1,384,4096]{2,1,0:T(8,128)(2,1)S(1)}, bf16[1,384,4096]{2,1,0:T(8,128)(2,1)}, u32[]{:S(2)}) copy-start(bf16[1,384,4096]{2,1,0:T(8,128)(2,1)} %param.14) | copy-start | bytes 9437188
  12.4 19.0 %all-to-all-start = ((bf16[16,3,4096]{2,1,0:T(4,128)(2,1)}), bf16[16,3,4096]{2,1,0:T(4,128)(2,1)}, u32[]{:S(2)}, u32[]{:S(2)}) async-start(bf16[16,3,4096]{2,1,0:T(4,128)(2,1)} %bitcast.52), calls=%async_computation | async-start | bytes 1048576 | tf_op jit(solution)/shard_map/all_to_all | solution.py:120
  89.5 55.7 %all-to-all-start.1 = ((bf16[16,24,4096]{2,1,0:T(8,128)(2,1)}), bf16[16,24,4096]{2,1,0:T(8,128)(2,1)}, u32[]{:S(2)}, u32[]{:S(2)}) async-start(bf16[16,24,4096]{2,1,0:T(8,128)(2,1)} %bitcast.47), calls=%async_computation.1 | async-start | bytes 6291456 | tf_op jit(solution)/shard_map/all_to_all | solution.py:58
  94.9 186.9 %all-gather.3.cloned.1.call-start = ((), (), s32[]{:S(2)}) async-start(), calls=%async_computation.12 | async-start | bytes 3538944 | tf_op jit(solution)/shard_map/all_gather | solution.py:128
  187.6 44.8 %all-to-all-start.2 = ((bf16[16,24,4096]{2,1,0:T(8,128)(2,1)}), bf16[16,24,4096]{2,1,0:T(8,128)(2,1)}, u32[]{:S(2)}, u32[]{:S(2)}) async-start(bf16[16,24,4096]{2,1,0:T(8,128)(2,1)} %all-to-all-done.1), calls=%async_computation.2 | async-start | bytes 6291456 | tf_op jit(solution)/shard_map/all_to_all | solution.py:57
  192.0 102.3 %all-gather.5.cloned.1.call-start = ((), (), s32[]{:S(2)}) async-start(), calls=%async_computation.14 | async-start | bytes 3538944 | tf_op jit(solution)/shard_map/all_gather | solution.py:129
  277.2 39.9 %all-to-all-start.6 = ((bf16[16,24,4096]{2,1,0:T(8,128)(2,1)}), bf16[16,24,4096]{2,1,0:T(8,128)(2,1)}, u32[]{:S(2)}, u32[]{:S(2)}) async-start(bf16[16,24,4096]{2,1,0:T(8,128)(2,1)} %all_to_all.51), calls=%async_computation.6 | async-start | bytes 6291456 | tf_op jit(solution)/shard_map/all_to_all | solution.py:71
  281.7 170.3 %all-reduce.3.cloned.1.call-start = ((), (), s32[]{:S(2)}) async-start(), calls=%async_computation.16 | async-start | bytes 16777216
  308.3 4.7 copy-start.3
  322.9 3.9 copy-start.7
  322.9 3.9 copy-start.4
  340.4 156.0 %reduce-scatter.3.cloned.1.call-start = ((), (), s32[]{:S(2)}) async-start(), calls=%async_computation.13 | async-start | bytes 7077888 | tf_op jit(solution)/shard_map/reduce_scatter | solution.py:140
  349.0 3.4 copy-start.9
  349.0 181.9 %reduce-scatter.5.cloned.1.call-start = ((), (), s32[]{:S(2)}) async-start(), calls=%async_computation.15 | async-start | bytes 2359296 | tf_op jit(solution)/shard_map/reduce_scatter | solution.py:94
  454.6 44.5 %all-to-all-start.9 = ((f32[16,3,4096]{2,1,0:T(4,128)}), f32[16,3,4096]{2,1,0:T(4,128)}, u32[]{:S(2)}, u32[]{:S(2)}) async-start(f32[16,3,4096]{2,1,0:T(4,128)} %constant_dynamic-slice_fusion), calls=%async_computation.10 | async-start | bytes 2097152 | tf_op jit(solution)/shard_map/all_to_all | solution.py:147
  461.3 3.5 copy-start.8
  468.3 37.5 %copy-start.2 = (bf16[384,4096]{1,0:T(8,128)(2,1)S(1)}, bf16[384,4096]{1,0:T(8,128)(2,1)}, u32[]{:S(2)}) copy-start(bf16[384,4096]{1,0:T(8,128)(2,1)} %reshape.93) | copy-start | bytes 9437188
  468.3 37.5 %copy-start.6 = (bf16[384,384]{1,0:T(8,128)(2,1)S(1)}, bf16[384,384]{1,0:T(8,128)(2,1)}, u32[]{:S(2)}) copy-start(bf16[384,384]{1,0:T(8,128)(2,1)} %get-tuple-element.10) | copy-start | bytes 884740
  499.1 22.0 %all-to-all-start.7 = ((f32[16,3,4096]{2,1,0:T(4,128)}), f32[16,3,4096]{2,1,0:T(4,128)}, u32[]{:S(2)}, u32[]{:S(2)}) async-start(f32[16,3,4096]{2,1,0:T(4,128)} %copy.50), calls=%async_computation.8 | async-start | bytes 2097152 | tf_op jit(solution)/shard_map/all_to_all | solution.py:146
  505.9 25.0 %copy-start.1 = (bf16[8,4096]{1,0:T(8,128)(2,1)S(1)}, bf16[8,4096]{1,0:T(8,128)(2,1)}, u32[]{:S(2)}) copy-start(bf16[8,4096]{1,0:T(8,128)(2,1)} %param.8) | copy-start | bytes 196612
Sparse Core Ops, SparseCore 0:
  98.0 39.8 all-gather.2
  195.2 28.0 all-gather.4
  340.5 111.4 all-reduce.2
  454.3 42.0 reduce-scatter.2
  499.2 31.6 reduce-scatter.4
where the time goes:
time: 541 us; the launch traced here: 537 us
  waiting for transfers between devices  238 us (44%)
  blocking collectives  145 us (27%)
  local copies, waits for them, and re-layouts  52.3 us (10%)
  matrix products  43 us (8%)
  starting transfers between devices  36.9 us (7%)
  between operations  14.6 us (3%)
  other arithmetic  7.55 us (1%)
    unnamed x6, waiting for transfers between devices  98.4 us
    all_to_all x1, waiting for transfers between devices, relay_pieces(): lax.all_to_all(first, 'branch', split_axis=0, concat_axis=0, tiled=True)  48.2 us
    all_to_all x1, blocking collectives, relay_pieces(): lax.all_to_all(third, 'branch', split_axis=0, concat_axis=0, tiled=True)  45.3 us
    all_to_all x1, blocking collectives, relay_pieces(): lax.all_to_all(lax.all_to_all(second, 'branch', split_axis=0, concat_axis...  44.8 us
    all_to_all x1, blocking collectives, relay_pieces(): lax.all_to_all(second, 'branch', split_axis=0, concat_axis=0, tiled=True)  42.3 us
    all_to_all x1, waiting for transfers between devices, relay_pieces(): lax.all_to_all(lax.all_to_all(first, 'branch', split_axis=0, concat_axis=...  38.2 us
    reduce_scatter x1, waiting for transfers between devices, on_device(): lax.psum_scatter(partial_out.reshape(shape_back), 'branch', scatter_dimen...  28.1 us
    all_to_all x1, blocking collectives, on_device(): lax.all_to_all(duplicate(send_grads, copies), 'wide', split_axis=0, conca...  12.6 us
  transfers between devices with their start and end apart: 11, of which 8 were waited for; matrix products, arithmetic and copies ran while one was open for 14% of the time, Pallas kernels for 0%

commit v1 on v0

v1 whole, which is shorter than its diff:
```python
import jax
import jax.numpy as jnp
from jax import lax
from jax.experimental import pallas as pl
from jax.experimental.pallas import tpu as pltpu
from jax.sharding import PartitionSpec as P

F32 = jnp.float32
BF16 = jnp.bfloat16
CAP = 3
LAST = (((1,), (1,)), ((), ()))
FIRST = (((0,), (0,)), ((), ()))
PARAMS = pltpu.CompilerParams(vmem_limit_bytes=56 * 1024 * 1024)


def select_kernel(pick_ref, scale_ref, rows_ref, xb_ref, gb_ref, xe_ref, ge_ref):
    features = rows_ref.shape[-1]
    parts = []
    for u in range(rows_ref.shape[1]):
        rows = rows_ref[:, u].reshape(-1, features)
        got = jnp.dot(pick_ref[u], rows, preferred_element_type=F32)
        parts.append(got * scale_ref[u])
    height = parts[0].shape[0] // 4
    for n, ref in enumerate((xb_ref, gb_ref, xe_ref, ge_ref)):
        both = [part[n * height : (n + 1) * height] for part in parts]
        ref[...] = jnp.concatenate(both, axis=0).astype(BF16)


def select_rows(pick, scale, rows):
    groups, picked, depth = pick.shape
    outer, _, per_block, features = rows.shape
    height = picked // 4
    shape = jax.ShapeDtypeStruct((groups * height, features), BF16)
    spec = pl.BlockSpec((2 * height, features), lambda i: (i, 0))
    return pl.pallas_call(
        select_kernel,
        grid=(groups // 2,),
        in_specs=[
            pl.BlockSpec((2, picked, depth), lambda i: (i, 0, 0)),
            pl.BlockSpec((2, picked, 1), lambda i: (i, 0, 0)),
            pl.BlockSpec((outer, 2, per_block, features), lambda i: (0, i, 0, 0)),
        ],
        out_specs=[spec] * 4,
        out_shape=[shape] * 4,
        compiler_params=PARAMS,
        name="select_rows",
    )(pick, scale, rows)


def forward_kernel(x_ref, wg_ref, wu_ref, wd_ref, gate_ref, up_ref, hid_ref, out_ref, acc):
    step = pl.program_id(0)
    gate = lax.dot_general(wg_ref[...], x_ref[...], LAST, preferred_element_type=F32)
    up = lax.dot_general(wu_ref[...], x_ref[...], LAST, preferred_element_type=F32)
    gate_ref[...] = gate
    up_ref[...] = up
    hid = (gate * jax.nn.sigmoid(gate) * up).astype(BF16)
    hid_ref[...] = hid
    part = lax.dot_general(hid, wd_ref[...], FIRST, preferred_element_type=F32)

    @pl.when(step == 0)
    def _():
        acc[...] = part

    @pl.when(step == pl.num_programs(0) - 1)
    def _():
        out_ref[...] = (acc[...] + part).astype(BF16)


def forward(x, wg, wu, wd):
    slots, features = x.shape
    hidden = wg.shape[0]
    tile = hidden // 2
    wspec = pl.BlockSpec((tile, features), lambda i: (i, 0))
    tspec = pl.BlockSpec((tile, slots), lambda i: (i, 0))
    whole = pl.BlockSpec((slots, features), lambda i: (0, 0))
    return pl.pallas_call(
        forward_kernel,
        grid=(2,),
        in_specs=[whole, wspec, wspec, wspec],
        out_specs=[tspec, tspec, tspec, whole],
        out_shape=[
            jax.ShapeDtypeStruct((hidden, slots), F32),
            jax.ShapeDtypeStruct((hidden, slots), F32),
            jax.ShapeDtypeStruct((hidden, slots), BF16),
            jax.ShapeDtypeStruct((slots, features), BF16),
        ],
        scratch_shapes=[pltpu.VMEM((slots, features), F32)],
        compiler_params=PARAMS,
        cost_estimate=pl.CostEstimate(
            flops=6 * slots * features * hidden,
            bytes_accessed=18 * 1024 * 1024,
            transcendentals=slots * hidden,
        ),
        name="expert_forward",
    )(x, wg, wu, wd)


def backward_kernel(
    g_ref, gate_ref, up_ref, hid_ref, wg_ref, wu_ref, wd_ref, send_ref, out_ref, acc
):
    step = pl.program_id(0)
    gate = gate_ref[...]
    up = up_ref[...]
    back = lax.dot_general(wd_ref[...], g_ref[...], LAST, preferred_element_type=F32)
    sig = jax.nn.sigmoid(gate)
    gate_grad = back * up * sig * (1.0 + gate * (1.0 - sig))
    up_grad = back * gate * sig
    pieces, stacked, slots = send_ref.shape
    rows = stacked // 3
    joined = jnp.concatenate(
        [
            gate_grad.reshape(pieces, rows, slots),
            up_grad.reshape(pieces, rows, slots),
            hid_ref[...].astype(F32).reshape(pieces, rows, slots),
        ],
        axis=1,
    )
    send_ref[...] = joined.astype(BF16)
    part = lax.dot_general(
        gate_grad.astype(BF16), wg_ref[...], FIRST, preferred_element_type=F32
    ) + lax.dot_general(up_grad.astype(BF16), wu_ref[...], FIRST, preferred_element_type=F32)

    @pl.when(step == 0)
    def _():
        acc[...] = part

    @pl.when(step == pl.num_programs(0) - 1)
    def _():
        out_ref[...] = (acc[...] + part).astype(BF16)


def backward(g, gate, up, hid, wg, wu, wd, pieces):
    slots, features = g.shape
    hidden = wg.shape[0]
    tile = hidden // 2
    wspec = pl.BlockSpec((tile, features), lambda i: (i, 0))
    tspec = pl.BlockSpec((tile, slots), lambda i: (i, 0))
    whole = pl.BlockSpec((slots, features), lambda i: (0, 0))
    stacked = 3 * hidden // pieces
    return pl.pallas_call(
        backward_kernel,
        grid=(2,),
        in_specs=[whole, tspec, tspec, tspec, wspec, wspec, wspec],
        out_specs=[pl.BlockSpec((pieces // 2, stacked, slots), lambda i: (i, 0, 0)), whole],
        out_shape=[
            jax.ShapeDtypeStruct((pieces, stacked, slots), BF16),
            jax.ShapeDtypeStruct((slots, features), BF16),
        ],
        scratch_shapes=[pltpu.VMEM((slots, features), F32)],
        compiler_params=PARAMS,
        cost_estimate=pl.CostEstimate(
            flops=6 * slots * features * hidden,
            bytes_accessed=18 * 1024 * 1024,
            transcendentals=slots * hidden,
        ),
        name="expert_backward",
    )(g, gate, up, hid, wg, wu, wd)


def weights_kernel(lhs_ref, x_ref, g_ref, gate_ref, up_ref, down_ref):
    pieces, stacked, slots = lhs_ref.shape
    rows = stacked // 3
    lhs = lhs_ref[...].astype(F32)

    def part(n):
        return lhs[:, n * rows : (n + 1) * rows].reshape(pieces * rows, slots).astype(BF16)

    for n, (src, dst) in enumerate(((x_ref, gate_ref), (x_ref, up_ref), (g_ref, down_ref))):
        dst[...] = jnp.dot(part(n), src[...], preferred_element_type=F32).astype(BF16)


def weight_grads(lhs, x, g):
    pieces, stacked, slots = lhs.shape
    features = x.shape[1]
    rows = stacked // 3
    group = 4
    whole = pl.BlockSpec((slots, features), lambda i: (0, 0))
    ospec = pl.BlockSpec((group * rows, features), lambda i: (i, 0))
    oshape = jax.ShapeDtypeStruct((pieces * rows, features), BF16)
    return pl.pallas_call(
        weights_kernel,
        grid=(pieces // group,),
        in_specs=[pl.BlockSpec((group, stacked, slots), lambda i: (i, 0, 0)), whole, whole],
        out_specs=[ospec] * 3,
        out_shape=[oshape] * 3,
        compiler_params=PARAMS,
        cost_estimate=pl.CostEstimate(
            flops=6 * slots * features * pieces * rows,
            bytes_accessed=16 * 1024 * 1024,
            transcendentals=0,
        ),
        name="weight_grads",
    )(lhs, x, g)


def route_pick(ids, probs, expert):
    named = ids == expert
    mine = jnp.any(named, axis=2)
    weight = jnp.sum(jnp.where(named, probs, 0.0), axis=2)
    tokens = ids.shape[1]
    earlier = jnp.arange(tokens)[:, None] < jnp.arange(tokens)[None, :]
    slot = jnp.sum(mine[:, :, None] & earlier[None], axis=1)
    chosen = mine[:, None, :] & (slot[:, None, :] == jnp.arange(CAP)[None, :, None])
    return chosen, jnp.sum(jnp.where(chosen, weight[:, None, :], 0.0), axis=2)


def exchange(value, axis):
    return lax.all_to_all(value, axis, split_axis=0, concat_axis=0, tiled=True)


def on_device(x_tokens, out_grad, expert_ids, gate_probs, w_gate, w_up, w_down, attn_out):
    experts = lax.axis_size("branch")
    wide = lax.axis_size("wide")
    blocks = experts * wide
    tokens, features = x_tokens.shape
    both = ("branch", "wide")
    branch_index = lax.axis_index("branch")
    wide_index = lax.axis_index("wide")

    gathered = lax.all_gather(
        jnp.concatenate([x_tokens, out_grad], axis=0), both, axis=0, tiled=True
    )
    gathered = gathered.reshape(experts, wide, 2 * tokens, features)

    meta = jnp.concatenate([expert_ids.astype(F32), gate_probs], axis=1)
    meta = jnp.pad(meta, ((0, 0), (0, 124)))
    meta = exchange(jnp.broadcast_to(meta[None], (blocks,) + meta.shape), both)
    ids = meta[:, :, 0:2].astype(jnp.int32)
    probs = meta[:, :, 2:4]

    attn = exchange(attn_out[0].reshape(experts, -1, attn_out.shape[2]), "branch")
    merged_attn = (jnp.sum(attn.astype(F32), axis=0) * (1.0 / experts)).astype(BF16)

    same = jnp.eye(experts, dtype=jnp.bool_)
    picks, scales = [], []
    for expert in (branch_index, wide_index // (wide // experts)):
        chosen, weight = route_pick(ids, probs, expert)
        chosen = chosen.reshape(experts, wide, CAP, tokens).transpose(1, 0, 2, 3)
        weight = weight.reshape(experts, wide, CAP).transpose(1, 0, 2).reshape(wide, experts * CAP)
        spread = chosen[:, :, :, None, None, :] & same[None, :, None, :, None, None]
        for kind in range(2):
            which = (jnp.arange(2) == kind)[None, None, None, None, :, None]
            picks.append((spread & which).reshape(wide, experts * CAP, experts * 2 * tokens))
            scales.append(weight if kind else jnp.ones_like(weight))
    pick = jnp.concatenate(picks, axis=1).astype(BF16)
    scale = jnp.concatenate(scales, axis=1)[:, :, None]
    xb, gb, xe, ge = select_rows(pick, scale, gathered)

    gate, up, hid, part_out = forward(xb, w_gate[0], w_up[0], w_down[0])
    send, part_in = backward(gb, gate, up, hid, w_gate[0], w_up[0], w_down[0], wide)

    def reduced(part):
        got = exchange(part.reshape(wide, experts * CAP, features), "wide")
        return jnp.sum(got.astype(F32), axis=0)

    sum_out = reduced(part_out)
    relayed = exchange(exchange(send, "branch"), "wide")
    sum_in = reduced(part_in)
    grad_gate, grad_up, grad_down = weight_grads(relayed, xe, ge)

    back = jnp.concatenate(
        [sum_out.reshape(experts, CAP, features), sum_in.reshape(experts, CAP, features)], axis=1
    )
    back = exchange(back.reshape(experts, 8 * CAP, features // 4), "branch")
    back = back.reshape(experts, 2, CAP, features)

    eids = expert_ids[None]
    own = [route_pick(eids, gate_probs[None], e)[0][0] for e in range(experts)]
    own = jnp.stack(own)
    named = expert_ids[None] == jnp.arange(experts)[:, None, None]
    own_weight = jnp.sum(jnp.where(named, gate_probs[None], 0.0), axis=2)
    chosen = own.astype(F32)
    mixed = jnp.sum(
        (chosen * own_weight[:, None, :])[:, :, :, None] * back[:, 0][:, :, None, :], axis=(0, 1)
    ).astype(BF16)
    token_grad = jnp.sum(chosen[:, :, :, None] * back[:, 1][:, :, None, :], axis=(0, 1)).astype(
        BF16
    )
    layout = (1, 1, wide, w_gate.shape[1] // wide, features)
    return (
        mixed,
        token_grad,
        merged_attn,
        grad_gate.reshape(layout),
        grad_up.reshape(layout),
        grad_down.reshape(layout),
    )


def solution(mesh):
    in_specs = (
        P(("branch", "wide"), None),
        P(("branch", "wide"), None),
        P(("branch", "wide"), None),
        P(("branch", "wide"), None),
        P("branch", "wide", None),
        P("branch", "wide", None),
        P("branch", "wide", None),
        P("branch", None, "wide"),
    )
    out_specs = (
        P(("branch", "wide"), None),
        P(("branch", "wide"), None),
        P("branch", "wide"),
        P("wide", "branch", None, None, None),
        P("wide", "branch", None, None, None),
        P("wide", "branch", None, None, None),
    )
    return jax.shard_map(
        on_device, mesh=mesh, in_specs=in_specs, out_specs=out_specs, check_vma=False
    )
```

time: 541 us -> 299 us (0.55)
  waiting for transfers between devices: 238 us -> 110 us
  blocking collectives: 145 us -> 62.7 us
  Pallas kernels: 0 us -> 52.7 us
  matrix products: 43 us -> 0 us
  local copies, waits for them, and re-layouts: 52.3 us -> 10.5 us
    unnamed x6 -> x1, waiting for transfers between devices: 98.4 us -> 0.02 us
    all_to_all x4 -> x2, blocking collectives: 145 us -> 62.7 us  [exchange(): return lax.all_to_all(value, axis, split_axis=0, concat_axis=0, tiled=True)]
    all_gather x2 -> x1, waiting for transfers between devices: 0.04 us -> 57 us  [on_device(): lax.all_gather(jnp.concatenate([x_tokens, out_grad], axis=0), both, axis=...]
    pallas_call x0 -> x4, Pallas kernels: none -> 52.7 us  [the longest x1 14.1 us: select_rows(): pl.pallas_call(select_kernel, grid=(groups // 2,), in_specs=[pl.BlockSpec...]
    all_to_all x6 -> x5, waiting for transfers between devices: 104 us -> 52.9 us  [exchange(): return lax.all_to_all(value, axis, split_axis=0, concat_axis=0, tiled=True)]
    dot_general x13 -> x0, matrix products: 43 us -> none  [the longest x1 6.46 us: expert_pass(): partial_out = jnp.dot(hidden, down_w, preferred_element_type=jnp.float32)]
    reduce_scatter x2 -> x0, waiting for transfers between devices: 35.1 us -> none  [the longest x1 28.1 us: on_device(): lax.psum_scatter(partial_out.reshape(shape_back), 'branch', scatter_dimen...]
    reshape x5 -> x10, local copies, waits for them, and re-layouts: 22.9 us -> 3.89 us  [the longest x1 1.13 us: on_device(): back = exchange(back.reshape(experts, 8 * CAP, features // 4), 'branch')]
  transfers between devices with their start and end apart: 11 -> 6, of which waited for: 8 -> 4; matrix products, arithmetic and copies ran while one was open for 14% -> 6% of each run, Pallas kernels for 0% -> 18%
where the time goes in v1:
time: 299 us
  waiting for transfers between devices  110 us (37%)
  blocking collectives  62.7 us (21%)
  Pallas kernels  52.7 us (18%)
  starting transfers between devices  35.9 us (12%)
  between operations  14.3 us (5%)
  other arithmetic  12.8 us (4%)
  local copies, waits for them, and re-layouts  10.5 us (4%)
    all_to_all x2, blocking collectives, exchange(): return lax.all_to_all(value, axis, split_axis=0, concat_axis=0, tiled=True)  62.7 us
    all_gather x1, waiting for transfers between devices, on_device(): lax.all_gather(jnp.concatenate([x_tokens, out_grad], axis=0), both, axis=...  57 us
    all_to_all x5, waiting for transfers between devices, exchange(): return lax.all_to_all(value, axis, split_axis=0, concat_axis=0, tiled=True)  52.9 us
    all_to_all x5, starting transfers between devices, exchange(): return lax.all_to_all(value, axis, split_axis=0, concat_axis=0, tiled=True)  35.8 us
    pallas_call x1, Pallas kernels, select_rows(): pl.pallas_call(select_kernel, grid=(groups // 2,), in_specs=[pl.BlockSpec...  14.1 us
    pallas_call x1, Pallas kernels, backward(): pl.pallas_call(backward_kernel, grid=(2,), in_specs=[whole, tspec, tspec,...  13.6 us
    pallas_call x1, Pallas kernels, forward(): pl.pallas_call(forward_kernel, grid=(2,), in_specs=[whole, wspec, wspec,...  13.4 us
    pallas_call x1, Pallas kernels, weight_grads(): pl.pallas_call(weights_kernel, grid=(pieces // group,), in_specs=[pl.Bloc...  11.5 us
  transfers between devices with their start and end apart: 6, of which 4 were waited for; matrix products, arithmetic and copies ran while one was open for 6% of the time, Pallas kernels for 18%

profile of v1, /device:TPU:1, one launch (start us, length us, event | category | flops | bytes accessed | tf_op | source)
XLA Modules:
  0.0 298.6 jit_solution(8215303139494244235)
XLA Ops:
  7.2 1.5 pad_maximum_fusion.1
  8.8 0.7 convert_element_type.138
  9.5 0.7 pad_maximum_fusion.2
  10.2 0.8 broadcast_in_dim.37
  11.1 11.5 %all-to-all-start = ((f32[128,8,128]{2,1,0:T(8,128)}), f32[128,8,128]{2,1,0:T(8,128)S(1)}, u32[]{:S(2)}, u32[]{:S(2)}) async-start(f32[128,8,128]{2,1,0:T(8,128)} %broadcast_in_dim.37), calls=%async_computation | async-start | bytes 1048576 | tf_op jit(solution)/shard_map/all_to_all | solution.py:208
  22.7 0.1 and.504
  22.9 0.1 and.508
  23.0 13.6 %all-to-all-done = f32[128,8,128]{2,1,0:T(8,128)S(1)} async-done(((f32[128,8,128]{2,1,0:T(8,128)}), f32[128,8,128]{2,1,0:T(8,128)S(1)}, u32[]{:S(2)}, u32[]{:S(2)}) %all-to-all-start) | async-done | bytes 524320 | tf_op jit(solution)/shard_map/all_to_all | solution.py:208
  36.6 4.7 %all-to-all-start.4 = ((bf16[8,512,256]{2,1,0:T(8,128)(2,1)}), bf16[8,512,256]{2,1,0:T(8,128)(2,1)S(1)}, u32[]{:S(2)}, u32[]{:S(2)}) async-start(bf16[8,512,256]{2,1,0:T(8,128)(2,1)} %bitcast.49), calls=%async_computation.4 | async-start | bytes 4194304 | tf_op jit(solution)/shard_map/all_to_all | solution.py:208
  41.3 0.9 fusion.20
  42.2 1.2 copy.130
  43.4 0.2 copy.131
  44.6 1.2 copy.129.scale_ref
  45.9 0.3 broadcast_and_fusion.1
  46.1 0.1 and.501
  46.3 0.5 copy.118
  46.8 0.1 and.520
  46.9 0.5 copy.122
  47.4 0.1 broadcast_and_fusion.4
  47.5 0.9 add_convert_fusion.pick_ref
  48.3 57.0 %all-gather.2.cloned.1.call-done = bf16[2048,4096]{1,0:T(8,128)(2,1)} async-done(((bf16[16,4096]{1,0:T(8,128)(2,1)}), bf16[2048,4096]{1,0:T(8,128)(2,1)}) %all-gather.2.cloned.1.call-update) | async-done | bytes 16777232 | tf_op jit(solution)/shard_map/all_gather | solution.py:220
  105.3 14.1 %select_rows.1 = (bf16[384,4096]{1,0:T(8,128)(2,1)}, bf16[384,4096]{1,0:T(8,128)(2,1)}, bf16[384,4096]{1,0:T(8,128)(2,1)}, bf16[384,4096]{1,0:T(8,128)(2,1)}) custom-call(bf16[16,96,128]{2,1,0:T(8,128)(2,1)} %add_convert_fusion.pick_ref, f32[16,96,1]{2,1,0:T(8,128)} %copy.129.scale_ref, bf16[8,16,16,4096]{3,2,1,0:T(8,128)(2,1)} %bitcast.40), custom_call_target="tpu_custom_call" | custom-call | tf_op jit(solution)/shard_map/select_rows/pallas_call | solution.py:35
  119.4 13.4 %expert_forward.1 = (f32[384,384]{1,0:T(8,128)}, f32[384,384]{1,0:T(8,128)}, bf16[384,384]{1,0:T(8,128)(2,1)}, bf16[384,4096]{1,0:T(8,128)(2,1)}) custom-call(bf16[384,4096]{1,0:T(8,128)(2,1)} %get-tuple-element.19.x_ref, bf16[384,4096]{1,0:T(8,128)(2,1)} %bitcast.43, bf16[384,4096]{1,0:T(8,128)(2,1)} %bitcast.45, bf16[384,4096]{1,0:T(8,128)(2,1)} %bitcast.47), custom_call_target="tpu_custom_call" | custom-call | flops 3623878656 | bytes 18874368 | tf_op jit(solution)/shard_map/expert_forward/pallas_call | solution.py:76
  132.8 13.6 %expert_backward.1 = (bf16[16,72,384]{2,1,0:T(8,128)(2,1)}, bf16[384,4096]{1,0:T(8,128)(2,1)}) custom-call(bf16[384,4096]{1,0:T(8,128)(2,1)} %get-tuple-element.21.g_ref, f32[384,384]{1,0:T(8,128)} %get-tuple-element.22.gate_ref, f32[384,384]{1,0:T(8,128)} %get-tuple-element.23.up_ref, bf16[384,384]{1,0:T(8,128)(2,1)} %get-tuple-element.24.hid_ref, ...), custom_call_target="tpu_custom_call" | custom-call | flops 3623878656 | bytes 18874368 | tf_op jit(solution)/shard_map/expert_backward/pallas_call | solution.py:140
  146.4 18.1 %all_to_all.35 = bf16[16,72,384]{2,1,0:T(8,128)(2,1)} all-to-all(bf16[16,72,384]{2,1,0:T(8,128)(2,1)} %get-tuple-element.26), channel_id=1, replica_groups=mesh['branch'=8,'wide'=16] {'branch'}, dimensions={0} | all-to-all | bytes 1769472 | tf_op jit(solution)/shard_map/all_to_all | solution.py:208
  164.5 44.6 %all_to_all.36 = bf16[16,24,4096]{2,1,0:T(8,128)(2,1)} all-to-all(bf16[16,24,4096]{2,1,0:T(8,128)(2,1)} %bitcast.42), channel_id=1, replica_groups=mesh['branch'=8,'wide'=16] {'wide'}, dimensions={0} | all-to-all | bytes 6291456 | tf_op jit(solution)/shard_map/all_to_all | solution.py:208
  209.1 4.1 %all-to-all-start.1 = ((bf16[16,24,4096]{2,1,0:T(8,128)(2,1)}), bf16[16,24,4096]{2,1,0:T(8,128)(2,1)S(1)}, u32[]{:S(2)}, u32[]{:S(2)}) async-start(bf16[16,24,4096]{2,1,0:T(8,128)(2,1)} %bitcast.41), calls=%async_computation.1 | async-start | bytes 6291456 | tf_op jit(solution)/shard_map/all_to_all | solution.py:208
  213.3 0.1 convert_reduce_fusion.11
  213.4 0.1 convert_reduce_fusion.9
  213.5 0.1 convert_reduce_fusion.7
  213.8 0.6 broadcast_select_fusion
  214.4 35.6 %all-to-all-done.1 = bf16[16,24,4096]{2,1,0:T(8,128)(2,1)S(1)} async-done(((bf16[16,24,4096]{2,1,0:T(8,128)(2,1)}), bf16[16,24,4096]{2,1,0:T(8,128)(2,1)S(1)}, u32[]{:S(2)}, u32[]{:S(2)}) %all-to-all-start.1) | async-done | bytes 3145760 | tf_op jit(solution)/shard_map/all_to_all | solution.py:208
  250.0 6.5 %all-to-all-start.6 = ((bf16[16,72,384]{2,1,0:T(8,128)(2,1)}), bf16[16,72,384]{2,1,0:T(8,128)(2,1)}, u32[]{:S(2)}, u32[]{:S(2)}) async-start(bf16[16,72,384]{2,1,0:T(8,128)(2,1)} %all_to_all.35), calls=%async_computation.6 | async-start | bytes 1769472 | tf_op jit(solution)/shard_map/all_to_all | solution.py:208
  256.5 2.4 convert_reduce_fusion
  258.9 1.0 reshape.1213
  259.9 0.5 convert_reduce_fusion.1
  260.4 1.0 reshape.1211
  261.3 1.4 pad_maximum_fusion
  262.8 1.1 reshape.1214
  263.9 3.6 %all-to-all-done.6.lhs_ref = bf16[16,72,384]{2,1,0:T(8,128)(2,1)} async-done(((bf16[16,72,384]{2,1,0:T(8,128)(2,1)}), bf16[16,72,384]{2,1,0:T(8,128)(2,1)}, u32[]{:S(2)}, u32[]{:S(2)}) %all-to-all-start.6) | async-done | bytes 884768 | tf_op jit(solution)/shard_map/all_to_all | solution.py:208
  267.5 9.1 %all-to-all-start.3 = ((f32[8,24,1024]{2,1,0:T(8,128)}), f32[8,24,1024]{2,1,0:T(8,128)S(1)}, u32[]{:S(2)}, u32[]{:S(2)}) async-start(f32[8,24,1024]{2,1,0:T(8,128)} %reshape.1214), calls=%async_computation.3 | async-start | bytes 1572864 | tf_op jit(solution)/shard_map/all_to_all | solution.py:208
  276.6 0.3 convert_reduce_fusion.2
  276.9 0.7 multiply_convert_fusion
  277.6 11.5 %weight_grads.1 = (bf16[384,4096]{1,0:T(8,128)(2,1)}, bf16[384,4096]{1,0:T(8,128)(2,1)}, bf16[384,4096]{1,0:T(8,128)(2,1)}) custom-call(bf16[16,72,384]{2,1,0:T(8,128)(2,1)} %all-to-all-done.6.lhs_ref, bf16[384,4096]{1,0:T(8,128)(2,1)} %get-tuple-element.27.x_ref, bf16[384,4096]{1,0:T(8,128)(2,1)} %get-tuple-element.28.g_ref), custom_call_target="tpu_custom_call" | custom-call | flops 3623878656 | bytes 16777216 | tf_op jit(solution)/shard_map/weight_grads/pallas_call | solution.py:180
  289.2 0.5 reshape.1215
  289.7 0.2 slice_bitcast_fusion
  289.9 0.9 multiply_reduce_fusion
  290.8 0.9 multiply_reduce_fusion.1
  (58 shorter events, 1.5 us)
Async XLA Ops:
  7.2 98.1 %all-gather.2.cloned.1.call-start = ((), (), s32[]{:S(2)}) async-start(), calls=%async_computation.7 | async-start | bytes 16908288 | tf_op jit(solution)/shard_map/all_gather | solution.py:220
  11.1 25.6 %all-to-all-start = ((f32[128,8,128]{2,1,0:T(8,128)}), f32[128,8,128]{2,1,0:T(8,128)S(1)}, u32[]{:S(2)}, u32[]{:S(2)}) async-start(f32[128,8,128]{2,1,0:T(8,128)} %broadcast_in_dim.37), calls=%async_computation | async-start | bytes 1048576 | tf_op jit(solution)/shard_map/all_to_all | solution.py:208
  36.6 109.8 %all-to-all-start.4 = ((bf16[8,512,256]{2,1,0:T(8,128)(2,1)}), bf16[8,512,256]{2,1,0:T(8,128)(2,1)S(1)}, u32[]{:S(2)}, u32[]{:S(2)}) async-start(bf16[8,512,256]{2,1,0:T(8,128)(2,1)} %bitcast.49), calls=%async_computation.4 | async-start | bytes 4194304 | tf_op jit(solution)/shard_map/all_to_all | solution.py:208
  146.4 62.7 %copy-start = (bf16[8,512,256]{2,1,0:T(8,128)(2,1)}, bf16[8,512,256]{2,1,0:T(8,128)(2,1)S(1)}, u32[]{:S(2)}) copy-start(bf16[8,512,256]{2,1,0:T(8,128)(2,1)S(1)} %all-to-all-done.4) | copy-start | bytes 6291460
  209.1 4.1 %copy-start.3 = (s32[8,2]{0,1:T(2,128)S(1)}, s32[8,2]{0,1:T(2,128)}, u32[]{:S(2)}) copy-start(s32[8,2]{0,1:T(2,128)} %param.10) | copy-start | bytes 196
  209.1 4.7 %copy-start.4 = (f32[8,2]{0,1:T(2,128)S(1)}, f32[8,2]{0,1:T(2,128)}, u32[]{:S(2)}) copy-start(f32[8,2]{0,1:T(2,128)} %param.11) | copy-start | bytes 196
  209.1 40.9 %all-to-all-start.1 = ((bf16[16,24,4096]{2,1,0:T(8,128)(2,1)}), bf16[16,24,4096]{2,1,0:T(8,128)(2,1)S(1)}, u32[]{:S(2)}, u32[]{:S(2)}) async-start(bf16[16,24,4096]{2,1,0:T(8,128)(2,1)} %bitcast.41), calls=%async_computation.1 | async-start | bytes 6291456 | tf_op jit(solution)/shard_map/all_to_all | solution.py:208
  250.0 17.5 %all-to-all-start.6 = ((bf16[16,72,384]{2,1,0:T(8,128)(2,1)}), bf16[16,72,384]{2,1,0:T(8,128)(2,1)}, u32[]{:S(2)}, u32[]{:S(2)}) async-start(bf16[16,72,384]{2,1,0:T(8,128)(2,1)} %all_to_all.35), calls=%async_computation.6 | async-start | bytes 1769472 | tf_op jit(solution)/shard_map/all_to_all | solution.py:208
  260.4 16.2 %copy-start.1 = (bf16[8,512,256]{2,1,0:T(8,128)(2,1)S(1)}, bf16[8,512,256]{2,1,0:T(8,128)(2,1)}, u32[]{:S(2)}) copy-start(bf16[8,512,256]{2,1,0:T(8,128)(2,1)} %copy-done) | copy-start | bytes 6291460
  267.5 21.6 %all-to-all-start.3 = ((f32[8,24,1024]{2,1,0:T(8,128)}), f32[8,24,1024]{2,1,0:T(8,128)S(1)}, u32[]{:S(2)}, u32[]{:S(2)}) async-start(f32[8,24,1024]{2,1,0:T(8,128)} %reshape.1214), calls=%async_computation.3 | async-start | bytes 1572864 | tf_op jit(solution)/shard_map/all_to_all | solution.py:208
  289.1 1.7 copy-start.2
Sparse Core Ops, SparseCore 0:
  11.7 93.5 all-gather.1

commit v2 on v1

v2 whole, which is shorter than its diff:
```python
import functools

import jax
import jax.numpy as jnp
from jax import lax
from jax.experimental import pallas as pl
from jax.experimental.pallas import tpu as pltpu
from jax.sharding import PartitionSpec as P

F32 = jnp.float32
BF16 = jnp.bfloat16
CAP = 3
LAST = (((1,), (1,)), ((), ()))
PARAMS = pltpu.CompilerParams(vmem_limit_bytes=58 * 1024 * 1024)


def split_rows(rows_ref):
    blocks, per_block, lanes = rows_ref.shape
    half = per_block // 2
    rows = rows_ref[...]
    x = rows[:, :half].reshape(blocks * half, lanes)
    g = rows[:, half:].reshape(blocks * half, lanes)
    return x, g


def one_hot_rows(place, count):
    row = lax.broadcasted_iota(jnp.int32, (count, place.shape[1]), 0)
    return jnp.where(row == place, 1.0, 0.0).astype(BF16)


def expert_kernel(
    place_ref, prob_ref, rows_ref, wg_ref, wu_ref, wd_ref,
    send_ref, back_ref,
    gate_acc, up_acc, hg_acc, acts, results, *, steps, groups,
):
    step = pl.program_id(0)
    slots = acts.shape[1]
    blocks = slots // CAP

    @pl.when(step < steps)
    def _():
        x, g = split_rows(rows_ref)
        for acc, lhs, w_ref in ((gate_acc, x, wg_ref), (up_acc, x, wu_ref), (hg_acc, g, wd_ref)):
            part = lax.dot_general(lhs, w_ref[...], LAST, preferred_element_type=F32)

            @pl.when(step == 0)
            def _(acc=acc, part=part):
                acc[...] = part

            @pl.when(step > 0)
            def _(acc=acc, part=part):
                acc[...] += part

    @pl.when(step == steps)
    def _():
        prob = prob_ref[...]
        gate = gate_acc[...]
        up = up_acc[...]
        sig = jax.nn.sigmoid(gate)
        back = hg_acc[...] * prob
        gate_sig = gate * sig
        pick = one_hot_rows(place_ref[...], slots)
        values = (
            back * up * sig * (1.0 + gate * (1.0 - sig)),
            back * gate_sig,
            gate_sig * up * prob,
        )
        pieces, stacked, _ = send_ref.shape
        height = stacked // 3
        turned = []
        for n, value in enumerate(values):
            got = jnp.dot(pick, value.astype(BF16), preferred_element_type=F32)
            acts[n] = got.astype(BF16)
            turned.append(got.T.reshape(pieces, height, slots))
        send_ref[...] = jnp.concatenate(turned, axis=1).astype(BF16)

    @pl.when((step >= steps) & (step < 2 * steps))
    def _():
        tile = step - steps
        out = jnp.dot(acts[2], wd_ref[...], preferred_element_type=F32)
        results[tile, 0] = out.astype(BF16)
        grad = jnp.dot(acts[0], wg_ref[...], preferred_element_type=F32) + jnp.dot(
            acts[1], wu_ref[...], preferred_element_type=F32
        )
        results[tile, 1] = grad.astype(BF16)

    @pl.when(step >= 2 * steps)
    def _():
        group = step - 2 * steps
        count = blocks // groups
        size = 8 * count
        row = lax.broadcasted_iota(jnp.int32, (size, size), 0)
        column = lax.broadcasted_iota(jnp.int32, (size, size), 1)
        turn = jnp.where(column == (row % 8) * count + row // 8, 1.0, 0.0).astype(BF16)
        pieces = [(o, s, j) for o in range(2) for s in range(CAP) for j in range(steps)]
        done = []
        for n in range(0, len(pieces), 8):
            slab = jnp.concatenate(
                [
                    results[j, o, pl.ds(pl.multiple_of(s * blocks + group * count, count), count), :]
                    for o, s, j in pieces[n : n + 8]
                ],
                axis=0,
            )
            mixed = jnp.dot(turn, slab, preferred_element_type=F32)
            done.append(mixed.reshape(count, 8, mixed.shape[1]))
        back_ref[...] = jnp.concatenate(done, axis=1).astype(BF16)


def expert(place, prob, rows, wg, wu, wd, pieces):
    blocks, per_block, features = rows.shape
    hidden = wg.shape[0]
    slots = blocks * CAP
    tokens = place.shape[1]
    steps, groups = 4, 4
    tile = features // steps

    def wtile(i):
        return (0, jnp.where(i < steps, i, jnp.minimum(i - steps, steps - 1)))

    wspec = pl.BlockSpec((hidden, tile), wtile)
    stacked = 3 * hidden // pieces
    return pl.pallas_call(
        functools.partial(expert_kernel, steps=steps, groups=groups),
        grid=(2 * steps + groups,),
        in_specs=[
            pl.BlockSpec((1, tokens), lambda i: (0, 0)),
            pl.BlockSpec((tokens, 1), lambda i: (0, 0)),
            pl.BlockSpec((blocks, per_block, tile), lambda i: (0, 0, jnp.minimum(i, steps - 1))),
            wspec, wspec, wspec,
        ],
        out_specs=[
            pl.BlockSpec((pieces, stacked, slots), lambda i: (0, 0, 0)),
            pl.BlockSpec(
                (blocks // groups, 8 * CAP, tile), lambda i: (jnp.maximum(i - 2 * steps, 0), 0, 0)
            ),
        ],
        out_shape=[
            jax.ShapeDtypeStruct((pieces, stacked, slots), BF16),
            jax.ShapeDtypeStruct((blocks, 8 * CAP, tile), BF16),
        ],
        scratch_shapes=[
            pltpu.VMEM((tokens, hidden), F32),
            pltpu.VMEM((tokens, hidden), F32),
            pltpu.VMEM((tokens, hidden), F32),
            pltpu.VMEM((3, slots, hidden), BF16),
            pltpu.VMEM((steps, 2, slots, tile), BF16),
        ],
        compiler_params=PARAMS,
        cost_estimate=pl.CostEstimate(
            flops=6 * tokens * features * hidden,
            bytes_accessed=42 * 1024 * 1024,
            transcendentals=tokens * hidden,
        ),
        name="expert",
    )(place, prob, rows, wg, wu, wd)


def pick_kernel(place_ref, rows_ref, x_ref, g_ref):
    x, g = split_rows(rows_ref)
    pick = one_hot_rows(place_ref[...], x_ref.shape[0])
    x_ref[...] = jnp.dot(pick, x, preferred_element_type=F32).astype(BF16)
    g_ref[...] = jnp.dot(pick, g, preferred_element_type=F32).astype(BF16)


def pick_rows(place, rows):
    blocks, per_block, features = rows.shape
    slots = blocks * CAP
    tokens = place.shape[1]
    steps = 4
    tile = features // steps
    spec = pl.BlockSpec((slots, tile), lambda i: (0, i))
    return pl.pallas_call(
        pick_kernel,
        grid=(steps,),
        in_specs=[
            pl.BlockSpec((1, tokens), lambda i: (0, 0)),
            pl.BlockSpec((blocks, per_block, tile), lambda i: (0, 0, i)),
        ],
        out_specs=[spec, spec],
        out_shape=[jax.ShapeDtypeStruct((slots, features), BF16)] * 2,
        compiler_params=PARAMS,
        cost_estimate=pl.CostEstimate(
            flops=4 * slots * tokens * features, bytes_accessed=24 * 1024 * 1024, transcendentals=0
        ),
        name="pick_rows",
    )(place, rows)


def combine_kernel(chosen_ref, got_ref, mixed_ref, grad_ref, acc):
    step = pl.program_id(0)
    total = jnp.sum(got_ref[0].astype(F32), axis=0)
    chosen = chosen_ref[0]
    tile = total.shape[1]
    tiles = mixed_ref.shape[1] // tile

    @pl.when(step == 0)
    def _():
        acc[...] = jnp.zeros_like(acc)

    for o in range(2):
        for j in range(tiles):
            part = acc[o, :, j * tile : (j + 1) * tile]
            for s in range(CAP):
                row = (o * CAP + s) * tiles + j
                part = part + chosen[:, s : s + 1] * total[row : row + 1]
            acc[o, :, j * tile : (j + 1) * tile] = part

    @pl.when(step == pl.num_programs(0) - 1)
    def _():
        mixed_ref[...] = acc[0].astype(BF16)
        grad_ref[...] = acc[1].astype(BF16)


def combine(chosen, got):
    experts, wide, rows, tile = got.shape
    tokens = chosen.shape[1]
    features = tile * rows // (2 * CAP)
    spec = pl.BlockSpec((tokens, features), lambda i: (0, 0))
    return pl.pallas_call(
        combine_kernel,
        grid=(experts,),
        in_specs=[
            pl.BlockSpec((1, tokens, CAP), lambda i: (i, 0, 0)),
            pl.BlockSpec((1, wide, rows, tile), lambda i: (i, 0, 0, 0)),
        ],
        out_specs=[spec, spec],
        out_shape=[jax.ShapeDtypeStruct((tokens, features), BF16)] * 2,
        scratch_shapes=[pltpu.VMEM((2, tokens, features), F32)],
        compiler_params=PARAMS,
        name="combine",
    )(chosen, got)


def weights_kernel(lhs_ref, x_ref, g_ref, gate_ref, up_ref, down_ref):
    pieces, stacked, slots = lhs_ref.shape
    rows = stacked // 3
    lhs = lhs_ref[...].astype(F32)
    for n, (src, dst) in enumerate(((x_ref, gate_ref), (x_ref, up_ref), (g_ref, down_ref))):
        part = lhs[:, n * rows : (n + 1) * rows].reshape(pieces * rows, slots).astype(BF16)
        dst[...] = jnp.dot(part, src[...], preferred_element_type=F32).astype(BF16)


def weight_grads(lhs, x, g):
    pieces, stacked, slots = lhs.shape
    features = x.shape[1]
    rows = stacked // 3
    tile = features // 8
    ispec = pl.BlockSpec((slots, tile), lambda i: (0, i))
    ospec = pl.BlockSpec((pieces * rows, tile), lambda i: (0, i))
    oshape = jax.ShapeDtypeStruct((pieces * rows, features), BF16)
    return pl.pallas_call(
        weights_kernel,
        grid=(features // tile,),
        in_specs=[pl.BlockSpec((pieces, stacked, slots), lambda i: (0, 0, 0)), ispec, ispec],
        out_specs=[ospec] * 3,
        out_shape=[oshape] * 3,
        compiler_params=PARAMS,
        cost_estimate=pl.CostEstimate(
            flops=6 * slots * features * pieces * rows,
            bytes_accessed=16 * 1024 * 1024,
            transcendentals=0,
        ),
        name="weight_grads",
    )(lhs, x, g)


def route_places(ids, probs, expert):
    named = ids == expert
    mine = jnp.any(named, axis=2)
    weight = jnp.sum(jnp.where(named, probs, 0.0), axis=2)
    blocks, tokens = mine.shape
    earlier = jnp.arange(tokens)[:, None] < jnp.arange(tokens)[None, :]
    slot = jnp.sum(mine[:, :, None] & earlier[None], axis=1)
    place = jnp.where(mine, slot * blocks + jnp.arange(blocks)[:, None], -1)
    return place.astype(jnp.int32).reshape(1, blocks * tokens), weight


def exchange(value, axis):
    return lax.all_to_all(value, axis, split_axis=0, concat_axis=0, tiled=True)


def on_device(x_tokens, out_grad, expert_ids, gate_probs, w_gate, w_up, w_down, attn_out):
    experts = lax.axis_size("branch")
    wide = lax.axis_size("wide")
    blocks = experts * wide
    tokens, features = x_tokens.shape
    both = ("branch", "wide")
    branch_index = lax.axis_index("branch")
    wide_index = lax.axis_index("wide")

    gathered = lax.all_gather(
        jnp.concatenate([x_tokens, out_grad], axis=0), both, axis=0, tiled=True
    )
    gathered = gathered.reshape(blocks, 2 * tokens, features)

    meta = jnp.concatenate([expert_ids.astype(F32), gate_probs], axis=1)
    meta = jnp.pad(meta, ((0, 0), (0, 124)))
    meta = exchange(jnp.broadcast_to(meta[None], (blocks,) + meta.shape), both)
    ids = meta[:, :, 0:2].astype(jnp.int32)
    probs = meta[:, :, 2:4]
    place, weight = route_places(ids, probs, branch_index)
    other_place, _ = route_places(ids, probs, wide_index // (wide // experts))

    attn = exchange(attn_out[0].reshape(experts, -1, attn_out.shape[2]), "branch")
    merged_attn = (jnp.sum(attn.astype(F32), axis=0) * (1.0 / experts)).astype(BF16)
    gathered, merged_attn = lax.optimization_barrier((gathered, merged_attn))

    send, back = expert(
        place, weight.reshape(-1, 1), gathered, w_gate[0], w_up[0], w_down[0], wide
    )

    spread = lax.all_gather(send, "branch", axis=0, tiled=True)
    spread = spread.reshape((experts, wide) + send.shape[1:])
    copies = wide // experts
    mine = lax.dynamic_slice_in_dim(spread, branch_index * copies, copies, 1)
    xe, ge = pick_rows(other_place, gathered)
    mine, xe, ge = lax.optimization_barrier((mine.reshape(send.shape), xe, ge))
    relayed = exchange(mine, "wide")

    got = exchange(back, both).reshape(experts, wide, 8 * CAP, -1)

    named = jnp.any(expert_ids[None] == jnp.arange(experts)[:, None, None], axis=2)
    earlier = jnp.arange(tokens)[:, None] < jnp.arange(tokens)[None, :]
    slot = jnp.sum(named[:, :, None] & earlier[None], axis=1)
    chosen = named[:, :, None] & (slot[:, :, None] == jnp.arange(CAP)[None, None, :])
    mixed, token_grad = combine(chosen.astype(F32), got)
    grad_gate, grad_up, grad_down = weight_grads(relayed, xe, ge)

    layout = (1, 1, wide, w_gate.shape[1] // wide, features)
    return (
        mixed,
        token_grad,
        merged_attn,
        grad_gate.reshape(layout),
        grad_up.reshape(layout),
        grad_down.reshape(layout),
    )


def solution(mesh):
    in_specs = (
        P(("branch", "wide"), None),
        P(("branch", "wide"), None),
        P(("branch", "wide"), None),
        P(("branch", "wide"), None),
        P("branch", "wide", None),
        P("branch", "wide", None),
        P("branch", "wide", None),
        P("branch", None, "wide"),
    )
    out_specs = (
        P(("branch", "wide"), None),
        P(("branch", "wide"), None),
        P("branch", "wide"),
        P("wide", "branch", None, None, None),
        P("wide", "branch", None, None, None),
        P("wide", "branch", None, None, None),
    )
    return jax.shard_map(
        on_device, mesh=mesh, in_specs=in_specs, out_specs=out_specs, check_vma=False
    )
```

time: 299 us -> 287 us (0.960)
  waiting for transfers between devices: 110 us -> 153 us
  blocking collectives: 62.7 us -> 25.7 us
  starting transfers between devices: 35.9 us -> 16.3 us
  Pallas kernels: 52.7 us -> 62.4 us
  other arithmetic: 12.8 us -> 4.85 us
    all_gather x0 -> x1, waiting for transfers between devices: none -> 79.9 us  [on_device(): spread = lax.all_gather(send, 'branch', axis=0, tiled=True)]
    all_to_all x2 -> x1, blocking collectives: 62.7 us -> 25.7 us  [exchange(): return lax.all_to_all(value, axis, split_axis=0, concat_axis=0, tiled=True)]
    all_gather x1, waiting for transfers between devices: 57 us -> 31.7 us  [on_device(): lax.all_gather(jnp.concatenate([x_tokens, out_grad], axis=0), both, axis=...]
    all_to_all x5 -> x3, starting transfers between devices: 35.8 us -> 16.2 us  [exchange(): return lax.all_to_all(value, axis, split_axis=0, concat_axis=0, tiled=True)]
    all_to_all x5 -> x3, waiting for transfers between devices: 52.9 us -> 41 us  [exchange(): return lax.all_to_all(value, axis, split_axis=0, concat_axis=0, tiled=True)]
    pallas_call x4, Pallas kernels: 52.7 us -> 62.4 us  [the longest x1 33.6 us: expert(): pl.pallas_call(functools.partial(expert_kernel, steps=steps, groups=group...]
    reduce_sum x12 -> x3, other arithmetic: 5.29 us -> 0.18 us  [the longest x1 0.09 us: on_device(): slot = jnp.sum(named[:, :, None] & earlier[None], axis=1)]
  transfers between devices with their start and end apart: 6 -> 5, of which waited for: 4 -> 5; matrix products, arithmetic and copies ran while one was open for 6% -> 4% of each run, Pallas kernels for 18% -> 7%
where the time goes in v2:
time: 287 us; the launch traced here: 284 us
  waiting for transfers between devices  153 us (53%)
  Pallas kernels  62.4 us (22%)
  blocking collectives  25.7 us (9%)
  starting transfers between devices  16.3 us (6%)
  between operations  14.1 us (5%)
  local copies, waits for them, and re-layouts  8.27 us (3%)
  other arithmetic  4.85 us (2%)
    all_gather x1, waiting for transfers between devices, on_device(): spread = lax.all_gather(send, 'branch', axis=0, tiled=True)  79.9 us
    all_to_all x3, waiting for transfers between devices, exchange(): return lax.all_to_all(value, axis, split_axis=0, concat_axis=0, tiled=True)  41 us
    pallas_call x1, Pallas kernels, expert(): pl.pallas_call(functools.partial(expert_kernel, steps=steps, groups=group...  33.6 us
    all_gather x1, waiting for transfers between devices, on_device(): lax.all_gather(jnp.concatenate([x_tokens, out_grad], axis=0), both, axis=...  31.7 us
    all_to_all x1, blocking collectives, exchange(): return lax.all_to_all(value, axis, split_axis=0, concat_axis=0, tiled=True)  25.7 us
    all_to_all x3, starting transfers between devices, exchange(): return lax.all_to_all(value, axis, split_axis=0, concat_axis=0, tiled=True)  16.2 us
    pallas_call x1, Pallas kernels, pick_rows(): pl.pallas_call(pick_kernel, grid=(steps,), in_specs=[pl.BlockSpec((1, tok...  11.8 us
    pallas_call x1, Pallas kernels, weight_grads(): pl.pallas_call(weights_kernel, grid=(features // tile,), in_specs=[pl.Blo...  10.1 us
  transfers between devices with their start and end apart: 5, of which 5 were waited for; matrix products, arithmetic and copies ran while one was open for 4% of the time, Pallas kernels for 7%

profile of v2, /device:TPU:1, one launch (start us, length us, event | category | flops | bytes accessed | tf_op | source)
XLA Modules:
  0.0 284.3 jit_solution(10135433690897035422)
XLA Ops:
  7.2 0.0 all-gather.3.cloned.1.call-start
  7.2 1.5 pad_maximum_fusion
  8.7 0.0 all-gather.3.cloned.1.call-update
  8.8 0.7 convert_element_type.28
  9.5 0.7 pad_maximum_fusion.1
  10.1 0.1 copy.54
  10.3 25.7 %all_to_all.20 = f32[128,8,128]{2,1,0:T(8,128)S(1)} all-to-all(f32[128,8,128]{2,1,0:T(8,128)S(1)} %broadcast_in_dim.10), channel_id=1, replica_groups=mesh['branch'=8,'wide'=16] {'branch','wide'}, dimensions={0} | all-to-all | bytes 1048576 | tf_op jit(solution)/shard_map/all_to_all | solution.py:280
  35.9 4.3 %all-to-all-start.1 = ((bf16[8,512,256]{2,1,0:T(8,128)(2,1)}), bf16[8,512,256]{2,1,0:T(8,128)(2,1)S(1)}, u32[]{:S(2)}, u32[]{:S(2)}) async-start(bf16[8,512,256]{2,1,0:T(8,128)(2,1)} %bitcast.11), calls=%async_computation.1 | async-start | bytes 4194304 | tf_op jit(solution)/shard_map/all_to_all | solution.py:280
  40.2 0.0 all-gather.5.cloned.1.call-start
  40.3 0.9 fusion.4
  41.2 1.2 copy.52
  42.4 0.2 copy.53
  42.7 0.1 convert_reduce_fusion.1
  42.8 0.1 copy.47
  42.9 0.7 select_n.40.place_ref
  43.6 0.1 copy.49
  43.7 1.0 reshape.138.prob_ref
  44.7 27.5 %all-to-all-done.1 = bf16[8,512,256]{2,1,0:T(8,128)(2,1)S(1)} async-done(((bf16[8,512,256]{2,1,0:T(8,128)(2,1)}), bf16[8,512,256]{2,1,0:T(8,128)(2,1)S(1)}, u32[]{:S(2)}, u32[]{:S(2)}) %all-to-all-start.1) | async-done | bytes 2097184 | tf_op jit(solution)/shard_map/all_to_all | solution.py:280
  72.1 0.3 convert_reduce_fusion
  72.4 0.7 multiply_convert_fusion
  73.2 31.7 %all-gather.3.cloned.1.call-done = bf16[2048,4096]{1,0:T(8,128)(2,1)} async-done(((bf16[16,4096]{1,0:T(8,128)(2,1)}), bf16[2048,4096]{1,0:T(8,128)(2,1)}) %all-gather.3.cloned.1.call-update) | async-done | bytes 16777232 | tf_op jit(solution)/shard_map/all_gather | solution.py:292
  104.9 33.6 %expert.1 = (bf16[16,72,384]{2,1,0:T(8,128)(2,1)}, bf16[128,24,1024]{2,1,0:T(8,128)(2,1)}) custom-call(s32[1,1024]{1,0:T(1,128)} %select_n.40.place_ref, f32[1024,1]{1,0:T(8,128)} %reshape.138.prob_ref, bf16[128,16,4096]{2,1,0:T(8,128)(2,1)} %bitcast.13, bf16[384,4096]{1,0:T(8,128)(2,1)} %bitcast.15, bf16[384,4096]{1,0:T(8,128)(2,1)} %bitcast.16, ...), custom_call_target="tpu_custom_call" | custom-call | flops 9663676416 | bytes 44040192 | tf_op jit(solution)/shard_map/expert/pallas_call | solution.py:123
  138.5 0.0 all-gather.5.cloned.1.call-update
  138.5 7.8 %all-to-all-start.2 = ((bf16[128,24,1024]{2,1,0:T(8,128)(2,1)}), bf16[128,24,1024]{2,1,0:T(8,128)(2,1)}, u32[]{:S(2)}, u32[]{:S(2)}) async-start(bf16[128,24,1024]{2,1,0:T(8,128)(2,1)} %get-tuple-element.21), calls=%async_computation.2 | async-start | bytes 12582912 | tf_op jit(solution)/shard_map/all_to_all | solution.py:280
  146.3 0.1 copy.51
  146.4 0.7 select_n.45.place_ref
  147.1 11.8 %pick_rows.1 = (bf16[384,4096]{1,0:T(8,128)(2,1)}, bf16[384,4096]{1,0:T(8,128)(2,1)}) custom-call(s32[1,1024]{1,0:T(1,128)} %select_n.45.place_ref, bf16[128,16,4096]{2,1,0:T(8,128)(2,1)} %bitcast.14), custom_call_target="tpu_custom_call" | custom-call | flops 6442450944 | bytes 25165824 | tf_op jit(solution)/shard_map/pick_rows/pallas_call | solution.py:173
  158.9 0.0 copy-start.1
  158.9 79.9 %all-gather.5.cloned.1.call-done = bf16[128,72,384]{2,1,0:T(8,128)(2,1)} async-done(((bf16[16,72,384]{2,1,0:T(8,128)(2,1)}), bf16[128,72,384]{2,1,0:T(8,128)(2,1)}) %all-gather.5.cloned.1.call-update) | async-done | bytes 7077904 | tf_op jit(solution)/shard_map/all_gather | solution.py:313
  238.8 2.2 constant_dynamic-slice_fusion
  241.0 7.6 %all-to-all-done.2 = bf16[128,24,1024]{2,1,0:T(8,128)(2,1)} async-done(((bf16[128,24,1024]{2,1,0:T(8,128)(2,1)}), bf16[128,24,1024]{2,1,0:T(8,128)(2,1)}, u32[]{:S(2)}, u32[]{:S(2)}) %all-to-all-start.2) | async-done | bytes 6291488 | tf_op jit(solution)/shard_map/all_to_all | solution.py:280
  248.5 4.2 %all-to-all-start.3 = ((bf16[16,72,384]{2,1,0:T(8,128)(2,1)}), bf16[16,72,384]{2,1,0:T(8,128)(2,1)S(1)}, u32[]{:S(2)}, u32[]{:S(2)}) async-start(bf16[16,72,384]{2,1,0:T(8,128)(2,1)} %bitcast.7), calls=%async_computation.3 | async-start | bytes 1769472 | tf_op jit(solution)/shard_map/all_to_all | solution.py:280
  252.7 0.0 copy-done.1
  252.7 0.1 convert_reduce_fusion.3
  252.8 0.7 fusion.1.chosen_ref
  253.5 6.9 %combine.1 = (bf16[8,4096]{1,0:T(8,128)(2,1)}, bf16[8,4096]{1,0:T(8,128)(2,1)}) custom-call(f32[8,8,3]{2,1,0:T(8,128)} %fusion.1.chosen_ref, bf16[8,16,24,1024]{3,2,1,0:T(8,128)(2,1)} %bitcast.5.got_ref), custom_call_target="tpu_custom_call" | custom-call | tf_op jit(solution)/shard_map/combine/pallas_call | solution.py:220
  260.4 6.0 %all-to-all-done.3.lhs_ref = bf16[16,72,384]{2,1,0:T(8,128)(2,1)S(1)} async-done(((bf16[16,72,384]{2,1,0:T(8,128)(2,1)}), bf16[16,72,384]{2,1,0:T(8,128)(2,1)S(1)}, u32[]{:S(2)}, u32[]{:S(2)}) %all-to-all-start.3) | async-done | bytes 884768 | tf_op jit(solution)/shard_map/all_to_all | solution.py:280
  266.4 0.0 copy-start
  266.4 0.9 copy-done
  267.4 10.1 %weight_grads.1 = (bf16[384,4096]{1,0:T(8,128)(2,1)}, bf16[384,4096]{1,0:T(8,128)(2,1)}, bf16[384,4096]{1,0:T(8,128)(2,1)}) custom-call(bf16[16,72,384]{2,1,0:T(8,128)(2,1)} %copy-done, bf16[384,4096]{1,0:T(8,128)(2,1)} %get-tuple-element.29.x_ref, bf16[384,4096]{1,0:T(8,128)(2,1)} %get-tuple-element.30.g_ref), custom_call_target="tpu_custom_call" | custom-call | flops 3623878656 | bytes 16777216 | tf_op jit(solution)/shard_map/weight_grads/pallas_call | solution.py:252
  (8 shorter events, 0.1 us)
Async XLA Ops:
  7.2 97.7 %all-gather.3.cloned.1.call-start = ((), (), s32[]{:S(2)}) async-start(), calls=%async_computation.4 | async-start | bytes 16908288 | tf_op jit(solution)/shard_map/all_gather | solution.py:292
  35.9 36.2 %all-to-all-start.1 = ((bf16[8,512,256]{2,1,0:T(8,128)(2,1)}), bf16[8,512,256]{2,1,0:T(8,128)(2,1)S(1)}, u32[]{:S(2)}, u32[]{:S(2)}) async-start(bf16[8,512,256]{2,1,0:T(8,128)(2,1)} %bitcast.11), calls=%async_computation.1 | async-start | bytes 4194304 | tf_op jit(solution)/shard_map/all_to_all | solution.py:280
  40.2 198.6 %all-gather.5.cloned.1.call-start = ((), (), s32[]{:S(2)}) async-start(), calls=%async_computation.5 | async-start | bytes 7962624 | tf_op jit(solution)/shard_map/all_gather | solution.py:313
  138.5 110.0 %all-to-all-start.2 = ((bf16[128,24,1024]{2,1,0:T(8,128)(2,1)}), bf16[128,24,1024]{2,1,0:T(8,128)(2,1)}, u32[]{:S(2)}, u32[]{:S(2)}) async-start(bf16[128,24,1024]{2,1,0:T(8,128)(2,1)} %get-tuple-element.21), calls=%async_computation.2 | async-start | bytes 12582912 | tf_op jit(solution)/shard_map/all_to_all | solution.py:280
  158.9 93.8 %copy-start.1 = (s32[8,2]{0,1:T(2,128)S(1)}, s32[8,2]{0,1:T(2,128)}, u32[]{:S(2)}) copy-start(s32[8,2]{0,1:T(2,128)} %param.10) | copy-start | bytes 196
  248.5 17.9 %all-to-all-start.3 = ((bf16[16,72,384]{2,1,0:T(8,128)(2,1)}), bf16[16,72,384]{2,1,0:T(8,128)(2,1)S(1)}, u32[]{:S(2)}, u32[]{:S(2)}) async-start(bf16[16,72,384]{2,1,0:T(8,128)(2,1)} %bitcast.7), calls=%async_computation.3 | async-start | bytes 1769472 | tf_op jit(solution)/shard_map/all_to_all | solution.py:280
  266.4 0.9 copy-start
Sparse Core Ops, SparseCore 0:
  11.7 93.1 all-gather.2
  138.6 100.1 all-gather.4

commit v3 on v2

--- a/solution.py
+++ b/solution.py
@@ -10,6 +10,7 @@
 F32 = jnp.float32
 BF16 = jnp.bfloat16
 CAP = 3
+SIDE = 4
 LAST = (((1,), (1,)), ((), ()))
 PARAMS = pltpu.CompilerParams(vmem_limit_bytes=58 * 1024 * 1024)
 
@@ -31,11 +32,10 @@
 def expert_kernel(
     place_ref, prob_ref, rows_ref, wg_ref, wu_ref, wd_ref,
     send_ref, back_ref,
-    gate_acc, up_acc, hg_acc, acts, results, *, steps, groups,
+    gate_acc, up_acc, hg_acc, acts, *, steps,
 ):
     step = pl.program_id(0)
     slots = acts.shape[1]
-    blocks = slots // CAP
 
     @pl.when(step < steps)
     def _():
@@ -74,37 +74,15 @@
             turned.append(got.T.reshape(pieces, height, slots))
         send_ref[...] = jnp.concatenate(turned, axis=1).astype(BF16)
 
-    @pl.when((step >= steps) & (step < 2 * steps))
+    @pl.when(step >= steps)
     def _():
-        tile = step - steps
         out = jnp.dot(acts[2], wd_ref[...], preferred_element_type=F32)
-        results[tile, 0] = out.astype(BF16)
         grad = jnp.dot(acts[0], wg_ref[...], preferred_element_type=F32) + jnp.dot(
             acts[1], wu_ref[...], preferred_element_type=F32
         )
-        results[tile, 1] = grad.astype(BF16)
-
-    @pl.when(step >= 2 * steps)
-    def _():
-        group = step - 2 * steps
-        count = blocks // groups
-        size = 8 * count
-        row = lax.broadcasted_iota(jnp.int32, (size, size), 0)
-        column = lax.broadcasted_iota(jnp.int32, (size, size), 1)
-        turn = jnp.where(column == (row % 8) * count + row // 8, 1.0, 0.0).astype(BF16)
-        pieces = [(o, s, j) for o in range(2) for s in range(CAP) for j in range(steps)]
-        done = []
-        for n in range(0, len(pieces), 8):
-            slab = jnp.concatenate(
-                [
-                    results[j, o, pl.ds(pl.multiple_of(s * blocks + group * count, count), count), :]
-                    for o, s, j in pieces[n : n + 8]
-                ],
-                axis=0,
-            )
-            mixed = jnp.dot(turn, slab, preferred_element_type=F32)
-            done.append(mixed.reshape(count, 8, mixed.shape[1]))
-        back_ref[...] = jnp.concatenate(done, axis=1).astype(BF16)
+        wide, _, height, tile = back_ref.shape
+        back_ref[:, 0] = out.reshape(wide, height, tile).astype(BF16)
+        back_ref[:, 1] = grad.reshape(wide, height, tile).astype(BF16)
 
 
 def expert(place, prob, rows, wg, wu, wd, pieces):
@@ -112,17 +90,17 @@
     hidden = wg.shape[0]
     slots = blocks * CAP
     tokens = place.shape[1]
-    steps, groups = 4, 4
+    steps = 4
     tile = features // steps
 
     def wtile(i):
-        return (0, jnp.where(i < steps, i, jnp.minimum(i - steps, steps - 1)))
+        return (0, jnp.where(i < steps, i, i - steps))
 
     wspec = pl.BlockSpec((hidden, tile), wtile)
     stacked = 3 * hidden // pieces
     return pl.pallas_call(
-        functools.partial(expert_kernel, steps=steps, groups=groups),
-        grid=(2 * steps + groups,),
+        functools.partial(expert_kernel, steps=steps),
+        grid=(2 * steps,),
         in_specs=[
             pl.BlockSpec((1, tokens), lambda i: (0, 0)),
             pl.BlockSpec((tokens, 1), lambda i: (0, 0)),
@@ -132,19 +110,18 @@
         out_specs=[
             pl.BlockSpec((pieces, stacked, slots), lambda i: (0, 0, 0)),
             pl.BlockSpec(
-                (blocks // groups, 8 * CAP, tile), lambda i: (jnp.maximum(i - 2 * steps, 0), 0, 0)
+                (pieces, 2, slots // pieces, tile), lambda i: (0, 0, 0, jnp.maximum(i - steps, 0))
             ),
         ],
         out_shape=[
             jax.ShapeDtypeStruct((pieces, stacked, slots), BF16),
-            jax.ShapeDtypeStruct((blocks, 8 * CAP, tile), BF16),
+            jax.ShapeDtypeStruct((pieces, 2, slots // pieces, features), BF16),
         ],
         scratch_shapes=[
             pltpu.VMEM((tokens, hidden), F32),
             pltpu.VMEM((tokens, hidden), F32),
             pltpu.VMEM((tokens, hidden), F32),
             pltpu.VMEM((3, slots, hidden), BF16),
-            pltpu.VMEM((steps, 2, slots, tile), BF16),
         ],
         compiler_params=PARAMS,
         cost_estimate=pl.CostEstimate(
@@ -187,46 +164,59 @@
     )(place, rows)
 
 
-def combine_kernel(chosen_ref, got_ref, mixed_ref, grad_ref, acc):
-    step = pl.program_id(0)
-    total = jnp.sum(got_ref[0].astype(F32), axis=0)
-    chosen = chosen_ref[0]
-    tile = total.shape[1]
-    tiles = mixed_ref.shape[1] // tile
-
-    @pl.when(step == 0)
-    def _():
-        acc[...] = jnp.zeros_like(acc)
-
-    for o in range(2):
-        for j in range(tiles):
-            part = acc[o, :, j * tile : (j + 1) * tile]
+def gather_kernel(got_ref, ret_ref):
+    total = jnp.sum(got_ref[...].astype(F32), axis=0)
+    experts, padded, tile = ret_ref.shape
+    blank = jnp.zeros((padded // 2 - CAP, tile), F32)
+    for block in range(experts):
+        rows = []
+        for o in range(2):
+            rows += [total[o, block * CAP : (block + 1) * CAP], blank]
+        ret_ref[block] = jnp.concatenate(rows, axis=0).astype(BF16)
+
+
+def gather_blocks(got, experts):
+    parts, _, height, features = got.shape
+    steps = 4
+    tile = features // steps
+    return pl.pallas_call(
+        gather_kernel,
+        grid=(steps,),
+        in_specs=[pl.BlockSpec((parts, 2, height, tile), lambda i: (0, 0, 0, i))],
+        out_specs=pl.BlockSpec((experts, 8, tile), lambda i: (0, 0, i)),
+        out_shape=jax.ShapeDtypeStruct((experts, 8, features), BF16),
+        compiler_params=PARAMS,
+        name="gather_blocks",
+    )(got)
+
+
+def combine_kernel(chosen_ref, got_ref, mixed_ref, grad_ref):
+    experts = got_ref.shape[0]
+    for o, ref in enumerate((mixed_ref, grad_ref)):
+        total = jnp.zeros(ref.shape, F32)
+        for e in range(experts):
+            rows = got_ref[e].astype(F32)
+            chosen = chosen_ref[e]
             for s in range(CAP):
-                row = (o * CAP + s) * tiles + j
-                part = part + chosen[:, s : s + 1] * total[row : row + 1]
-            acc[o, :, j * tile : (j + 1) * tile] = part
-
-    @pl.when(step == pl.num_programs(0) - 1)
-    def _():
-        mixed_ref[...] = acc[0].astype(BF16)
-        grad_ref[...] = acc[1].astype(BF16)
+                total = total + chosen[:, s : s + 1] * rows[4 * o + s : 4 * o + s + 1]
+        ref[...] = total.astype(BF16)
 
 
 def combine(chosen, got):
-    experts, wide, rows, tile = got.shape
+    experts, padded, features = got.shape
     tokens = chosen.shape[1]
-    features = tile * rows // (2 * CAP)
-    spec = pl.BlockSpec((tokens, features), lambda i: (0, 0))
+    steps = 2
+    tile = features // steps
+    spec = pl.BlockSpec((tokens, tile), lambda i: (0, i))
     return pl.pallas_call(
         combine_kernel,
-        grid=(experts,),
+        grid=(steps,),
         in_specs=[
-            pl.BlockSpec((1, tokens, CAP), lambda i: (i, 0, 0)),
-            pl.BlockSpec((1, wide, rows, tile), lambda i: (i, 0, 0, 0)),
+            pl.BlockSpec((experts, tokens, CAP), lambda i: (0, 0, 0)),
+            pl.BlockSpec((experts, padded, tile), lambda i: (0, 0, i)),
         ],
         out_specs=[spec, spec],
         out_shape=[jax.ShapeDtypeStruct((tokens, features), BF16)] * 2,
-        scratch_shapes=[pltpu.VMEM((2, tokens, features), F32)],
         compiler_params=PARAMS,
         name="combine",
     )(chosen, got)
@@ -265,15 +255,30 @@
     )(lhs, x, g)
 
 
-def route_places(ids, probs, expert):
+def route_places(ids, probs, expert, wide):
     named = ids == expert
     mine = jnp.any(named, axis=2)
     weight = jnp.sum(jnp.where(named, probs, 0.0), axis=2)
     blocks, tokens = mine.shape
     earlier = jnp.arange(tokens)[:, None] < jnp.arange(tokens)[None, :]
     slot = jnp.sum(mine[:, :, None] & earlier[None], axis=1)
-    place = jnp.where(mine, slot * blocks + jnp.arange(blocks)[:, None], -1)
+    block = jnp.arange(blocks)
+    column, branch = block % wide, block // wide
+    turned = column % SIDE * SIDE + column // SIDE
+    group = jnp.where(expert % 2 == 0, column, turned)
+    start = (group * (blocks // wide) + branch) * CAP
+    place = jnp.where(mine, start[:, None] + slot, -1)
     return place.astype(jnp.int32).reshape(1, blocks * tokens), weight
+
+
+def stage_groups(experts, wide, odd):
+    groups = []
+    for branch in range(experts):
+        for k in range(SIDE):
+            fast = branch % 2 != odd
+            members = [k * SIDE + n if fast else n * SIDE + k for n in range(SIDE)]
+            groups.append([branch * wide + m for m in members])
+    return groups
 
 
 def exchange(value, axis):
@@ -299,8 +304,8 @@
     meta = exchange(jnp.broadcast_to(meta[None], (blocks,) + meta.shape), both)
     ids = meta[:, :, 0:2].astype(jnp.int32)
     probs = meta[:, :, 2:4]
-    place, weight = route_places(ids, probs, branch_index)
-    other_place, _ = route_places(ids, probs, wide_index // (wide // experts))
+    place, weight = route_places(ids, probs, branch_index, wide)
+    other_place, _ = route_places(ids, probs, wide_index // (wide // experts), wide)
 
     attn = exchange(attn_out[0].reshape(experts, -1, attn_out.shape[2]), "branch")
     merged_attn = (jnp.sum(attn.astype(F32), axis=0) * (1.0 / experts)).astype(BF16)
@@ -314,18 +319,32 @@
     spread = spread.reshape((experts, wide) + send.shape[1:])
     copies = wide // experts
     mine = lax.dynamic_slice_in_dim(spread, branch_index * copies, copies, 1)
+    def stage(value, odd):
+        return lax.all_to_all(
+            value,
+            both,
+            split_axis=0,
+            concat_axis=0,
+            axis_index_groups=stage_groups(experts, wide, odd),
+            tiled=True,
+        )
+
+    first = stage(back, 0)
     xe, ge = pick_rows(other_place, gathered)
-    mine, xe, ge = lax.optimization_barrier((mine.reshape(send.shape), xe, ge))
+    first, mine, xe, ge = lax.optimization_barrier((first, mine.reshape(send.shape), xe, ge))
     relayed = exchange(mine, "wide")
-
-    got = exchange(back, both).reshape(experts, wide, 8 * CAP, -1)
+    first = first.reshape((SIDE, SIDE) + back.shape[1:])
+    second = jnp.sum(first.astype(F32), axis=0).astype(BF16)
+    second, relayed = lax.optimization_barrier((second, relayed))
+    returned = gather_blocks(stage(second, 1), experts)
+    grad_gate, grad_up, grad_down = weight_grads(relayed, xe, ge)
+    got = exchange(returned, "branch")
 
     named = jnp.any(expert_ids[None] == jnp.arange(experts)[:, None, None], axis=2)
     earlier = jnp.arange(tokens)[:, None] < jnp.arange(tokens)[None, :]
     slot = jnp.sum(named[:, :, None] & earlier[None], axis=1)
     chosen = named[:, :, None] & (slot[:, :, None] == jnp.arange(CAP)[None, None, :])
     mixed, token_grad = combine(chosen.astype(F32), got)
-    grad_gate, grad_up, grad_down = weight_grads(relayed, xe, ge)
 
     layout = (1, 1, wide, w_gate.shape[1] // wide, features)
     return (

time: 287 us -> 253 us (0.88)
  waiting for transfers between devices: 153 us -> 106 us
  starting transfers between devices: 16.3 us -> 27.4 us
  other arithmetic: 4.85 us -> 10.4 us
  Pallas kernels: 62.4 us -> 59.1 us
    all_gather x1, waiting for transfers between devices: 79.9 us -> 25.8 us  [on_device(): spread = lax.all_gather(send, 'branch', axis=0, tiled=True)]
    all_to_all x0 -> x2, waiting for transfers between devices: none -> 12.7 us  [stage(): lax.all_to_all(value, both, split_axis=0, concat_axis=0, axis_index_group...]
    all_to_all x0 -> x2, starting transfers between devices: none -> 8.79 us  [stage(): lax.all_to_all(value, both, split_axis=0, concat_axis=0, axis_index_group...]
    all_to_all x3, waiting for transfers between devices: 41 us -> 35.3 us  [exchange(): return lax.all_to_all(value, axis, split_axis=0, concat_axis=0, tiled=True)]
    reduce_sum x0 -> x1, other arithmetic: none -> 5.59 us  [on_device(): second = jnp.sum(first.astype(F32), axis=0).astype(BF16)]
    pallas_call x2 -> x3, Pallas kernels: 40.5 us -> 37.1 us  [the longest x1 31.1 us: expert(): pl.pallas_call(functools.partial(expert_kernel, steps=steps), grid=(2 * s...]
  transfers between devices with their start and end apart: 5 -> 7, of which waited for: 5 -> 5; matrix products, arithmetic and copies ran while one was open for 4% -> 6% of each run, Pallas kernels for 7% -> 9%
where the time goes in v3:
time: 253 us; the launch traced here: 252 us
  waiting for transfers between devices  106 us (42%)
  Pallas kernels  59.1 us (23%)
  starting transfers between devices  27.4 us (11%)
  blocking collectives  25.7 us (10%)
  between operations  14.2 us (6%)
  other arithmetic  10.4 us (4%)
  local copies, waits for them, and re-layouts  9.27 us (4%)
    all_to_all x3, waiting for transfers between devices, exchange(): return lax.all_to_all(value, axis, split_axis=0, concat_axis=0, tiled=True)  35.3 us
    all_gather x1, waiting for transfers between devices, on_device(): lax.all_gather(jnp.concatenate([x_tokens, out_grad], axis=0), both, axis=...  31.7 us
    pallas_call x1, Pallas kernels, expert(): pl.pallas_call(functools.partial(expert_kernel, steps=steps), grid=(2 * s...  31.1 us
    all_gather x1, waiting for transfers between devices, on_device(): spread = lax.all_gather(send, 'branch', axis=0, tiled=True)  25.8 us
    all_to_all x1, blocking collectives, exchange(): return lax.all_to_all(value, axis, split_axis=0, concat_axis=0, tiled=True)  25.7 us
    all_to_all x3, starting transfers between devices, exchange(): return lax.all_to_all(value, axis, split_axis=0, concat_axis=0, tiled=True)  18.6 us
    all_to_all x2, waiting for transfers between devices, stage(): lax.all_to_all(value, both, split_axis=0, concat_axis=0, axis_index_group...  12.7 us
    pallas_call x1, Pallas kernels, pick_rows(): pl.pallas_call(pick_kernel, grid=(steps,), in_specs=[pl.BlockSpec((1, tok...  11.9 us
  transfers between devices with their start and end apart: 7, of which 5 were waited for; matrix products, arithmetic and copies ran while one was open for 6% of the time, Pallas kernels for 9%

profile of v3, /device:TPU:1, one launch (start us, length us, event | category | flops | bytes accessed | tf_op | source)
XLA Modules:
  0.0 251.7 jit_solution(17562731152766019881)
XLA Ops:
  7.2 0.0 all-gather.3.cloned.1.call-start
  7.2 1.5 pad_maximum_fusion
  8.7 0.0 all-gather.3.cloned.1.call-update
  8.8 0.7 convert_element_type.30
  9.5 0.7 pad_maximum_fusion.1
  10.1 0.1 copy.54
  10.3 25.7 %all_to_all.30 = f32[128,8,128]{2,1,0:T(8,128)S(1)} all-to-all(f32[128,8,128]{2,1,0:T(8,128)S(1)} %broadcast_in_dim.10), channel_id=1, replica_groups=mesh['branch'=8,'wide'=16] {'branch','wide'}, dimensions={0} | all-to-all | bytes 1048576 | tf_op jit(solution)/shard_map/all_to_all | solution.py:285
  35.9 4.3 %all-to-all-start.1 = ((bf16[8,512,256]{2,1,0:T(8,128)(2,1)}), bf16[8,512,256]{2,1,0:T(8,128)(2,1)S(1)}, u32[]{:S(2)}, u32[]{:S(2)}) async-start(bf16[8,512,256]{2,1,0:T(8,128)(2,1)} %bitcast.11), calls=%async_computation.1 | async-start | bytes 4194304 | tf_op jit(solution)/shard_map/all_to_all | solution.py:285
  40.2 0.0 all-gather.5.cloned.1.call-start
  40.3 0.9 fusion.12
  41.2 1.2 copy.52
  42.4 0.2 copy.53
  42.7 0.1 copy.49
  42.8 0.1 convert_reduce_fusion.1
  42.9 0.1 copy.47
  43.0 0.7 select_n.143.place_ref
  43.7 1.0 reshape.186.prob_ref
  44.7 27.4 %all-to-all-done.1 = bf16[8,512,256]{2,1,0:T(8,128)(2,1)S(1)} async-done(((bf16[8,512,256]{2,1,0:T(8,128)(2,1)}), bf16[8,512,256]{2,1,0:T(8,128)(2,1)S(1)}, u32[]{:S(2)}, u32[]{:S(2)}) %all-to-all-start.1) | async-done | bytes 2097184 | tf_op jit(solution)/shard_map/all_to_all | solution.py:285
  72.1 0.3 convert_reduce_fusion
  72.4 0.7 multiply_convert_fusion
  73.2 31.7 %all-gather.3.cloned.1.call-done = bf16[2048,4096]{1,0:T(8,128)(2,1)} async-done(((bf16[16,4096]{1,0:T(8,128)(2,1)}), bf16[2048,4096]{1,0:T(8,128)(2,1)}) %all-gather.3.cloned.1.call-update) | async-done | bytes 16777232 | tf_op jit(solution)/shard_map/all_gather | solution.py:297
  104.9 31.1 %expert.1 = (bf16[16,72,384]{2,1,0:T(8,128)(2,1)}, bf16[16,2,24,4096]{3,2,1,0:T(8,128)(2,1)}) custom-call(s32[1,1024]{1,0:T(1,128)} %select_n.143.place_ref, f32[1024,1]{1,0:T(8,128)} %reshape.186.prob_ref, bf16[128,16,4096]{2,1,0:T(8,128)(2,1)} %bitcast.13, bf16[384,4096]{1,0:T(8,128)(2,1)} %bitcast.15, bf16[384,4096]{1,0:T(8,128)(2,1)} %bitcast.16, ...), custom_call_target="tpu_custom_call" | custom-call | flops 9663676416 | bytes 44040192 | tf_op jit(solution)/shard_map/expert/pallas_call | solution.py:101
  136.0 0.0 all-gather.5.cloned.1.call-update
  136.1 5.2 %all-to-all-start.2 = ((bf16[16,2,24,4096]{3,2,1,0:T(8,128)(2,1)}), bf16[16,2,24,4096]{3,2,1,0:T(8,128)(2,1)}, u32[]{:S(2)}, u32[]{:S(2)}) async-start(bf16[16,2,24,4096]{3,2,1,0:T(8,128)(2,1)} %get-tuple-element.24), calls=%async_computation.2 | async-start | bytes 12582912 | tf_op jit(solution)/shard_map/all_to_all | solution.py:323
  141.3 0.1 copy.51
  141.4 0.7 select_n.151.place_ref
  142.1 11.9 %pick_rows.1 = (bf16[384,4096]{1,0:T(8,128)(2,1)}, bf16[384,4096]{1,0:T(8,128)(2,1)}) custom-call(s32[1,1024]{1,0:T(1,128)} %select_n.151.place_ref, bf16[128,16,4096]{2,1,0:T(8,128)(2,1)} %bitcast.14), custom_call_target="tpu_custom_call" | custom-call | flops 6442450944 | bytes 25165824 | tf_op jit(solution)/shard_map/pick_rows/pallas_call | solution.py:150
  154.0 25.8 %all-gather.5.cloned.1.call-done = bf16[128,72,384]{2,1,0:T(8,128)(2,1)} async-done(((bf16[16,72,384]{2,1,0:T(8,128)(2,1)}), bf16[128,72,384]{2,1,0:T(8,128)(2,1)}) %all-gather.5.cloned.1.call-update) | async-done | bytes 7077904 | tf_op jit(solution)/shard_map/all_gather | solution.py:318
  179.9 2.2 constant_dynamic-slice_fusion
  182.0 0.0 all-to-all-done.2
  182.0 6.7 %all-to-all-start.3 = ((bf16[16,72,384]{2,1,0:T(8,128)(2,1)}), bf16[16,72,384]{2,1,0:T(8,128)(2,1)S(1)}, u32[]{:S(2)}, u32[]{:S(2)}) async-start(bf16[16,72,384]{2,1,0:T(8,128)(2,1)} %bitcast.6), calls=%async_computation.3 | async-start | bytes 1769472 | tf_op jit(solution)/shard_map/all_to_all | solution.py:285
  188.8 5.6 %reduce_sum.62 = bf16[4,2,24,4096]{3,2,1,0:T(8,128)(2,1)} reduce(bf16[4,4,2,24,4096]{4,3,2,1,0:T(8,128)(2,1)} %bitcast.7, bf16[]{:T(256)} %constant.109.clone.1), dimensions={0}, to_apply=%region_8.9 | reduce | flops 2359296 | bytes 7864322 | tf_op jit(solution)/shard_map/reduce_sum | solution.py:337
  194.3 0.0 copy-start.3
  194.3 7.9 %all-to-all-done.3.lhs_ref = bf16[16,72,384]{2,1,0:T(8,128)(2,1)S(1)} async-done(((bf16[16,72,384]{2,1,0:T(8,128)(2,1)}), bf16[16,72,384]{2,1,0:T(8,128)(2,1)S(1)}, u32[]{:S(2)}, u32[]{:S(2)}) %all-to-all-start.3) | async-done | bytes 884768 | tf_op jit(solution)/shard_map/all_to_all | solution.py:285
  202.2 0.0 copy-start.2
  202.2 3.6 %all-to-all-start.4 = ((bf16[4,2,24,4096]{3,2,1,0:T(8,128)(2,1)}), bf16[4,2,24,4096]{3,2,1,0:T(8,128)(2,1)S(1)}, u32[]{:S(2)}, u32[]{:S(2)}) async-start(bf16[4,2,24,4096]{3,2,1,0:T(8,128)(2,1)} %reduce_sum.62), calls=%async_computation.4 | async-start | bytes 3145728 | tf_op jit(solution)/shard_map/all_to_all | solution.py:323
  205.8 0.0 copy-done.3
  205.8 0.1 convert_reduce_fusion.3
  205.9 12.7 %all-to-all-done.4.got_ref = bf16[4,2,24,4096]{3,2,1,0:T(8,128)(2,1)S(1)} async-done(((bf16[4,2,24,4096]{3,2,1,0:T(8,128)(2,1)}), bf16[4,2,24,4096]{3,2,1,0:T(8,128)(2,1)S(1)}, u32[]{:S(2)}, u32[]{:S(2)}) %all-to-all-start.4) | async-done | bytes 1572896 | tf_op jit(solution)/shard_map/all_to_all | solution.py:323
  218.6 1.1 copy-done
  219.7 3.6 %gather_blocks.1 = bf16[8,8,4096]{2,1,0:T(8,128)(2,1)} custom-call(bf16[4,2,24,4096]{3,2,1,0:T(8,128)(2,1)} %copy-done), custom_call_target="tpu_custom_call" | custom-call | tf_op jit(solution)/shard_map/gather_blocks/pallas_call | solution.py:182
  223.3 0.0 copy-done.2
  223.3 7.6 %all-to-all-start.5 = ((bf16[8,8,4096]{2,1,0:T(8,128)(2,1)}), bf16[8,8,4096]{2,1,0:T(8,128)(2,1)S(1)}, u32[]{:S(2)}, u32[]{:S(2)}) async-start(bf16[8,8,4096]{2,1,0:T(8,128)(2,1)} %gather_blocks.1), calls=%async_computation.5 | async-start | bytes 1048576 | tf_op jit(solution)/shard_map/all_to_all | solution.py:285
  230.9 0.7 fusion.1.chosen_ref
  231.6 10.1 %weight_grads.1 = (bf16[384,4096]{1,0:T(8,128)(2,1)}, bf16[384,4096]{1,0:T(8,128)(2,1)}, bf16[384,4096]{1,0:T(8,128)(2,1)}) custom-call(bf16[16,72,384]{2,1,0:T(8,128)(2,1)} %copy-done.2, bf16[384,4096]{1,0:T(8,128)(2,1)} %get-tuple-element.35.x_ref, bf16[384,4096]{1,0:T(8,128)(2,1)} %get-tuple-element.36.g_ref), custom_call_target="tpu_custom_call" | custom-call | flops 3623878656 | bytes 16777216 | tf_op jit(solution)/shard_map/weight_grads/pallas_call | solution.py:242
  241.6 0.0 all-to-all-done.5.got_ref
  241.6 0.8 copy-done.1
  242.4 2.4 combine.1
  (12 shorter events, 0.1 us)
Async XLA Ops:
  7.2 97.7 %all-gather.3.cloned.1.call-start = ((), (), s32[]{:S(2)}) async-start(), calls=%async_computation.6 | async-start | bytes 16908288 | tf_op jit(solution)/shard_map/all_gather | solution.py:297
  35.9 36.2 %all-to-all-start.1 = ((bf16[8,512,256]{2,1,0:T(8,128)(2,1)}), bf16[8,512,256]{2,1,0:T(8,128)(2,1)S(1)}, u32[]{:S(2)}, u32[]{:S(2)}) async-start(bf16[8,512,256]{2,1,0:T(8,128)(2,1)} %bitcast.11), calls=%async_computation.1 | async-start | bytes 4194304 | tf_op jit(solution)/shard_map/all_to_all | solution.py:285
  40.2 139.6 %all-gather.5.cloned.1.call-start = ((), (), s32[]{:S(2)}) async-start(), calls=%async_computation.7 | async-start | bytes 7962624 | tf_op jit(solution)/shard_map/all_gather | solution.py:318
  136.1 46.0 %all-to-all-start.2 = ((bf16[16,2,24,4096]{3,2,1,0:T(8,128)(2,1)}), bf16[16,2,24,4096]{3,2,1,0:T(8,128)(2,1)}, u32[]{:S(2)}, u32[]{:S(2)}) async-start(bf16[16,2,24,4096]{3,2,1,0:T(8,128)(2,1)} %get-tuple-element.24), calls=%async_computation.2 | async-start | bytes 12582912 | tf_op jit(solution)/shard_map/all_to_all | solution.py:323
  182.0 20.2 %all-to-all-start.3 = ((bf16[16,72,384]{2,1,0:T(8,128)(2,1)}), bf16[16,72,384]{2,1,0:T(8,128)(2,1)S(1)}, u32[]{:S(2)}, u32[]{:S(2)}) async-start(bf16[16,72,384]{2,1,0:T(8,128)(2,1)} %bitcast.6), calls=%async_computation.3 | async-start | bytes 1769472 | tf_op jit(solution)/shard_map/all_to_all | solution.py:285
  194.3 11.5 %copy-start.3 = (s32[8,2]{0,1:T(2,128)S(1)}, s32[8,2]{0,1:T(2,128)}, u32[]{:S(2)}) copy-start(s32[8,2]{0,1:T(2,128)} %param.10) | copy-start | bytes 196
  202.2 21.1 %copy-start.2 = (bf16[16,72,384]{2,1,0:T(8,128)(2,1)}, bf16[16,72,384]{2,1,0:T(8,128)(2,1)S(1)}, u32[]{:S(2)}) copy-start(bf16[16,72,384]{2,1,0:T(8,128)(2,1)S(1)} %all-to-all-done.3.lhs_ref) | copy-start | bytes 2654212
  202.2 16.4 %all-to-all-start.4 = ((bf16[4,2,24,4096]{3,2,1,0:T(8,128)(2,1)}), bf16[4,2,24,4096]{3,2,1,0:T(8,128)(2,1)S(1)}, u32[]{:S(2)}, u32[]{:S(2)}) async-start(bf16[4,2,24,4096]{3,2,1,0:T(8,128)(2,1)} %reduce_sum.62), calls=%async_computation.4 | async-start | bytes 3145728 | tf_op jit(solution)/shard_map/all_to_all | solution.py:323
  218.6 1.1 copy-start
  223.3 18.3 %all-to-all-start.5 = ((bf16[8,8,4096]{2,1,0:T(8,128)(2,1)}), bf16[8,8,4096]{2,1,0:T(8,128)(2,1)S(1)}, u32[]{:S(2)}, u32[]{:S(2)}) async-start(bf16[8,8,4096]{2,1,0:T(8,128)(2,1)} %gather_blocks.1), calls=%async_computation.5 | async-start | bytes 1048576 | tf_op jit(solution)/shard_map/all_to_all | solution.py:285
  241.6 0.8 copy-start.1
Sparse Core Ops, SparseCore 0:
  11.7 93.1 all-gather.2
  136.2 43.6 all-gather.4

commit v4 on v3

--- a/solution.py
+++ b/solution.py
@@ -13,6 +13,9 @@
 SIDE = 4
 LAST = (((1,), (1,)), ((), ()))
 PARAMS = pltpu.CompilerParams(vmem_limit_bytes=58 * 1024 * 1024)
+
+
+SMALL = pltpu.CompilerParams(vmem_limit_bytes=16 * 1024 * 1024)
 
 
 def split_rows(rows_ref):
@@ -32,7 +35,7 @@
 def expert_kernel(
     place_ref, prob_ref, rows_ref, wg_ref, wu_ref, wd_ref,
     send_ref, back_ref,
-    gate_acc, up_acc, hg_acc, acts, *, steps,
+    gate_acc, up_acc, hg_acc, acts, kept, *, steps,
 ):
     step = pl.program_id(0)
     slots = acts.shape[1]
@@ -40,8 +43,11 @@
     @pl.when(step < steps)
     def _():
         x, g = split_rows(rows_ref)
-        for acc, lhs, w_ref in ((gate_acc, x, wg_ref), (up_acc, x, wu_ref), (hg_acc, g, wd_ref)):
-            part = lax.dot_general(lhs, w_ref[...], LAST, preferred_element_type=F32)
+        ops = ((gate_acc, x, wg_ref), (up_acc, x, wu_ref), (hg_acc, g, wd_ref))
+        for n, (acc, rhs, w_ref) in enumerate(ops):
+            w = w_ref[...]
+            kept[step, n] = w
+            part = lax.dot_general(w, rhs, LAST, preferred_element_type=F32)
 
             @pl.when(step == 0)
             def _(acc=acc, part=part):
@@ -69,20 +75,21 @@
         height = stacked // 3
         turned = []
         for n, value in enumerate(values):
-            got = jnp.dot(pick, value.astype(BF16), preferred_element_type=F32)
-            acts[n] = got.astype(BF16)
-            turned.append(got.T.reshape(pieces, height, slots))
+            got = lax.dot_general(value.astype(BF16), pick, LAST, preferred_element_type=F32)
+            acts[n] = got.T.astype(BF16)
+            turned.append(got.reshape(pieces, height, slots))
         send_ref[...] = jnp.concatenate(turned, axis=1).astype(BF16)
 
     @pl.when(step >= steps)
     def _():
-        out = jnp.dot(acts[2], wd_ref[...], preferred_element_type=F32)
-        grad = jnp.dot(acts[0], wg_ref[...], preferred_element_type=F32) + jnp.dot(
-            acts[1], wu_ref[...], preferred_element_type=F32
+        tile = step - steps
+        out = jnp.dot(acts[2], kept[tile, 2], preferred_element_type=F32)
+        grad = jnp.dot(acts[0], kept[tile, 0], preferred_element_type=F32) + jnp.dot(
+            acts[1], kept[tile, 1], preferred_element_type=F32
         )
-        wide, _, height, tile = back_ref.shape
-        back_ref[:, 0] = out.reshape(wide, height, tile).astype(BF16)
-        back_ref[:, 1] = grad.reshape(wide, height, tile).astype(BF16)
+        wide, _, height, width = back_ref.shape
+        back_ref[:, 0] = out.reshape(wide, height, width).astype(BF16)
+        back_ref[:, 1] = grad.reshape(wide, height, width).astype(BF16)
 
 
 def expert(place, prob, rows, wg, wu, wd, pieces):
@@ -92,18 +99,14 @@
     tokens = place.shape[1]
     steps = 4
     tile = features // steps
-
-    def wtile(i):
-        return (0, jnp.where(i < steps, i, i - steps))
-
-    wspec = pl.BlockSpec((hidden, tile), wtile)
+    wspec = pl.BlockSpec((hidden, tile), lambda i: (0, jnp.minimum(i, steps - 1)))
+    line = pl.BlockSpec((1, tokens), lambda i: (0, 0))
     stacked = 3 * hidden // pieces
     return pl.pallas_call(
         functools.partial(expert_kernel, steps=steps),
         grid=(2 * steps,),
         in_specs=[
-            pl.BlockSpec((1, tokens), lambda i: (0, 0)),
-            pl.BlockSpec((tokens, 1), lambda i: (0, 0)),
+            line, line,
             pl.BlockSpec((blocks, per_block, tile), lambda i: (0, 0, jnp.minimum(i, steps - 1))),
             wspec, wspec, wspec,
         ],
@@ -118,15 +121,16 @@
             jax.ShapeDtypeStruct((pieces, 2, slots // pieces, features), BF16),
         ],
         scratch_shapes=[
-            pltpu.VMEM((tokens, hidden), F32),
-            pltpu.VMEM((tokens, hidden), F32),
-            pltpu.VMEM((tokens, hidden), F32),
+            pltpu.VMEM((hidden, tokens), F32),
+            pltpu.VMEM((hidden, tokens), F32),
+            pltpu.VMEM((hidden, tokens), F32),
             pltpu.VMEM((3, slots, hidden), BF16),
+            pltpu.VMEM((steps, 3, hidden, tile), BF16),
         ],
         compiler_params=PARAMS,
         cost_estimate=pl.CostEstimate(
             flops=6 * tokens * features * hidden,
-            bytes_accessed=42 * 1024 * 1024,
+            bytes_accessed=33 * 1024 * 1024,
             transcendentals=tokens * hidden,
         ),
         name="expert",
@@ -185,7 +189,7 @@
         in_specs=[pl.BlockSpec((parts, 2, height, tile), lambda i: (0, 0, 0, i))],
         out_specs=pl.BlockSpec((experts, 8, tile), lambda i: (0, 0, i)),
         out_shape=jax.ShapeDtypeStruct((experts, 8, features), BF16),
-        compiler_params=PARAMS,
+        compiler_params=SMALL,
         name="gather_blocks",
     )(got)
 
@@ -217,7 +221,7 @@
         ],
         out_specs=[spec, spec],
         out_shape=[jax.ShapeDtypeStruct((tokens, features), BF16)] * 2,
-        compiler_params=PARAMS,
+        compiler_params=SMALL,
         name="combine",
     )(chosen, got)
 
@@ -307,18 +311,21 @@
     place, weight = route_places(ids, probs, branch_index, wide)
     other_place, _ = route_places(ids, probs, wide_index // (wide // experts), wide)
 
-    attn = exchange(attn_out[0].reshape(experts, -1, attn_out.shape[2]), "branch")
-    merged_attn = (jnp.sum(attn.astype(F32), axis=0) * (1.0 / experts)).astype(BF16)
-    gathered, merged_attn = lax.optimization_barrier((gathered, merged_attn))
+    scaled = (attn_out[0].astype(F32) * (1.0 / experts)).astype(BF16)
+    gathered, scaled = lax.optimization_barrier((gathered, scaled))
 
     send, back = expert(
-        place, weight.reshape(-1, 1), gathered, w_gate[0], w_up[0], w_down[0], wide
+        place, weight.reshape(1, -1), gathered, w_gate[0], w_up[0], w_down[0], wide
     )
 
     spread = lax.all_gather(send, "branch", axis=0, tiled=True)
+    xe, ge = pick_rows(other_place, gathered)
+    spread, scaled, xe, ge = lax.optimization_barrier((spread, scaled, xe, ge))
     spread = spread.reshape((experts, wide) + send.shape[1:])
     copies = wide // experts
     mine = lax.dynamic_slice_in_dim(spread, branch_index * copies, copies, 1)
+    merged_attn = lax.psum_scatter(scaled, "branch", scatter_dimension=0, tiled=True)
+
     def stage(value, odd):
         return lax.all_to_all(
             value,
@@ -330,8 +337,7 @@
         )
 
     first = stage(back, 0)
-    xe, ge = pick_rows(other_place, gathered)
-    first, mine, xe, ge = lax.optimization_barrier((first, mine.reshape(send.shape), xe, ge))
+    first, mine = lax.optimization_barrier((first, mine.reshape(send.shape)))
     relayed = exchange(mine, "wide")
     first = first.reshape((SIDE, SIDE) + back.shape[1:])
     second = jnp.sum(first.astype(F32), axis=0).astype(BF16)

time: 253 us -> 235 us (0.929)
  blocking collectives: 25.7 us -> 0 us
  waiting for transfers between devices: 106 us -> 115 us
  Pallas kernels: 59.1 us -> 51.6 us
  starting transfers between devices: 27.4 us -> 34.7 us
  local copies, waits for them, and re-layouts: 9.27 us -> 6.13 us
    all_gather x1, waiting for transfers between devices: 31.7 us -> 58.1 us  [on_device(): lax.all_gather(jnp.concatenate([x_tokens, out_grad], axis=0), both, axis=...]
    all_to_all x1 -> x0, blocking collectives: 25.7 us -> none  [exchange(): return lax.all_to_all(value, axis, split_axis=0, concat_axis=0, tiled=True)]
    all_to_all x3, waiting for transfers between devices: 35.3 us -> 18.4 us  [exchange(): return lax.all_to_all(value, axis, split_axis=0, concat_axis=0, tiled=True)]
    all_to_all x3, starting transfers between devices: 18.6 us -> 25.7 us  [exchange(): return lax.all_to_all(value, axis, split_axis=0, concat_axis=0, tiled=True)]
    pallas_call x1, Pallas kernels: 31.1 us -> 26.3 us  [expert(): pl.pallas_call(functools.partial(expert_kernel, steps=steps), grid=(2 * s...]
    unnamed x11 -> x7, local copies, waits for them, and re-layouts: 3.45 us -> 0.53 us
    convert_element_type x1, other arithmetic: 0.74 us -> 3.33 us  [on_device(): scaled = (attn_out[0].astype(F32) * (1.0 / experts)).astype(BF16)]
  transfers between devices with their start and end apart: 7 -> 8, of which waited for: 5 -> 5; matrix products, arithmetic and copies ran while one was open for 6% -> 7% of each run, Pallas kernels for 9% -> 11%
where the time goes in v4:
time: 235 us; the launch traced here: 234 us
  waiting for transfers between devices  115 us (49%)
  Pallas kernels  51.6 us (22%)
  starting transfers between devices  34.7 us (15%)
  between operations  13.9 us (6%)
  other arithmetic  12.3 us (5%)
  local copies, waits for them, and re-layouts  6.13 us (3%)
    all_gather x1, waiting for transfers between devices, on_device(): lax.all_gather(jnp.concatenate([x_tokens, out_grad], axis=0), both, axis=...  58.1 us
    pallas_call x1, Pallas kernels, expert(): pl.pallas_call(functools.partial(expert_kernel, steps=steps), grid=(2 * s...  26.3 us
    all_gather x1, waiting for transfers between devices, on_device(): spread = lax.all_gather(send, 'branch', axis=0, tiled=True)  25.8 us
    all_to_all x3, starting transfers between devices, exchange(): return lax.all_to_all(value, axis, split_axis=0, concat_axis=0, tiled=True)  25.7 us
    all_to_all x3, waiting for transfers between devices, exchange(): return lax.all_to_all(value, axis, split_axis=0, concat_axis=0, tiled=True)  18.4 us
    all_to_all x2, waiting for transfers between devices, stage(): lax.all_to_all(value, both, split_axis=0, concat_axis=0, axis_index_group...  12.7 us
    pallas_call x1, Pallas kernels, pick_rows(): pl.pallas_call(pick_kernel, grid=(steps,), in_specs=[pl.BlockSpec((1, tok...  11.9 us
    pallas_call x1, Pallas kernels, weight_grads(): pl.pallas_call(weights_kernel, grid=(features // tile,), in_specs=[pl.Blo...  10.1 us
  transfers between devices with their start and end apart: 8, of which 5 were waited for; matrix products, arithmetic and copies ran while one was open for 7% of the time, Pallas kernels for 11%

profile of v4, /device:TPU:1, one launch (start us, length us, event | category | flops | bytes accessed | tf_op | source)
XLA Modules:
  0.0 233.6 jit_solution(16062631484485355997)
XLA Ops:
  7.2 0.0 all-gather.3.cloned.1.call-start
  7.2 1.5 pad_maximum_fusion
  8.7 0.0 all-gather.3.cloned.1.call-update
  8.8 0.7 convert_element_type.34
  9.5 0.7 pad_maximum_fusion.1
  10.1 0.1 copy.48
  10.2 0.8 broadcast_in_dim.10
  11.1 11.5 %all-to-all-start = ((f32[128,8,128]{2,1,0:T(8,128)}), f32[128,8,128]{2,1,0:T(8,128)S(1)}, u32[]{:S(2)}, u32[]{:S(2)}) async-start(f32[128,8,128]{2,1,0:T(8,128)} %broadcast_in_dim.10), calls=%async_computation | async-start | bytes 1048576 | tf_op jit(solution)/shard_map/all_to_all | solution.py:289
  22.6 0.0 all-gather.5.cloned.1.call-start
  22.6 3.3 %fusion = bf16[4096,256]{1,0:T(8,128)(2,1)} fusion(bf16[1,4096,256]{2,1,0:T(8,128)(2,1)} %param.15), kind=kLoop, calls=%fused_computation.1 | loop fusion | flops 3145728 | bytes 4194304 | tf_op jit(solution)/shard_map/convert_element_type | solution.py:314
  26.0 10.6 %all-to-all-done = f32[128,8,128]{2,1,0:T(8,128)S(1)} async-done(((f32[128,8,128]{2,1,0:T(8,128)}), f32[128,8,128]{2,1,0:T(8,128)S(1)}, u32[]{:S(2)}, u32[]{:S(2)}) %all-to-all-start) | async-done | bytes 524320 | tf_op jit(solution)/shard_map/all_to_all | solution.py:289
  36.6 0.2 fusion.13
  36.8 0.2 copy.46
  37.0 0.2 copy.47
  37.3 0.1 copy.44
  37.4 0.7 reshape.182.prob_ref
  38.1 0.1 convert_reduce_fusion
  38.2 0.1 copy.42
  38.3 0.7 select_n.143.place_ref
  39.0 58.1 %all-gather.3.cloned.1.call-done = bf16[2048,4096]{1,0:T(8,128)(2,1)} async-done(((bf16[16,4096]{1,0:T(8,128)(2,1)}), bf16[2048,4096]{1,0:T(8,128)(2,1)}) %all-gather.3.cloned.1.call-update) | async-done | bytes 16777232 | tf_op jit(solution)/shard_map/all_gather | solution.py:301
  97.1 26.3 %expert.1 = (bf16[16,72,384]{2,1,0:T(8,128)(2,1)}, bf16[16,2,24,4096]{3,2,1,0:T(8,128)(2,1)}) custom-call(s32[1,1024]{1,0:T(1,128)} %select_n.143.place_ref, f32[1,1024]{1,0:T(1,128)} %reshape.182.prob_ref, bf16[128,16,4096]{2,1,0:T(8,128)(2,1)} %bitcast.13, bf16[384,4096]{1,0:T(8,128)(2,1)} %bitcast.15, bf16[384,4096]{1,0:T(8,128)(2,1)} %bitcast.16, ...), custom_call_target="tpu_custom_call" | custom-call | flops 9663676416 | bytes 34603008 | tf_op jit(solution)/shard_map/expert/pallas_call | solution.py:105
  123.4 0.0 all-gather.5.cloned.1.call-update
  123.5 5.2 %all-to-all-start.1 = ((bf16[16,2,24,4096]{3,2,1,0:T(8,128)(2,1)}), bf16[16,2,24,4096]{3,2,1,0:T(8,128)(2,1)}, u32[]{:S(2)}, u32[]{:S(2)}) async-start(bf16[16,2,24,4096]{3,2,1,0:T(8,128)(2,1)} %get-tuple-element.26), calls=%async_computation.1 | async-start | bytes 12582912 | tf_op jit(solution)/shard_map/all_to_all | solution.py:330
  128.7 0.0 reduce-scatter.2.cloned.1.call-start
  128.7 0.1 copy.45
  128.9 0.7 select_n.150.place_ref
  129.5 11.9 %pick_rows.1 = (bf16[384,4096]{1,0:T(8,128)(2,1)}, bf16[384,4096]{1,0:T(8,128)(2,1)}) custom-call(s32[1,1024]{1,0:T(1,128)} %select_n.150.place_ref, bf16[128,16,4096]{2,1,0:T(8,128)(2,1)} %bitcast.14), custom_call_target="tpu_custom_call" | custom-call | flops 6442450944 | bytes 25165824 | tf_op jit(solution)/shard_map/pick_rows/pallas_call | solution.py:154
  141.5 25.8 %all-gather.5.cloned.1.call-done = bf16[128,72,384]{2,1,0:T(8,128)(2,1)} async-done(((bf16[16,72,384]{2,1,0:T(8,128)(2,1)}), bf16[128,72,384]{2,1,0:T(8,128)(2,1)}) %all-gather.5.cloned.1.call-update) | async-done | bytes 7077904 | tf_op jit(solution)/shard_map/all_gather | solution.py:321
  167.3 0.0 reduce-scatter.2.cloned.1.call-update
  167.3 2.2 constant_dynamic-slice_fusion
  169.5 0.0 all-to-all-done.1
  169.5 6.7 %all-to-all-start.2 = ((bf16[16,72,384]{2,1,0:T(8,128)(2,1)}), bf16[16,72,384]{2,1,0:T(8,128)(2,1)S(1)}, u32[]{:S(2)}, u32[]{:S(2)}) async-start(bf16[16,72,384]{2,1,0:T(8,128)(2,1)} %bitcast.6), calls=%async_computation.2 | async-start | bytes 1769472 | tf_op jit(solution)/shard_map/all_to_all | solution.py:289
  176.2 5.7 %reduce_sum.52 = bf16[4,2,24,4096]{3,2,1,0:T(8,128)(2,1)} reduce(bf16[4,4,2,24,4096]{4,3,2,1,0:T(8,128)(2,1)} %bitcast.7, bf16[]{:T(256)} %constant.109.clone.1), dimensions={0}, to_apply=%region_7.8 | reduce | flops 2359296 | bytes 7864322 | tf_op jit(solution)/shard_map/reduce_sum | solution.py:343
  181.9 0.0 copy-start.1
  181.9 7.8 %all-to-all-done.2.lhs_ref = bf16[16,72,384]{2,1,0:T(8,128)(2,1)S(1)} async-done(((bf16[16,72,384]{2,1,0:T(8,128)(2,1)}), bf16[16,72,384]{2,1,0:T(8,128)(2,1)S(1)}, u32[]{:S(2)}, u32[]{:S(2)}) %all-to-all-start.2) | async-done | bytes 884768 | tf_op jit(solution)/shard_map/all_to_all | solution.py:289
  189.7 0.0 copy-start
  189.7 3.6 %all-to-all-start.3 = ((bf16[4,2,24,4096]{3,2,1,0:T(8,128)(2,1)}), bf16[4,2,24,4096]{3,2,1,0:T(8,128)(2,1)S(1)}, u32[]{:S(2)}, u32[]{:S(2)}) async-start(bf16[4,2,24,4096]{3,2,1,0:T(8,128)(2,1)} %reduce_sum.52), calls=%async_computation.3 | async-start | bytes 3145728 | tf_op jit(solution)/shard_map/all_to_all | solution.py:330
  193.3 0.0 copy-done.1
  193.3 0.1 convert_reduce_fusion.2
  193.4 12.7 %all-to-all-done.3.got_ref = bf16[4,2,24,4096]{3,2,1,0:T(8,128)(2,1)S(1)} async-done(((bf16[4,2,24,4096]{3,2,1,0:T(8,128)(2,1)}), bf16[4,2,24,4096]{3,2,1,0:T(8,128)(2,1)S(1)}, u32[]{:S(2)}, u32[]{:S(2)}) %all-to-all-start.3) | async-done | bytes 1572896 | tf_op jit(solution)/shard_map/all_to_all | solution.py:330
  206.1 1.8 gather_blocks.1
  207.8 0.0 copy-done
  207.8 7.5 %all-to-all-start.4 = ((bf16[8,8,4096]{2,1,0:T(8,128)(2,1)}), bf16[8,8,4096]{2,1,0:T(8,128)(2,1)S(1)}, u32[]{:S(2)}, u32[]{:S(2)}) async-start(bf16[8,8,4096]{2,1,0:T(8,128)(2,1)} %gather_blocks.1), calls=%async_computation.4 | async-start | bytes 1048576 | tf_op jit(solution)/shard_map/all_to_all | solution.py:289
  215.4 0.1 fusion.2.chosen_ref
  215.5 10.1 %weight_grads.1 = (bf16[384,4096]{1,0:T(8,128)(2,1)}, bf16[384,4096]{1,0:T(8,128)(2,1)}, bf16[384,4096]{1,0:T(8,128)(2,1)}) custom-call(bf16[16,72,384]{2,1,0:T(8,128)(2,1)} %copy-done, bf16[384,4096]{1,0:T(8,128)(2,1)} %get-tuple-element.39.x_ref, bf16[384,4096]{1,0:T(8,128)(2,1)} %get-tuple-element.40.g_ref), custom_call_target="tpu_custom_call" | custom-call | flops 3623878656 | bytes 16777216 | tf_op jit(solution)/shard_map/weight_grads/pallas_call | solution.py:246
  225.6 0.0 all-to-all-done.4.got_ref
  225.6 1.5 combine.1
  227.1 0.0 reduce-scatter.2.cloned.1.call-done
  (9 shorter events, 0.1 us)
Async XLA Ops:
  7.2 90.0 %all-gather.3.cloned.1.call-start = ((), (), s32[]{:S(2)}) async-start(), calls=%async_computation.6 | async-start | bytes 16908288 | tf_op jit(solution)/shard_map/all_gather | solution.py:301
  11.1 25.6 %all-to-all-start = ((f32[128,8,128]{2,1,0:T(8,128)}), f32[128,8,128]{2,1,0:T(8,128)S(1)}, u32[]{:S(2)}, u32[]{:S(2)}) async-start(f32[128,8,128]{2,1,0:T(8,128)} %broadcast_in_dim.10), calls=%async_computation | async-start | bytes 1048576 | tf_op jit(solution)/shard_map/all_to_all | solution.py:289
  22.6 144.7 %all-gather.5.cloned.1.call-start = ((), (), s32[]{:S(2)}) async-start(), calls=%async_computation.7 | async-start | bytes 7962624 | tf_op jit(solution)/shard_map/all_gather | solution.py:321
  123.5 46.0 %all-to-all-start.1 = ((bf16[16,2,24,4096]{3,2,1,0:T(8,128)(2,1)}), bf16[16,2,24,4096]{3,2,1,0:T(8,128)(2,1)}, u32[]{:S(2)}, u32[]{:S(2)}) async-start(bf16[16,2,24,4096]{3,2,1,0:T(8,128)(2,1)} %get-tuple-element.26), calls=%async_computation.1 | async-start | bytes 12582912 | tf_op jit(solution)/shard_map/all_to_all | solution.py:330
  128.7 98.4 %reduce-scatter.2.cloned.1.call-start = ((), (), s32[]{:S(2)}) async-start(), calls=%async_computation.8 | async-start | bytes 2359296 | tf_op jit(solution)/shard_map/reduce_scatter | solution.py:327
  169.5 20.2 %all-to-all-start.2 = ((bf16[16,72,384]{2,1,0:T(8,128)(2,1)}), bf16[16,72,384]{2,1,0:T(8,128)(2,1)S(1)}, u32[]{:S(2)}, u32[]{:S(2)}) async-start(bf16[16,72,384]{2,1,0:T(8,128)(2,1)} %bitcast.6), calls=%async_computation.2 | async-start | bytes 1769472 | tf_op jit(solution)/shard_map/all_to_all | solution.py:289
  181.9 11.4 %copy-start.1 = (s32[8,2]{0,1:T(2,128)S(1)}, s32[8,2]{0,1:T(2,128)}, u32[]{:S(2)}) copy-start(s32[8,2]{0,1:T(2,128)} %param.10) | copy-start | bytes 196
  189.7 18.2 %copy-start = (bf16[16,72,384]{2,1,0:T(8,128)(2,1)}, bf16[16,72,384]{2,1,0:T(8,128)(2,1)S(1)}, u32[]{:S(2)}) copy-start(bf16[16,72,384]{2,1,0:T(8,128)(2,1)S(1)} %all-to-all-done.2.lhs_ref) | copy-start | bytes 2654212
  189.7 16.4 %all-to-all-start.3 = ((bf16[4,2,24,4096]{3,2,1,0:T(8,128)(2,1)}), bf16[4,2,24,4096]{3,2,1,0:T(8,128)(2,1)S(1)}, u32[]{:S(2)}, u32[]{:S(2)}) async-start(bf16[4,2,24,4096]{3,2,1,0:T(8,128)(2,1)} %reduce_sum.52), calls=%async_computation.3 | async-start | bytes 3145728 | tf_op jit(solution)/shard_map/all_to_all | solution.py:330
  207.8 17.7 %all-to-all-start.4 = ((bf16[8,8,4096]{2,1,0:T(8,128)(2,1)}), bf16[8,8,4096]{2,1,0:T(8,128)(2,1)S(1)}, u32[]{:S(2)}, u32[]{:S(2)}) async-start(bf16[8,8,4096]{2,1,0:T(8,128)(2,1)} %gather_blocks.1), calls=%async_computation.4 | async-start | bytes 1048576 | tf_op jit(solution)/shard_map/all_to_all | solution.py:289
Sparse Core Ops, SparseCore 0:
  11.7 85.3 all-gather.2
  123.6 43.6 all-gather.4
  170.3 30.7 reduce-scatter.1

commit v5 on v4

--- a/solution.py
+++ b/solution.py
@@ -35,7 +35,7 @@
 def expert_kernel(
     place_ref, prob_ref, rows_ref, wg_ref, wu_ref, wd_ref,
     send_ref, back_ref,
-    gate_acc, up_acc, hg_acc, acts, kept, *, steps,
+    pair_acc, hg_acc, acts, kept, *, steps,
 ):
     step = pl.program_id(0)
     slots = acts.shape[1]
@@ -43,10 +43,10 @@
     @pl.when(step < steps)
     def _():
         x, g = split_rows(rows_ref)
-        ops = ((gate_acc, x, wg_ref), (up_acc, x, wu_ref), (hg_acc, g, wd_ref))
-        for n, (acc, rhs, w_ref) in enumerate(ops):
-            w = w_ref[...]
-            kept[step, n] = w
+        for n, w_ref in enumerate((wg_ref, wu_ref, wd_ref)):
+            kept[step, n] = w_ref[...]
+        pair = jnp.concatenate([wg_ref[...], wu_ref[...]], axis=0)
+        for acc, w, rhs in ((pair_acc, pair, x), (hg_acc, wd_ref[...], g)):
             part = lax.dot_general(w, rhs, LAST, preferred_element_type=F32)
 
             @pl.when(step == 0)
@@ -60,8 +60,9 @@
     @pl.when(step == steps)
     def _():
         prob = prob_ref[...]
-        gate = gate_acc[...]
-        up = up_acc[...]
+        hidden = hg_acc.shape[0]
+        gate = pair_acc[:hidden]
+        up = pair_acc[hidden:]
         sig = jax.nn.sigmoid(gate)
         back = hg_acc[...] * prob
         gate_sig = gate * sig
@@ -121,8 +122,7 @@
             jax.ShapeDtypeStruct((pieces, 2, slots // pieces, features), BF16),
         ],
         scratch_shapes=[
-            pltpu.VMEM((hidden, tokens), F32),
-            pltpu.VMEM((hidden, tokens), F32),
+            pltpu.VMEM((2 * hidden, tokens), F32),
             pltpu.VMEM((hidden, tokens), F32),
             pltpu.VMEM((3, slots, hidden), BF16),
             pltpu.VMEM((steps, 3, hidden, tile), BF16),
@@ -168,8 +168,35 @@
     )(place, rows)
 
 
-def gather_kernel(got_ref, ret_ref):
-    total = jnp.sum(got_ref[...].astype(F32), axis=0)
+def first_sum_kernel(position_ref, got_ref, *refs):
+    total, outs = refs[-1], refs[:-1]
+    total[...] = jnp.sum(got_ref[...].astype(F32), axis=0)
+    for distance, ref in enumerate(outs):
+        ref[...] = total[lax.rem(position_ref[0] + distance, len(outs))].astype(BF16)
+
+
+def first_sum(position, got):
+    parts, _, _, height, features = got.shape
+    steps = 4
+    tile = features // steps
+    return pl.pallas_call(
+        first_sum_kernel,
+        grid=(steps,),
+        in_specs=[
+            pl.BlockSpec(memory_space=pltpu.SMEM),
+            pl.BlockSpec((parts, parts, 2, height, tile), lambda i: (0, 0, 0, 0, i)),
+        ],
+        out_specs=[pl.BlockSpec((2, height, tile), lambda i: (0, 0, i))] * parts,
+        out_shape=[jax.ShapeDtypeStruct((2, height, features), BF16)] * parts,
+        scratch_shapes=[pltpu.VMEM((parts, 2, height, tile), F32)],
+        compiler_params=SMALL,
+        name="first_sum",
+    )(position, got)
+
+
+def gather_kernel(*refs):
+    ret_ref = refs[-1]
+    total = sum(ref[...].astype(F32) for ref in refs[:-1])
     experts, padded, tile = ret_ref.shape
     blank = jnp.zeros((padded // 2 - CAP, tile), F32)
     for block in range(experts):
@@ -180,18 +207,18 @@
 
 
 def gather_blocks(got, experts):
-    parts, _, height, features = got.shape
+    _, height, features = got[0].shape
     steps = 4
     tile = features // steps
     return pl.pallas_call(
         gather_kernel,
         grid=(steps,),
-        in_specs=[pl.BlockSpec((parts, 2, height, tile), lambda i: (0, 0, 0, i))],
+        in_specs=[pl.BlockSpec((2, height, tile), lambda i: (0, 0, i))] * len(got),
         out_specs=pl.BlockSpec((experts, 8, tile), lambda i: (0, 0, i)),
         out_shape=jax.ShapeDtypeStruct((experts, 8, features), BF16),
         compiler_params=SMALL,
         name="gather_blocks",
-    )(got)
+    )(*got)
 
 
 def combine_kernel(chosen_ref, got_ref, mixed_ref, grad_ref):
@@ -326,23 +353,29 @@
     mine = lax.dynamic_slice_in_dim(spread, branch_index * copies, copies, 1)
     merged_attn = lax.psum_scatter(scaled, "branch", scatter_dimension=0, tiled=True)
 
-    def stage(value, odd):
-        return lax.all_to_all(
-            value,
-            both,
-            split_axis=0,
-            concat_axis=0,
-            axis_index_groups=stage_groups(experts, wide, odd),
-            tiled=True,
-        )
-
-    first = stage(back, 0)
+    first = lax.all_to_all(
+        back,
+        both,
+        split_axis=0,
+        concat_axis=0,
+        axis_index_groups=stage_groups(experts, wide, 0),
+        tiled=True,
+    )
     first, mine = lax.optimization_barrier((first, mine.reshape(send.shape)))
     relayed = exchange(mine, "wide")
-    first = first.reshape((SIDE, SIDE) + back.shape[1:])
-    second = jnp.sum(first.astype(F32), axis=0).astype(BF16)
-    second, relayed = lax.optimization_barrier((second, relayed))
-    returned = gather_blocks(stage(second, 1), experts)
+    position = jnp.where(branch_index % 2 == 0, wide_index % SIDE, wide_index // SIDE)
+    sums = first_sum(
+        position.astype(jnp.int32).reshape(1), first.reshape((SIDE, SIDE) + back.shape[1:])
+    )
+    second = [sums[0]]
+    for distance in range(1, SIDE):
+        pairs = [
+            (group[n], group[(n + distance) % SIDE])
+            for group in stage_groups(experts, wide, 1)
+            for n in range(SIDE)
+        ]
+        second.append(lax.ppermute(sums[distance], both, pairs))
+    returned = gather_blocks(second, experts)
     grad_gate, grad_up, grad_down = weight_grads(relayed, xe, ge)
     got = exchange(returned, "branch")
 

time: 235 us -> 224 us (0.953)
  waiting for transfers between devices: 115 us -> 107 us
  other arithmetic: 12.3 us -> 6.56 us
  Pallas kernels: 51.6 us -> 55.9 us
    ppermute x0 -> x3, waiting for transfers between devices: none -> 12.8 us  [on_device(): second.append(lax.ppermute(sums[distance], both, pairs))]
    all_to_all x2 -> x1, waiting for transfers between devices: 12.7 us -> 0.01 us  [on_device(): lax.all_to_all(back, both, split_axis=0, concat_axis=0, axis_index_groups...]
    all_to_all x3, waiting for transfers between devices: 18.4 us -> 10.6 us  [exchange(): return lax.all_to_all(value, axis, split_axis=0, concat_axis=0, tiled=True)]
    reduce_sum x1 -> x0, other arithmetic: 5.71 us -> none  [on_device(): second = jnp.sum(first.astype(F32), axis=0).astype(BF16)]
    ppermute x0 -> x3, starting transfers between devices: none -> 4.99 us  [on_device(): second.append(lax.ppermute(sums[distance], both, pairs))]
    pallas_call x1 -> x2, Pallas kernels: 1.76 us -> 6.04 us  [the longest x1 4.26 us: first_sum(): pl.pallas_call(first_sum_kernel, grid=(steps,), in_specs=[pl.BlockSpec(me...]
    all_to_all x2 -> x1, starting transfers between devices: 8.8 us -> 5.25 us  [on_device(): lax.all_to_all(back, both, split_axis=0, concat_axis=0, axis_index_groups...]
    all_to_all x3, starting transfers between devices: 25.7 us -> 23.2 us  [exchange(): return lax.all_to_all(value, axis, split_axis=0, concat_axis=0, tiled=True)]
  transfers between devices with their start and end apart: 8 -> 10, of which waited for: 5 -> 5; matrix products, arithmetic and copies ran while one was open for 7% -> 5% of each run, Pallas kernels for 11% -> 13%
where the time goes in v5:
time: 224 us; the launch traced here: 223 us
  waiting for transfers between devices  107 us (48%)
  Pallas kernels  55.9 us (25%)
  starting transfers between devices  33.5 us (15%)
  between operations  13.9 us (6%)
  other arithmetic  6.56 us (3%)
  local copies, waits for them, and re-layouts  6.14 us (3%)
    all_gather x1, waiting for transfers between devices, on_device(): lax.all_gather(jnp.concatenate([x_tokens, out_grad], axis=0), both, axis=...  58.1 us
    pallas_call x1, Pallas kernels, expert(): pl.pallas_call(functools.partial(expert_kernel, steps=steps), grid=(2 * s...  26.3 us
    all_gather x1, waiting for transfers between devices, on_device(): spread = lax.all_gather(send, 'branch', axis=0, tiled=True)  25.8 us
    all_to_all x3, starting transfers between devices, exchange(): return lax.all_to_all(value, axis, split_axis=0, concat_axis=0, tiled=True)  23.2 us
    ppermute x3, waiting for transfers between devices, on_device(): second.append(lax.ppermute(sums[distance], both, pairs))  12.8 us
    pallas_call x1, Pallas kernels, pick_rows(): pl.pallas_call(pick_kernel, grid=(steps,), in_specs=[pl.BlockSpec((1, tok...  11.9 us
    all_to_all x3, waiting for transfers between devices, exchange(): return lax.all_to_all(value, axis, split_axis=0, concat_axis=0, tiled=True)  10.6 us
    pallas_call x1, Pallas kernels, weight_grads(): pl.pallas_call(weights_kernel, grid=(features // tile,), in_specs=[pl.Blo...  10.1 us
  transfers between devices with their start and end apart: 10, of which 5 were waited for; matrix products, arithmetic and copies ran while one was open for 5% of the time, Pallas kernels for 13%

profile of v5, /device:TPU:1, one launch (start us, length us, event | category | flops | bytes accessed | tf_op | source)
XLA Modules:
  0.0 223.4 jit_solution(117545692544668161)
XLA Ops:
  7.2 0.0 all-gather.3.cloned.1.call-start
  7.2 1.5 pad_maximum_fusion
  8.7 0.0 all-gather.3.cloned.1.call-update
  8.8 0.7 convert_element_type.32
  9.5 0.7 pad_maximum_fusion.1
  10.1 0.1 copy.48
  10.2 0.8 broadcast_in_dim.10
  11.1 11.5 %all-to-all-start = ((f32[128,8,128]{2,1,0:T(8,128)}), f32[128,8,128]{2,1,0:T(8,128)S(1)}, u32[]{:S(2)}, u32[]{:S(2)}) async-start(f32[128,8,128]{2,1,0:T(8,128)} %broadcast_in_dim.10), calls=%async_computation | async-start | bytes 1048576 | tf_op jit(solution)/shard_map/all_to_all | solution.py:316
  22.6 0.0 all-gather.5.cloned.1.call-start
  22.6 3.3 %fusion = bf16[4096,256]{1,0:T(8,128)(2,1)} fusion(bf16[1,4096,256]{2,1,0:T(8,128)(2,1)} %param.15), kind=kLoop, calls=%fused_computation.1 | loop fusion | flops 3145728 | bytes 4194304 | tf_op jit(solution)/shard_map/convert_element_type | solution.py:341
  26.0 10.6 %all-to-all-done = f32[128,8,128]{2,1,0:T(8,128)S(1)} async-done(((f32[128,8,128]{2,1,0:T(8,128)}), f32[128,8,128]{2,1,0:T(8,128)S(1)}, u32[]{:S(2)}, u32[]{:S(2)}) %all-to-all-start) | async-done | bytes 524320 | tf_op jit(solution)/shard_map/all_to_all | solution.py:316
  36.6 0.2 fusion.13
  36.8 0.2 copy.46
  37.0 0.2 copy.47
  37.3 0.1 copy.44
  37.4 0.7 reshape.186.prob_ref
  38.1 0.1 convert_reduce_fusion
  38.2 0.1 copy.42
  38.3 0.7 select_n.158.place_ref
  39.0 58.1 %all-gather.3.cloned.1.call-done = bf16[2048,4096]{1,0:T(8,128)(2,1)} async-done(((bf16[16,4096]{1,0:T(8,128)(2,1)}), bf16[2048,4096]{1,0:T(8,128)(2,1)}) %all-gather.3.cloned.1.call-update) | async-done | bytes 16777232 | tf_op jit(solution)/shard_map/all_gather | solution.py:328
  97.1 26.3 %expert.1 = (bf16[16,72,384]{2,1,0:T(8,128)(2,1)}, bf16[16,2,24,4096]{3,2,1,0:T(8,128)(2,1)}) custom-call(s32[1,1024]{1,0:T(1,128)} %select_n.158.place_ref, f32[1,1024]{1,0:T(1,128)} %reshape.186.prob_ref, bf16[128,16,4096]{2,1,0:T(8,128)(2,1)} %bitcast.14, bf16[384,4096]{1,0:T(8,128)(2,1)} %bitcast.16, bf16[384,4096]{1,0:T(8,128)(2,1)} %bitcast.17, ...), custom_call_target="tpu_custom_call" | custom-call | flops 9663676416 | bytes 34603008 | tf_op jit(solution)/shard_map/expert/pallas_call | solution.py:106
  123.4 0.0 all-gather.5.cloned.1.call-update
  123.5 5.2 %all-to-all-start.1 = ((bf16[16,2,24,4096]{3,2,1,0:T(8,128)(2,1)}), bf16[16,2,24,4096]{3,2,1,0:T(8,128)(2,1)}, u32[]{:S(2)}, u32[]{:S(2)}) async-start(bf16[16,2,24,4096]{3,2,1,0:T(8,128)(2,1)} %get-tuple-element.28), calls=%async_computation.1 | async-start | bytes 12582912 | tf_op jit(solution)/shard_map/all_to_all | solution.py:356
  128.7 0.0 reduce-scatter.2.cloned.1.call-start
  128.8 0.1 copy.45
  128.9 0.7 select_n.165.place_ref
  129.6 11.9 %pick_rows.1 = (bf16[384,4096]{1,0:T(8,128)(2,1)}, bf16[384,4096]{1,0:T(8,128)(2,1)}) custom-call(s32[1,1024]{1,0:T(1,128)} %select_n.165.place_ref, bf16[128,16,4096]{2,1,0:T(8,128)(2,1)} %bitcast.15), custom_call_target="tpu_custom_call" | custom-call | flops 6442450944 | bytes 25165824 | tf_op jit(solution)/shard_map/pick_rows/pallas_call | solution.py:154
  141.5 25.8 %all-gather.5.cloned.1.call-done = bf16[128,72,384]{2,1,0:T(8,128)(2,1)} async-done(((bf16[16,72,384]{2,1,0:T(8,128)(2,1)}), bf16[128,72,384]{2,1,0:T(8,128)(2,1)}) %all-gather.5.cloned.1.call-update) | async-done | bytes 7077904 | tf_op jit(solution)/shard_map/all_gather | solution.py:348
  167.3 0.0 reduce-scatter.2.cloned.1.call-update
  167.3 2.2 constant_dynamic-slice_fusion
  169.5 0.0 all-to-all-done.1
  169.5 6.7 %all-to-all-start.3 = ((bf16[16,72,384]{2,1,0:T(8,128)(2,1)}), bf16[16,72,384]{2,1,0:T(8,128)(2,1)S(1)}, u32[]{:S(2)}, u32[]{:S(2)}) async-start(bf16[16,72,384]{2,1,0:T(8,128)(2,1)} %bitcast.7), calls=%async_computation.4 | async-start | bytes 1769472 | tf_op jit(solution)/shard_map/all_to_all | solution.py:316
  176.2 0.0 copy-start.1
  176.2 4.3 %first_sum.1 = (bf16[2,24,4096]{2,1,0:T(8,128)(2,1)S(1)}, bf16[2,24,4096]{2,1,0:T(8,128)(2,1)S(1)}, bf16[2,24,4096]{2,1,0:T(8,128)(2,1)S(1)}, bf16[2,24,4096]{2,1,0:T(8,128)(2,1)S(1)}) custom-call(s32[1]{0:T(128)} %bitcast.position_ref, bf16[4,4,2,24,4096]{4,3,2,1,0:T(8,128)(2,1)} %bitcast.8.got_ref), custom_call_target="tpu_custom_call" | custom-call | tf_op jit(solution)/shard_map/first_sum/pallas_call | solution.py:182
  180.5 1.4 collective-permute-start
  181.9 2.4 %collective-permute-start.1 = (bf16[2,24,4096]{2,1,0:T(8,128)(2,1)S(1)}, bf16[2,24,4096]{2,1,0:T(8,128)(2,1)S(1)}, u32[]{:S(2)}, u32[]{:S(2)}) collective-permute-start(bf16[2,24,4096]{2,1,0:T(8,128)(2,1)S(1)} %get-tuple-element.37), channel_id=1, source_target_pairs={{0,2},{1,3},{2,0},{3,1},{4,6},{5,7},{6,4},{7,5},{8,10},{9,11},{10,... | collective-permute-start | bytes 1179656 | tf_op jit(solution)/shard_map/ppermute | solution.py:377
  184.3 1.2 collective-permute-start.2
  185.5 0.1 convert_reduce_fusion.2
  185.6 8.3 %collective-permute-done.refs_1_ = bf16[2,24,4096]{2,1,0:T(8,128)(2,1)S(1)} collective-permute-done((bf16[2,24,4096]{2,1,0:T(8,128)(2,1)S(1)}, bf16[2,24,4096]{2,1,0:T(8,128)(2,1)S(1)}, u32[]{:S(2)}, u32[]{:S(2)}) %collective-permute-start) | collective-permute-done | bytes 393248 | tf_op jit(solution)/shard_map/ppermute | solution.py:377
  193.9 4.5 %collective-permute-done.1.refs_2_ = bf16[2,24,4096]{2,1,0:T(8,128)(2,1)S(1)} collective-permute-done((bf16[2,24,4096]{2,1,0:T(8,128)(2,1)S(1)}, bf16[2,24,4096]{2,1,0:T(8,128)(2,1)S(1)}, u32[]{:S(2)}, u32[]{:S(2)}) %collective-permute-start.1) | collective-permute-done | bytes 393248 | tf_op jit(solution)/shard_map/ppermute | solution.py:377
  198.4 0.0 collective-permute-done.2.refs_3_
  198.4 1.8 gather_blocks.1
  200.2 0.0 all-to-all-done.3.lhs_ref
  200.2 5.0 %all-to-all-start.2 = ((bf16[8,8,4096]{2,1,0:T(8,128)(2,1)}), bf16[8,8,4096]{2,1,0:T(8,128)(2,1)S(1)}, u32[]{:S(2)}, u32[]{:S(2)}) async-start(bf16[8,8,4096]{2,1,0:T(8,128)(2,1)} %gather_blocks.1), calls=%async_computation.2 | async-start | bytes 1048576 | tf_op jit(solution)/shard_map/all_to_all | solution.py:316
  205.2 0.1 fusion.2.chosen_ref
  205.3 10.1 %weight_grads.1 = (bf16[384,4096]{1,0:T(8,128)(2,1)}, bf16[384,4096]{1,0:T(8,128)(2,1)}, bf16[384,4096]{1,0:T(8,128)(2,1)}) custom-call(bf16[16,72,384]{2,1,0:T(8,128)(2,1)} %copy-done, bf16[384,4096]{1,0:T(8,128)(2,1)} %get-tuple-element.43.x_ref, bf16[384,4096]{1,0:T(8,128)(2,1)} %get-tuple-element.44.g_ref), custom_call_target="tpu_custom_call" | custom-call | flops 3623878656 | bytes 16777216 | tf_op jit(solution)/shard_map/weight_grads/pallas_call | solution.py:273
  215.3 0.0 all-to-all-done.2.got_ref
  215.3 1.5 combine.1
  (13 shorter events, 0.1 us)
Async XLA Ops:
  7.2 90.0 %all-gather.3.cloned.1.call-start = ((), (), s32[]{:S(2)}) async-start(), calls=%async_computation.5 | async-start | bytes 16908288 | tf_op jit(solution)/shard_map/all_gather | solution.py:328
  11.1 25.6 %all-to-all-start = ((f32[128,8,128]{2,1,0:T(8,128)}), f32[128,8,128]{2,1,0:T(8,128)S(1)}, u32[]{:S(2)}, u32[]{:S(2)}) async-start(f32[128,8,128]{2,1,0:T(8,128)} %broadcast_in_dim.10), calls=%async_computation | async-start | bytes 1048576 | tf_op jit(solution)/shard_map/all_to_all | solution.py:316
  22.6 144.7 %all-gather.5.cloned.1.call-start = ((), (), s32[]{:S(2)}) async-start(), calls=%async_computation.6 | async-start | bytes 7962624 | tf_op jit(solution)/shard_map/all_gather | solution.py:348
  123.5 46.0 %all-to-all-start.1 = ((bf16[16,2,24,4096]{3,2,1,0:T(8,128)(2,1)}), bf16[16,2,24,4096]{3,2,1,0:T(8,128)(2,1)}, u32[]{:S(2)}, u32[]{:S(2)}) async-start(bf16[16,2,24,4096]{3,2,1,0:T(8,128)(2,1)} %get-tuple-element.28), calls=%async_computation.1 | async-start | bytes 12582912 | tf_op jit(solution)/shard_map/all_to_all | solution.py:356
  128.7 88.2 %reduce-scatter.2.cloned.1.call-start = ((), (), s32[]{:S(2)}) async-start(), calls=%async_computation.7 | async-start | bytes 2359296 | tf_op jit(solution)/shard_map/reduce_scatter | solution.py:354
  169.5 30.7 %all-to-all-start.3 = ((bf16[16,72,384]{2,1,0:T(8,128)(2,1)}), bf16[16,72,384]{2,1,0:T(8,128)(2,1)S(1)}, u32[]{:S(2)}, u32[]{:S(2)}) async-start(bf16[16,72,384]{2,1,0:T(8,128)(2,1)} %bitcast.7), calls=%async_computation.4 | async-start | bytes 1769472 | tf_op jit(solution)/shard_map/all_to_all | solution.py:316
  176.2 9.3 %copy-start.1 = (s32[8,2]{0,1:T(2,128)S(1)}, s32[8,2]{0,1:T(2,128)}, u32[]{:S(2)}) copy-start(s32[8,2]{0,1:T(2,128)} %param.10) | copy-start | bytes 196
  180.5 13.4 %collective-permute-start = (bf16[2,24,4096]{2,1,0:T(8,128)(2,1)S(1)}, bf16[2,24,4096]{2,1,0:T(8,128)(2,1)S(1)}, u32[]{:S(2)}, u32[]{:S(2)}) collective-permute-start(bf16[2,24,4096]{2,1,0:T(8,128)(2,1)S(1)} %get-tuple-element.36), channel_id=1, source_target_pairs={{0,1},{1,2},{2,3},{3,0},{4,5},{5,6},{6,7},{7,4},{8,9},{9,10},{10,1... | collective-permute-start | bytes 1179656 | tf_op jit(solution)/shard_map/ppermute | solution.py:377
  181.9 16.5 %collective-permute-start.1 = (bf16[2,24,4096]{2,1,0:T(8,128)(2,1)S(1)}, bf16[2,24,4096]{2,1,0:T(8,128)(2,1)S(1)}, u32[]{:S(2)}, u32[]{:S(2)}) collective-permute-start(bf16[2,24,4096]{2,1,0:T(8,128)(2,1)S(1)} %get-tuple-element.37), channel_id=1, source_target_pairs={{0,2},{1,3},{2,0},{3,1},{4,6},{5,7},{6,4},{7,5},{8,10},{9,11},{10,... | collective-permute-start | bytes 1179656 | tf_op jit(solution)/shard_map/ppermute | solution.py:377
  184.3 14.1 %collective-permute-start.2 = (bf16[2,24,4096]{2,1,0:T(8,128)(2,1)S(1)}, bf16[2,24,4096]{2,1,0:T(8,128)(2,1)S(1)}, u32[]{:S(2)}, u32[]{:S(2)}) collective-permute-start(bf16[2,24,4096]{2,1,0:T(8,128)(2,1)S(1)} %get-tuple-element.38), channel_id=1, source_target_pairs={{0,3},{1,0},{2,1},{3,2},{4,7},{5,4},{6,5},{7,6},{8,11},{9,8},{10,9... | collective-permute-start | bytes 1179656 | tf_op jit(solution)/shard_map/ppermute | solution.py:377
  200.2 5.0 %copy-start = (bf16[16,72,384]{2,1,0:T(8,128)(2,1)}, bf16[16,72,384]{2,1,0:T(8,128)(2,1)S(1)}, u32[]{:S(2)}) copy-start(bf16[16,72,384]{2,1,0:T(8,128)(2,1)S(1)} %all-to-all-done.3.lhs_ref) | copy-start | bytes 2654212
  200.2 15.1 %all-to-all-start.2 = ((bf16[8,8,4096]{2,1,0:T(8,128)(2,1)}), bf16[8,8,4096]{2,1,0:T(8,128)(2,1)S(1)}, u32[]{:S(2)}, u32[]{:S(2)}) async-start(bf16[8,8,4096]{2,1,0:T(8,128)(2,1)} %gather_blocks.1), calls=%async_computation.2 | async-start | bytes 1048576 | tf_op jit(solution)/shard_map/all_to_all | solution.py:316
Sparse Core Ops, SparseCore 0:
  11.7 85.3 all-gather.2
  123.6 43.6 all-gather.4
  170.3 30.8 reduce-scatter.1

commit v6 on v5

--- a/solution.py
+++ b/solution.py
@@ -33,12 +33,12 @@
 
 
 def expert_kernel(
-    place_ref, prob_ref, rows_ref, wg_ref, wu_ref, wd_ref,
-    send_ref, back_ref,
-    pair_acc, hg_acc, acts, kept, *, steps,
+    position_ref, place_ref, prob_ref, rows_ref, wg_ref, wu_ref, wd_ref, send_ref, *refs, steps
 ):
+    back_refs, (pair_acc, hg_acc, flat, acts, kept) = refs[:-5], refs[-5:]
     step = pl.program_id(0)
     slots = acts.shape[1]
+    chunk = slots // len(back_refs)
 
     @pl.when(step < steps)
     def _():
@@ -77,7 +77,11 @@
         turned = []
         for n, value in enumerate(values):
             got = lax.dot_general(value.astype(BF16), pick, LAST, preferred_element_type=F32)
-            acts[n] = got.T.astype(BF16)
+            flat[...] = got.T.astype(BF16)
+            for distance in range(len(back_refs)):
+                member = lax.rem(position_ref[0] + distance, len(back_refs))
+                rows = pl.ds(pl.multiple_of(member * chunk, chunk), chunk)
+                acts[n, distance * chunk : (distance + 1) * chunk] = flat[rows]
             turned.append(got.reshape(pieces, height, slots))
         send_ref[...] = jnp.concatenate(turned, axis=1).astype(BF16)
 
@@ -88,12 +92,14 @@
         grad = jnp.dot(acts[0], kept[tile, 0], preferred_element_type=F32) + jnp.dot(
             acts[1], kept[tile, 1], preferred_element_type=F32
         )
-        wide, _, height, width = back_ref.shape
-        back_ref[:, 0] = out.reshape(wide, height, width).astype(BF16)
-        back_ref[:, 1] = grad.reshape(wide, height, width).astype(BF16)
-
-
-def expert(place, prob, rows, wg, wu, wd, pieces):
+        for distance, ref in enumerate(back_refs):
+            count, _, height, width = ref.shape
+            for o, value in enumerate((out, grad)):
+                part = value[distance * chunk : (distance + 1) * chunk]
+                ref[:, o] = part.reshape(count, height, width).astype(BF16)
+
+
+def expert(position, place, prob, rows, wg, wu, wd, pieces):
     blocks, per_block, features = rows.shape
     hidden = wg.shape[0]
     slots = blocks * CAP
@@ -107,23 +113,28 @@
         functools.partial(expert_kernel, steps=steps),
         grid=(2 * steps,),
         in_specs=[
-            line, line,
+            pl.BlockSpec(memory_space=pltpu.SMEM), line, line,
             pl.BlockSpec((blocks, per_block, tile), lambda i: (0, 0, jnp.minimum(i, steps - 1))),
             wspec, wspec, wspec,
         ],
         out_specs=[
             pl.BlockSpec((pieces, stacked, slots), lambda i: (0, 0, 0)),
+        ]
+        + [
             pl.BlockSpec(
-                (pieces, 2, slots // pieces, tile), lambda i: (0, 0, 0, jnp.maximum(i - steps, 0))
-            ),
-        ],
+                (pieces // SIDE, 2, slots // pieces, tile),
+                lambda i: (0, 0, 0, jnp.maximum(i - steps, 0)),
+            )
+        ]
+        * SIDE,
         out_shape=[
             jax.ShapeDtypeStruct((pieces, stacked, slots), BF16),
-            jax.ShapeDtypeStruct((pieces, 2, slots // pieces, features), BF16),
-        ],
+        ]
+        + [jax.ShapeDtypeStruct((pieces // SIDE, 2, slots // pieces, features), BF16)] * SIDE,
         scratch_shapes=[
             pltpu.VMEM((2 * hidden, tokens), F32),
             pltpu.VMEM((hidden, tokens), F32),
+            pltpu.VMEM((slots, hidden), BF16),
             pltpu.VMEM((3, slots, hidden), BF16),
             pltpu.VMEM((steps, 3, hidden, tile), BF16),
         ],
@@ -134,7 +145,7 @@
             transcendentals=tokens * hidden,
         ),
         name="expert",
-    )(place, prob, rows, wg, wu, wd)
+    )(position, place, prob, rows, wg, wu, wd)
 
 
 def pick_kernel(place_ref, rows_ref, x_ref, g_ref):
@@ -168,15 +179,16 @@
     )(place, rows)
 
 
-def first_sum_kernel(position_ref, got_ref, *refs):
-    total, outs = refs[-1], refs[:-1]
-    total[...] = jnp.sum(got_ref[...].astype(F32), axis=0)
+def first_sum_kernel(position_ref, *refs):
+    half = len(refs) // 2
+    total, outs = refs[-1], refs[half:-1]
+    total[...] = sum(ref[...].astype(F32) for ref in refs[:half])
     for distance, ref in enumerate(outs):
         ref[...] = total[lax.rem(position_ref[0] + distance, len(outs))].astype(BF16)
 
 
 def first_sum(position, got):
-    parts, _, _, height, features = got.shape
+    parts, _, height, features = got[0].shape
     steps = 4
     tile = features // steps
     return pl.pallas_call(
@@ -184,14 +196,14 @@
         grid=(steps,),
         in_specs=[
             pl.BlockSpec(memory_space=pltpu.SMEM),
-            pl.BlockSpec((parts, parts, 2, height, tile), lambda i: (0, 0, 0, 0, i)),
-        ],
+        ]
+        + [pl.BlockSpec((parts, 2, height, tile), lambda i: (0, 0, 0, i))] * parts,
         out_specs=[pl.BlockSpec((2, height, tile), lambda i: (0, 0, i))] * parts,
         out_shape=[jax.ShapeDtypeStruct((2, height, features), BF16)] * parts,
         scratch_shapes=[pltpu.VMEM((parts, 2, height, tile), F32)],
         compiler_params=SMALL,
         name="first_sum",
-    )(position, got)
+    )(position, *got)
 
 
 def gather_kernel(*refs):
@@ -341,40 +353,37 @@
     scaled = (attn_out[0].astype(F32) * (1.0 / experts)).astype(BF16)
     gathered, scaled = lax.optimization_barrier((gathered, scaled))
 
-    send, back = expert(
-        place, weight.reshape(1, -1), gathered, w_gate[0], w_up[0], w_down[0], wide
-    )
-
-    spread = lax.all_gather(send, "branch", axis=0, tiled=True)
+    slow, fast = wide_index // SIDE, wide_index % SIDE
+    even = branch_index % 2 == 0
+    position_one = jnp.where(even, slow, fast).astype(jnp.int32).reshape(1)
+    position_two = jnp.where(even, fast, slow).astype(jnp.int32).reshape(1)
+
+    send, *chunks = expert(
+        position_one,
+        place,
+        weight.reshape(1, -1),
+        gathered,
+        w_gate[0],
+        w_up[0],
+        w_down[0],
+        wide,
+    )
+
+    def deliver(parts, odd):
+        groups = stage_groups(experts, wide, odd)
+        got = [parts[0]]
+        for distance in range(1, SIDE):
+            pairs = [(g[n], g[(n + distance) % SIDE]) for g in groups for n in range(SIDE)]
+            got.append(lax.ppermute(parts[distance], both, pairs))
+        return got
+
+    first = deliver(chunks, 0)
+    mine = exchange(send, "branch")
     xe, ge = pick_rows(other_place, gathered)
-    spread, scaled, xe, ge = lax.optimization_barrier((spread, scaled, xe, ge))
-    spread = spread.reshape((experts, wide) + send.shape[1:])
-    copies = wide // experts
-    mine = lax.dynamic_slice_in_dim(spread, branch_index * copies, copies, 1)
+    first, mine, scaled, xe, ge = lax.optimization_barrier((first, mine, scaled, xe, ge))
     merged_attn = lax.psum_scatter(scaled, "branch", scatter_dimension=0, tiled=True)
-
-    first = lax.all_to_all(
-        back,
-        both,
-        split_axis=0,
-        concat_axis=0,
-        axis_index_groups=stage_groups(experts, wide, 0),
-        tiled=True,
-    )
-    first, mine = lax.optimization_barrier((first, mine.reshape(send.shape)))
     relayed = exchange(mine, "wide")
-    position = jnp.where(branch_index % 2 == 0, wide_index % SIDE, wide_index // SIDE)
-    sums = first_sum(
-        position.astype(jnp.int32).reshape(1), first.reshape((SIDE, SIDE) + back.shape[1:])
-    )
-    second = [sums[0]]
-    for distance in range(1, SIDE):
-        pairs = [
-            (group[n], group[(n + distance) % SIDE])
-            for group in stage_groups(experts, wide, 1)
-            for n in range(SIDE)
-        ]
-        second.append(lax.ppermute(sums[distance], both, pairs))
+    second = deliver(first_sum(position_two, first), 1)
     returned = gather_blocks(second, experts)
     grad_gate, grad_up, grad_down = weight_grads(relayed, xe, ge)
     got = exchange(returned, "branch")

time: 224 us -> 219 us (0.978)
  waiting for transfers between devices: 107 us -> 98.6 us
  starting transfers between devices: 33.5 us -> 38.2 us
    all_gather x1 -> x0, waiting for transfers between devices: 25.8 us -> none  [on_device(): spread = lax.all_gather(send, 'branch', axis=0, tiled=True)]
    ppermute x3 -> x6, waiting for transfers between devices: 12.8 us -> 28.5 us  [deliver(): got.append(lax.ppermute(parts[distance], both, pairs))]
    all_to_all x3 -> x4, starting transfers between devices: 23.2 us -> 28.7 us  [exchange(): return lax.all_to_all(value, axis, split_axis=0, concat_axis=0, tiled=True)]
    all_to_all x1 -> x0, starting transfers between devices: 5.25 us -> none  [on_device(): lax.all_to_all(back, both, split_axis=0, concat_axis=0, axis_index_groups...]
    ppermute x3 -> x6, starting transfers between devices: 4.99 us -> 9.43 us  [deliver(): got.append(lax.ppermute(parts[distance], both, pairs))]
    all_to_all x3 -> x4, waiting for transfers between devices: 10.6 us -> 11.9 us  [exchange(): return lax.all_to_all(value, axis, split_axis=0, concat_axis=0, tiled=True)]
  transfers between devices with their start and end apart: 10 -> 12, of which waited for: 5 -> 6; matrix products, arithmetic and copies ran while one was open for 5% -> 4% of each run, Pallas kernels for 13% -> 13%
where the time goes in v6:
time: 219 us; the launch traced here: 218 us
  waiting for transfers between devices  98.6 us (45%)
  Pallas kernels  56.2 us (26%)
  starting transfers between devices  38.2 us (17%)
  between operations  14.2 us (6%)
  other arithmetic  6.58 us (3%)
  local copies, waits for them, and re-layouts  3.95 us (2%)
    all_gather x1, waiting for transfers between devices, on_device(): lax.all_gather(jnp.concatenate([x_tokens, out_grad], axis=0), both, axis=...  58.1 us
    all_to_all x4, starting transfers between devices, exchange(): return lax.all_to_all(value, axis, split_axis=0, concat_axis=0, tiled=True)  28.7 us
    ppermute x6, waiting for transfers between devices, deliver(): got.append(lax.ppermute(parts[distance], both, pairs))  28.5 us
    pallas_call x1, Pallas kernels, expert(): pl.pallas_call(functools.partial(expert_kernel, steps=steps), grid=(2 * s...  27.8 us
    all_to_all x4, waiting for transfers between devices, exchange(): return lax.all_to_all(value, axis, split_axis=0, concat_axis=0, tiled=True)  11.9 us
    pallas_call x1, Pallas kernels, pick_rows(): pl.pallas_call(pick_kernel, grid=(steps,), in_specs=[pl.BlockSpec((1, tok...  11.4 us
    pallas_call x1, Pallas kernels, weight_grads(): pl.pallas_call(weights_kernel, grid=(features // tile,), in_specs=[pl.Blo...  10.1 us
    ppermute x6, starting transfers between devices, deliver(): got.append(lax.ppermute(parts[distance], both, pairs))  9.43 us
  transfers between devices with their start and end apart: 12, of which 6 were waited for; matrix products, arithmetic and copies ran while one was open for 4% of the time, Pallas kernels for 13%

profile of v6, /device:TPU:1, one launch (start us, length us, event | category | flops | bytes accessed | tf_op | source)
XLA Modules:
  0.0 217.7 jit_solution(4192419702226603106)
XLA Ops:
  7.2 0.0 all-gather.2.cloned.1.call-start
  7.2 1.5 pad_maximum_fusion
  8.7 0.0 all-gather.2.cloned.1.call-update
  8.8 0.7 convert_element_type.32
  9.5 0.7 pad_maximum_fusion.1
  10.1 0.1 copy.46
  10.2 0.8 broadcast_in_dim.10
  11.1 11.5 %all-to-all-start = ((f32[128,8,128]{2,1,0:T(8,128)}), f32[128,8,128]{2,1,0:T(8,128)S(1)}, u32[]{:S(2)}, u32[]{:S(2)}) async-start(f32[128,8,128]{2,1,0:T(8,128)} %broadcast_in_dim.10), calls=%async_computation | async-start | bytes 1048576 | tf_op jit(solution)/shard_map/all_to_all | solution.py:328
  22.6 3.3 %fusion = bf16[4096,256]{1,0:T(8,128)(2,1)} fusion(bf16[1,4096,256]{2,1,0:T(8,128)(2,1)} %param.15), kind=kLoop, calls=%fused_computation.1 | loop fusion | flops 3145728 | bytes 4194304 | tf_op jit(solution)/shard_map/convert_element_type | solution.py:353
  26.0 10.7 %all-to-all-done = f32[128,8,128]{2,1,0:T(8,128)S(1)} async-done(((f32[128,8,128]{2,1,0:T(8,128)}), f32[128,8,128]{2,1,0:T(8,128)S(1)}, u32[]{:S(2)}, u32[]{:S(2)}) %all-to-all-start) | async-done | bytes 524320 | tf_op jit(solution)/shard_map/all_to_all | solution.py:328
  36.6 0.2 fusion.13
  36.8 0.2 copy.44
  37.0 0.2 copy.45
  37.3 0.1 convert_reduce_fusion
  37.4 0.1 copy.40
  37.5 0.7 select_n.159.place_ref
  38.2 0.1 copy.42
  38.3 0.7 reshape.181.prob_ref
  39.0 58.1 %all-gather.2.cloned.1.call-done = bf16[2048,4096]{1,0:T(8,128)(2,1)} async-done(((bf16[16,4096]{1,0:T(8,128)(2,1)}), bf16[2048,4096]{1,0:T(8,128)(2,1)}) %all-gather.2.cloned.1.call-update) | async-done | bytes 16777232 | tf_op jit(solution)/shard_map/all_gather | solution.py:340
  97.1 27.8 %expert.1 = (bf16[16,72,384]{2,1,0:T(8,128)(2,1)}, bf16[4,2,24,4096]{3,2,1,0:T(8,128)(2,1)}, bf16[4,2,24,4096]{3,2,1,0:T(8,128)(2,1)}, bf16[4,2,24,4096]{3,2,1,0:T(8,128)(2,1)}, bf16[4,2,24,4096]{3,2,1,0:T(8,128)(2,1)}) custom-call(s32[1]{0:T(128)} %bitcast.1.position_ref, s32[1,1024]{1,0:T(1,128)} %select_n.159.place_ref, f32[1,1024]{1,0:T(1,128)} %reshape.181.prob_ref, ...), custom_call_target="tpu_custom_call" | custom-call | flops 9663676416 | bytes 34603008 | tf_op jit(solution)/shard_map/expert/pallas_call | solution.py:112
  124.9 0.8 collective-permute-start
  125.7 2.6 %collective-permute-start.1 = (bf16[4,2,24,4096]{3,2,1,0:T(8,128)(2,1)}, bf16[4,2,24,4096]{3,2,1,0:T(8,128)(2,1)}, u32[]{:S(2)}, u32[]{:S(2)}) collective-permute-start(bf16[4,2,24,4096]{3,2,1,0:T(8,128)(2,1)} %get-tuple-element.35), channel_id=1, source_target_pairs={{0,8},{4,12},{8,0},{12,4},{1,9},{5,13},{9,1},{13,5},{2,10},{6,14},... | collective-permute-start | bytes 4718600 | tf_op jit(solution)/shard_map/ppermute | solution.py:377
  128.3 1.1 collective-permute-start.2
  129.4 5.7 %all-to-all-start.1 = ((bf16[16,72,384]{2,1,0:T(8,128)(2,1)}), bf16[16,72,384]{2,1,0:T(8,128)(2,1)}, u32[]{:S(2)}, u32[]{:S(2)}) async-start(bf16[16,72,384]{2,1,0:T(8,128)(2,1)} %get-tuple-element.37), calls=%async_computation.1 | async-start | bytes 1769472 | tf_op jit(solution)/shard_map/all_to_all | solution.py:328
  135.1 0.1 copy.43
  135.2 0.7 select_n.166.place_ref
  135.8 11.4 %pick_rows.1 = (bf16[384,4096]{1,0:T(8,128)(2,1)}, bf16[384,4096]{1,0:T(8,128)(2,1)}) custom-call(s32[1,1024]{1,0:T(1,128)} %select_n.166.place_ref, bf16[128,16,4096]{2,1,0:T(8,128)(2,1)} %bitcast.12), custom_call_target="tpu_custom_call" | custom-call | flops 6442450944 | bytes 25165824 | tf_op jit(solution)/shard_map/pick_rows/pallas_call | solution.py:165
  147.3 1.2 all-to-all-done.1
  148.5 15.1 %collective-permute-done.1.refs_2_ = bf16[4,2,24,4096]{3,2,1,0:T(8,128)(2,1)} collective-permute-done((bf16[4,2,24,4096]{3,2,1,0:T(8,128)(2,1)}, bf16[4,2,24,4096]{3,2,1,0:T(8,128)(2,1)}, u32[]{:S(2)}, u32[]{:S(2)}) %collective-permute-start.1) | collective-permute-done | bytes 1572896 | tf_op jit(solution)/shard_map/ppermute | solution.py:377
  163.6 0.0 collective-permute-done.2.refs_3_
  163.6 0.0 reduce-scatter.2.cloned.1.call-update
  163.6 6.2 %all-to-all-start.3 = ((bf16[16,72,384]{2,1,0:T(8,128)(2,1)}), bf16[16,72,384]{2,1,0:T(8,128)(2,1)}, u32[]{:S(2)}, u32[]{:S(2)}) async-start(bf16[16,72,384]{2,1,0:T(8,128)(2,1)} %all-to-all-done.1), calls=%async_computation.4 | async-start | bytes 1769472 | tf_op jit(solution)/shard_map/all_to_all | solution.py:328
  169.8 0.0 copy-start.1
  169.8 3.7 %first_sum.1 = (bf16[2,24,4096]{2,1,0:T(8,128)(2,1)S(1)}, bf16[2,24,4096]{2,1,0:T(8,128)(2,1)S(1)}, bf16[2,24,4096]{2,1,0:T(8,128)(2,1)S(1)}, bf16[2,24,4096]{2,1,0:T(8,128)(2,1)S(1)}) custom-call(s32[1]{0:T(128)} %bitcast.position_ref, bf16[4,2,24,4096]{3,2,1,0:T(8,128)(2,1)S(1)} %copy-done, bf16[4,2,24,4096]{3,2,1,0:T(8,128)(2,1)S(1)} %collective-permute-done.refs_1_, ...), custom_call_target="tpu_custom_call" | custom-call | tf_op jit(solution)/shard_map/first_sum/pallas_call | solution.py:194
  173.5 1.4 collective-permute-start.3
  174.9 2.4 %collective-permute-start.4 = (bf16[2,24,4096]{2,1,0:T(8,128)(2,1)S(1)}, bf16[2,24,4096]{2,1,0:T(8,128)(2,1)S(1)}, u32[]{:S(2)}, u32[]{:S(2)}) collective-permute-start(bf16[2,24,4096]{2,1,0:T(8,128)(2,1)S(1)} %get-tuple-element.47), channel_id=1, source_target_pairs={{0,2},{1,3},{2,0},{3,1},{4,6},{5,7},{6,4},{7,5},{8,10},{9,11},{10,... | collective-permute-start | bytes 1179656 | tf_op jit(solution)/shard_map/ppermute | solution.py:377
  177.3 1.2 collective-permute-start.5
  178.5 0.1 convert_reduce_fusion.2
  178.6 8.9 %collective-permute-done.3.refs_1_ = bf16[2,24,4096]{2,1,0:T(8,128)(2,1)S(1)} collective-permute-done((bf16[2,24,4096]{2,1,0:T(8,128)(2,1)S(1)}, bf16[2,24,4096]{2,1,0:T(8,128)(2,1)S(1)}, u32[]{:S(2)}, u32[]{:S(2)}) %collective-permute-start.3) | collective-permute-done | bytes 393248 | tf_op jit(solution)/shard_map/ppermute | solution.py:377
  187.5 4.6 %collective-permute-done.4.refs_2_ = bf16[2,24,4096]{2,1,0:T(8,128)(2,1)S(1)} collective-permute-done((bf16[2,24,4096]{2,1,0:T(8,128)(2,1)S(1)}, bf16[2,24,4096]{2,1,0:T(8,128)(2,1)S(1)}, u32[]{:S(2)}, u32[]{:S(2)}) %collective-permute-start.4) | collective-permute-done | bytes 393248 | tf_op jit(solution)/shard_map/ppermute | solution.py:377
  192.1 0.0 collective-permute-done.5.refs_3_
  192.1 1.8 gather_blocks.1
  193.8 0.0 all-to-all-done.3.lhs_ref
  193.8 5.4 %all-to-all-start.2 = ((bf16[8,8,4096]{2,1,0:T(8,128)(2,1)}), bf16[8,8,4096]{2,1,0:T(8,128)(2,1)S(1)}, u32[]{:S(2)}, u32[]{:S(2)}) async-start(bf16[8,8,4096]{2,1,0:T(8,128)(2,1)} %gather_blocks.1), calls=%async_computation.2 | async-start | bytes 1048576 | tf_op jit(solution)/shard_map/all_to_all | solution.py:328
  199.2 0.1 fusion.2.chosen_ref
  199.3 10.1 %weight_grads.1 = (bf16[384,4096]{1,0:T(8,128)(2,1)}, bf16[384,4096]{1,0:T(8,128)(2,1)}, bf16[384,4096]{1,0:T(8,128)(2,1)}) custom-call(bf16[16,72,384]{2,1,0:T(8,128)(2,1)} %all-to-all-done.3.lhs_ref, bf16[384,4096]{1,0:T(8,128)(2,1)} %get-tuple-element.53.x_ref, bf16[384,4096]{1,0:T(8,128)(2,1)} %get-tuple-element.54.g_ref), custom_call_target="tpu_custom_call" | custom-call | flops 3623878656 | bytes 16777216 | tf_op jit(solution)/shard_map/weight_grads/pallas_call | solution.py:285
  209.4 0.0 all-to-all-done.2.got_ref
  209.4 1.5 combine.1
  (15 shorter events, 0.1 us)
Async XLA Ops:
  7.2 90.0 %all-gather.2.cloned.1.call-start = ((), (), s32[]{:S(2)}) async-start(), calls=%async_computation.5 | async-start | bytes 16908288 | tf_op jit(solution)/shard_map/all_gather | solution.py:340
  11.1 25.6 %all-to-all-start = ((f32[128,8,128]{2,1,0:T(8,128)}), f32[128,8,128]{2,1,0:T(8,128)S(1)}, u32[]{:S(2)}, u32[]{:S(2)}) async-start(f32[128,8,128]{2,1,0:T(8,128)} %broadcast_in_dim.10), calls=%async_computation | async-start | bytes 1048576 | tf_op jit(solution)/shard_map/all_to_all | solution.py:328
  124.9 23.6 %collective-permute-start = (bf16[4,2,24,4096]{3,2,1,0:T(8,128)(2,1)}, bf16[4,2,24,4096]{3,2,1,0:T(8,128)(2,1)S(1)}, u32[]{:S(2)}, u32[]{:S(2)}) collective-permute-start(bf16[4,2,24,4096]{3,2,1,0:T(8,128)(2,1)} %get-tuple-element.34), channel_id=1, source_target_pairs={{0,4},{4,8},{8,12},{12,0},{1,5},{5,9},{9,13},{13,1},{2,6},{6,10},{... | collective-permute-start | bytes 4718600 | tf_op jit(solution)/shard_map/ppermute | solution.py:377
  125.7 37.8 %collective-permute-start.1 = (bf16[4,2,24,4096]{3,2,1,0:T(8,128)(2,1)}, bf16[4,2,24,4096]{3,2,1,0:T(8,128)(2,1)}, u32[]{:S(2)}, u32[]{:S(2)}) collective-permute-start(bf16[4,2,24,4096]{3,2,1,0:T(8,128)(2,1)} %get-tuple-element.35), channel_id=1, source_target_pairs={{0,8},{4,12},{8,0},{12,4},{1,9},{5,13},{9,1},{13,5},{2,10},{6,14},... | collective-permute-start | bytes 4718600 | tf_op jit(solution)/shard_map/ppermute | solution.py:377
  128.3 35.3 %collective-permute-start.2 = (bf16[4,2,24,4096]{3,2,1,0:T(8,128)(2,1)}, bf16[4,2,24,4096]{3,2,1,0:T(8,128)(2,1)}, u32[]{:S(2)}, u32[]{:S(2)}) collective-permute-start(bf16[4,2,24,4096]{3,2,1,0:T(8,128)(2,1)} %get-tuple-element.36), channel_id=1, source_target_pairs={{0,12},{4,0},{8,4},{12,8},{1,13},{5,1},{9,5},{13,9},{2,14},{6,2},{... | collective-permute-start | bytes 4718600 | tf_op jit(solution)/shard_map/ppermute | solution.py:377
  129.4 19.1 %all-to-all-start.1 = ((bf16[16,72,384]{2,1,0:T(8,128)(2,1)}), bf16[16,72,384]{2,1,0:T(8,128)(2,1)}, u32[]{:S(2)}, u32[]{:S(2)}) async-start(bf16[16,72,384]{2,1,0:T(8,128)(2,1)} %get-tuple-element.37), calls=%async_computation.1 | async-start | bytes 1769472 | tf_op jit(solution)/shard_map/all_to_all | solution.py:328
  135.1 75.8 %reduce-scatter.2.cloned.1.call-start = ((), (), s32[]{:S(2)}) async-start(), calls=%async_computation.6 | async-start | bytes 2359296 | tf_op jit(solution)/shard_map/reduce_scatter | solution.py:384
  147.2 22.6 %copy-start = (bf16[4,2,24,4096]{3,2,1,0:T(8,128)(2,1)S(1)}, bf16[4,2,24,4096]{3,2,1,0:T(8,128)(2,1)}, u32[]{:S(2)}) copy-start(bf16[4,2,24,4096]{3,2,1,0:T(8,128)(2,1)} %get-tuple-element.41.refs_0_) | copy-start | bytes 4718596
  163.6 30.3 %all-to-all-start.3 = ((bf16[16,72,384]{2,1,0:T(8,128)(2,1)}), bf16[16,72,384]{2,1,0:T(8,128)(2,1)}, u32[]{:S(2)}, u32[]{:S(2)}) async-start(bf16[16,72,384]{2,1,0:T(8,128)(2,1)} %all-to-all-done.1), calls=%async_computation.4 | async-start | bytes 1769472 | tf_op jit(solution)/shard_map/all_to_all | solution.py:328
  169.8 8.7 %copy-start.1 = (s32[8,2]{0,1:T(2,128)S(1)}, s32[8,2]{0,1:T(2,128)}, u32[]{:S(2)}) copy-start(s32[8,2]{0,1:T(2,128)} %param.10) | copy-start | bytes 196
  173.5 13.9 %collective-permute-start.3 = (bf16[2,24,4096]{2,1,0:T(8,128)(2,1)S(1)}, bf16[2,24,4096]{2,1,0:T(8,128)(2,1)S(1)}, u32[]{:S(2)}, u32[]{:S(2)}) collective-permute-start(bf16[2,24,4096]{2,1,0:T(8,128)(2,1)S(1)} %get-tuple-element.46), channel_id=1, source_target_pairs={{0,1},{1,2},{2,3},{3,0},{4,5},{5,6},{6,7},{7,4},{8,9},{9,10},{10,1... | collective-permute-start | bytes 1179656 | tf_op jit(solution)/shard_map/ppermute | solution.py:377
  174.9 17.2 %collective-permute-start.4 = (bf16[2,24,4096]{2,1,0:T(8,128)(2,1)S(1)}, bf16[2,24,4096]{2,1,0:T(8,128)(2,1)S(1)}, u32[]{:S(2)}, u32[]{:S(2)}) collective-permute-start(bf16[2,24,4096]{2,1,0:T(8,128)(2,1)S(1)} %get-tuple-element.47), channel_id=1, source_target_pairs={{0,2},{1,3},{2,0},{3,1},{4,6},{5,7},{6,4},{7,5},{8,10},{9,11},{10,... | collective-permute-start | bytes 1179656 | tf_op jit(solution)/shard_map/ppermute | solution.py:377
  177.3 14.8 %collective-permute-start.5 = (bf16[2,24,4096]{2,1,0:T(8,128)(2,1)S(1)}, bf16[2,24,4096]{2,1,0:T(8,128)(2,1)S(1)}, u32[]{:S(2)}, u32[]{:S(2)}) collective-permute-start(bf16[2,24,4096]{2,1,0:T(8,128)(2,1)S(1)} %get-tuple-element.48), channel_id=1, source_target_pairs={{0,3},{1,0},{2,1},{3,2},{4,7},{5,4},{6,5},{7,6},{8,11},{9,8},{10,9... | collective-permute-start | bytes 1179656 | tf_op jit(solution)/shard_map/ppermute | solution.py:377
  193.8 15.5 %all-to-all-start.2 = ((bf16[8,8,4096]{2,1,0:T(8,128)(2,1)}), bf16[8,8,4096]{2,1,0:T(8,128)(2,1)S(1)}, u32[]{:S(2)}, u32[]{:S(2)}) async-start(bf16[8,8,4096]{2,1,0:T(8,128)(2,1)} %gather_blocks.1), calls=%async_computation.2 | async-start | bytes 1048576 | tf_op jit(solution)/shard_map/all_to_all | solution.py:328
Sparse Core Ops, SparseCore 0:
  11.7 85.3 all-gather.1
  163.7 31.8 reduce-scatter.1

commit v7 on v6

--- a/solution.py
+++ b/solution.py
@@ -40,6 +40,11 @@
     slots = acts.shape[1]
     chunk = slots // len(back_refs)
 
+    @pl.when(step == 0)
+    def _():
+        pair_acc[...] = jnp.zeros_like(pair_acc)
+        hg_acc[...] = jnp.zeros_like(hg_acc)
+
     @pl.when(step < steps)
     def _():
         x, g = split_rows(rows_ref)
@@ -47,15 +52,7 @@
             kept[step, n] = w_ref[...]
         pair = jnp.concatenate([wg_ref[...], wu_ref[...]], axis=0)
         for acc, w, rhs in ((pair_acc, pair, x), (hg_acc, wd_ref[...], g)):
-            part = lax.dot_general(w, rhs, LAST, preferred_element_type=F32)
-
-            @pl.when(step == 0)
-            def _(acc=acc, part=part):
-                acc[...] = part
-
-            @pl.when(step > 0)
-            def _(acc=acc, part=part):
-                acc[...] += part
+            acc[...] += lax.dot_general(w, rhs, LAST, preferred_element_type=F32)
 
     @pl.when(step == steps)
     def _():

time: 219 us -> 216 us (0.986)
  Pallas kernels: 56.2 us -> 53.5 us
    pallas_call x1, Pallas kernels: 27.8 us -> 25 us  [expert(): pl.pallas_call(functools.partial(expert_kernel, steps=steps), grid=(2 * s...]
where the time goes in v7:
time: 216 us; the launch traced here: 215 us
  waiting for transfers between devices  98.6 us (46%)
  Pallas kernels  53.5 us (25%)
  starting transfers between devices  38.2 us (18%)
  between operations  14.2 us (7%)
  other arithmetic  6.58 us (3%)
  local copies, waits for them, and re-layouts  3.95 us (2%)
    all_gather x1, waiting for transfers between devices, on_device(): lax.all_gather(jnp.concatenate([x_tokens, out_grad], axis=0), both, axis=...  58.1 us
    all_to_all x4, starting transfers between devices, exchange(): return lax.all_to_all(value, axis, split_axis=0, concat_axis=0, tiled=True)  28.7 us
    ppermute x6, waiting for transfers between devices, deliver(): got.append(lax.ppermute(parts[distance], both, pairs))  28.5 us
    pallas_call x1, Pallas kernels, expert(): pl.pallas_call(functools.partial(expert_kernel, steps=steps), grid=(2 * s...  25 us
    all_to_all x4, waiting for transfers between devices, exchange(): return lax.all_to_all(value, axis, split_axis=0, concat_axis=0, tiled=True)  11.9 us
    pallas_call x1, Pallas kernels, pick_rows(): pl.pallas_call(pick_kernel, grid=(steps,), in_specs=[pl.BlockSpec((1, tok...  11.4 us
    pallas_call x1, Pallas kernels, weight_grads(): pl.pallas_call(weights_kernel, grid=(features // tile,), in_specs=[pl.Blo...  10.1 us
    ppermute x6, starting transfers between devices, deliver(): got.append(lax.ppermute(parts[distance], both, pairs))  9.45 us
  transfers between devices with their start and end apart: 12, of which 6 were waited for; matrix products, arithmetic and copies ran while one was open for 4% of the time, Pallas kernels for 13%

profile of v7, /device:TPU:1, one launch (start us, length us, event | category | flops | bytes accessed | tf_op | source)
XLA Modules:
  0.0 215.0 jit_solution(3980401002907291381)
XLA Ops:
  7.2 0.0 all-gather.2.cloned.1.call-start
  7.2 1.5 pad_maximum_fusion
  8.7 0.0 all-gather.2.cloned.1.call-update
  8.8 0.7 convert_element_type.32
  9.5 0.7 pad_maximum_fusion.1
  10.1 0.1 copy.46
  10.2 0.8 broadcast_in_dim.10
  11.1 11.5 %all-to-all-start = ((f32[128,8,128]{2,1,0:T(8,128)}), f32[128,8,128]{2,1,0:T(8,128)S(1)}, u32[]{:S(2)}, u32[]{:S(2)}) async-start(f32[128,8,128]{2,1,0:T(8,128)} %broadcast_in_dim.10), calls=%async_computation | async-start | bytes 1048576 | tf_op jit(solution)/shard_map/all_to_all | solution.py:325
  22.6 3.3 %fusion = bf16[4096,256]{1,0:T(8,128)(2,1)} fusion(bf16[1,4096,256]{2,1,0:T(8,128)(2,1)} %param.15), kind=kLoop, calls=%fused_computation.1 | loop fusion | flops 3145728 | bytes 4194304 | tf_op jit(solution)/shard_map/convert_element_type | solution.py:350
  26.0 10.7 %all-to-all-done = f32[128,8,128]{2,1,0:T(8,128)S(1)} async-done(((f32[128,8,128]{2,1,0:T(8,128)}), f32[128,8,128]{2,1,0:T(8,128)S(1)}, u32[]{:S(2)}, u32[]{:S(2)}) %all-to-all-start) | async-done | bytes 524320 | tf_op jit(solution)/shard_map/all_to_all | solution.py:325
  36.6 0.2 fusion.13
  36.8 0.2 copy.44
  37.0 0.2 copy.45
  37.3 0.1 convert_reduce_fusion
  37.4 0.1 copy.40
  37.5 0.7 select_n.159.place_ref
  38.2 0.1 copy.42
  38.3 0.7 reshape.181.prob_ref
  39.0 58.1 %all-gather.2.cloned.1.call-done = bf16[2048,4096]{1,0:T(8,128)(2,1)} async-done(((bf16[16,4096]{1,0:T(8,128)(2,1)}), bf16[2048,4096]{1,0:T(8,128)(2,1)}) %all-gather.2.cloned.1.call-update) | async-done | bytes 16777232 | tf_op jit(solution)/shard_map/all_gather | solution.py:337
  97.1 25.0 %expert.1 = (bf16[16,72,384]{2,1,0:T(8,128)(2,1)}, bf16[4,2,24,4096]{3,2,1,0:T(8,128)(2,1)}, bf16[4,2,24,4096]{3,2,1,0:T(8,128)(2,1)}, bf16[4,2,24,4096]{3,2,1,0:T(8,128)(2,1)}, bf16[4,2,24,4096]{3,2,1,0:T(8,128)(2,1)}) custom-call(s32[1]{0:T(128)} %bitcast.1.position_ref, s32[1,1024]{1,0:T(1,128)} %select_n.159.place_ref, f32[1,1024]{1,0:T(1,128)} %reshape.181.prob_ref, ...), custom_call_target="tpu_custom_call" | custom-call | flops 9663676416 | bytes 34603008 | tf_op jit(solution)/shard_map/expert/pallas_call | solution.py:109
  122.1 0.8 collective-permute-start
  122.9 2.6 %collective-permute-start.1 = (bf16[4,2,24,4096]{3,2,1,0:T(8,128)(2,1)}, bf16[4,2,24,4096]{3,2,1,0:T(8,128)(2,1)}, u32[]{:S(2)}, u32[]{:S(2)}) collective-permute-start(bf16[4,2,24,4096]{3,2,1,0:T(8,128)(2,1)} %get-tuple-element.35), channel_id=1, source_target_pairs={{0,8},{4,12},{8,0},{12,4},{1,9},{5,13},{9,1},{13,5},{2,10},{6,14},... | collective-permute-start | bytes 4718600 | tf_op jit(solution)/shard_map/ppermute | solution.py:374
  125.5 1.1 collective-permute-start.2
  126.6 5.7 %all-to-all-start.1 = ((bf16[16,72,384]{2,1,0:T(8,128)(2,1)}), bf16[16,72,384]{2,1,0:T(8,128)(2,1)}, u32[]{:S(2)}, u32[]{:S(2)}) async-start(bf16[16,72,384]{2,1,0:T(8,128)(2,1)} %get-tuple-element.37), calls=%async_computation.1 | async-start | bytes 1769472 | tf_op jit(solution)/shard_map/all_to_all | solution.py:325
  132.3 0.1 copy.43
  132.4 0.7 select_n.166.place_ref
  133.1 11.4 %pick_rows.1 = (bf16[384,4096]{1,0:T(8,128)(2,1)}, bf16[384,4096]{1,0:T(8,128)(2,1)}) custom-call(s32[1,1024]{1,0:T(1,128)} %select_n.166.place_ref, bf16[128,16,4096]{2,1,0:T(8,128)(2,1)} %bitcast.12), custom_call_target="tpu_custom_call" | custom-call | flops 6442450944 | bytes 25165824 | tf_op jit(solution)/shard_map/pick_rows/pallas_call | solution.py:162
  144.5 1.2 all-to-all-done.1
  145.7 0.0 collective-permute-done.refs_1_
  145.7 15.0 %collective-permute-done.1.refs_2_ = bf16[4,2,24,4096]{3,2,1,0:T(8,128)(2,1)} collective-permute-done((bf16[4,2,24,4096]{3,2,1,0:T(8,128)(2,1)}, bf16[4,2,24,4096]{3,2,1,0:T(8,128)(2,1)}, u32[]{:S(2)}, u32[]{:S(2)}) %collective-permute-start.1) | collective-permute-done | bytes 1572896 | tf_op jit(solution)/shard_map/ppermute | solution.py:374
  160.8 0.0 collective-permute-done.2.refs_3_
  160.8 0.0 reduce-scatter.2.cloned.1.call-update
  160.8 6.2 %all-to-all-start.3 = ((bf16[16,72,384]{2,1,0:T(8,128)(2,1)}), bf16[16,72,384]{2,1,0:T(8,128)(2,1)}, u32[]{:S(2)}, u32[]{:S(2)}) async-start(bf16[16,72,384]{2,1,0:T(8,128)(2,1)} %all-to-all-done.1), calls=%async_computation.4 | async-start | bytes 1769472 | tf_op jit(solution)/shard_map/all_to_all | solution.py:325
  167.0 0.0 copy-start.1
  167.0 3.7 %first_sum.1 = (bf16[2,24,4096]{2,1,0:T(8,128)(2,1)S(1)}, bf16[2,24,4096]{2,1,0:T(8,128)(2,1)S(1)}, bf16[2,24,4096]{2,1,0:T(8,128)(2,1)S(1)}, bf16[2,24,4096]{2,1,0:T(8,128)(2,1)S(1)}) custom-call(s32[1]{0:T(128)} %bitcast.position_ref, bf16[4,2,24,4096]{3,2,1,0:T(8,128)(2,1)S(1)} %copy-done, bf16[4,2,24,4096]{3,2,1,0:T(8,128)(2,1)S(1)} %collective-permute-done.refs_1_, ...), custom_call_target="tpu_custom_call" | custom-call | tf_op jit(solution)/shard_map/first_sum/pallas_call | solution.py:191
  170.8 1.4 collective-permute-start.3
  172.1 2.4 %collective-permute-start.4 = (bf16[2,24,4096]{2,1,0:T(8,128)(2,1)S(1)}, bf16[2,24,4096]{2,1,0:T(8,128)(2,1)S(1)}, u32[]{:S(2)}, u32[]{:S(2)}) collective-permute-start(bf16[2,24,4096]{2,1,0:T(8,128)(2,1)S(1)} %get-tuple-element.47), channel_id=1, source_target_pairs={{0,2},{1,3},{2,0},{3,1},{4,6},{5,7},{6,4},{7,5},{8,10},{9,11},{10,... | collective-permute-start | bytes 1179656 | tf_op jit(solution)/shard_map/ppermute | solution.py:374
  174.5 1.2 collective-permute-start.5
  175.7 0.1 convert_reduce_fusion.2
  175.8 8.9 %collective-permute-done.3.refs_1_ = bf16[2,24,4096]{2,1,0:T(8,128)(2,1)S(1)} collective-permute-done((bf16[2,24,4096]{2,1,0:T(8,128)(2,1)S(1)}, bf16[2,24,4096]{2,1,0:T(8,128)(2,1)S(1)}, u32[]{:S(2)}, u32[]{:S(2)}) %collective-permute-start.3) | collective-permute-done | bytes 393248 | tf_op jit(solution)/shard_map/ppermute | solution.py:374
  184.7 4.6 %collective-permute-done.4.refs_2_ = bf16[2,24,4096]{2,1,0:T(8,128)(2,1)S(1)} collective-permute-done((bf16[2,24,4096]{2,1,0:T(8,128)(2,1)S(1)}, bf16[2,24,4096]{2,1,0:T(8,128)(2,1)S(1)}, u32[]{:S(2)}, u32[]{:S(2)}) %collective-permute-start.4) | collective-permute-done | bytes 393248 | tf_op jit(solution)/shard_map/ppermute | solution.py:374
  189.3 0.0 collective-permute-done.5.refs_3_
  189.3 1.8 gather_blocks.1
  191.1 0.0 all-to-all-done.3.lhs_ref
  191.1 5.3 %all-to-all-start.2 = ((bf16[8,8,4096]{2,1,0:T(8,128)(2,1)}), bf16[8,8,4096]{2,1,0:T(8,128)(2,1)S(1)}, u32[]{:S(2)}, u32[]{:S(2)}) async-start(bf16[8,8,4096]{2,1,0:T(8,128)(2,1)} %gather_blocks.1), calls=%async_computation.2 | async-start | bytes 1048576 | tf_op jit(solution)/shard_map/all_to_all | solution.py:325
  196.4 0.1 fusion.2.chosen_ref
  196.5 10.1 %weight_grads.1 = (bf16[384,4096]{1,0:T(8,128)(2,1)}, bf16[384,4096]{1,0:T(8,128)(2,1)}, bf16[384,4096]{1,0:T(8,128)(2,1)}) custom-call(bf16[16,72,384]{2,1,0:T(8,128)(2,1)} %all-to-all-done.3.lhs_ref, bf16[384,4096]{1,0:T(8,128)(2,1)} %get-tuple-element.53.x_ref, bf16[384,4096]{1,0:T(8,128)(2,1)} %get-tuple-element.54.g_ref), custom_call_target="tpu_custom_call" | custom-call | flops 3623878656 | bytes 16777216 | tf_op jit(solution)/shard_map/weight_grads/pallas_call | solution.py:282
  206.6 1.5 combine.1
  (15 shorter events, 0.1 us)
Async XLA Ops:
  7.2 90.0 %all-gather.2.cloned.1.call-start = ((), (), s32[]{:S(2)}) async-start(), calls=%async_computation.5 | async-start | bytes 16908288 | tf_op jit(solution)/shard_map/all_gather | solution.py:337
  11.1 25.6 %all-to-all-start = ((f32[128,8,128]{2,1,0:T(8,128)}), f32[128,8,128]{2,1,0:T(8,128)S(1)}, u32[]{:S(2)}, u32[]{:S(2)}) async-start(f32[128,8,128]{2,1,0:T(8,128)} %broadcast_in_dim.10), calls=%async_computation | async-start | bytes 1048576 | tf_op jit(solution)/shard_map/all_to_all | solution.py:325
  122.1 23.6 %collective-permute-start = (bf16[4,2,24,4096]{3,2,1,0:T(8,128)(2,1)}, bf16[4,2,24,4096]{3,2,1,0:T(8,128)(2,1)S(1)}, u32[]{:S(2)}, u32[]{:S(2)}) collective-permute-start(bf16[4,2,24,4096]{3,2,1,0:T(8,128)(2,1)} %get-tuple-element.34), channel_id=1, source_target_pairs={{0,4},{4,8},{8,12},{12,0},{1,5},{5,9},{9,13},{13,1},{2,6},{6,10},{... | collective-permute-start | bytes 4718600 | tf_op jit(solution)/shard_map/ppermute | solution.py:374
  122.9 37.8 %collective-permute-start.1 = (bf16[4,2,24,4096]{3,2,1,0:T(8,128)(2,1)}, bf16[4,2,24,4096]{3,2,1,0:T(8,128)(2,1)}, u32[]{:S(2)}, u32[]{:S(2)}) collective-permute-start(bf16[4,2,24,4096]{3,2,1,0:T(8,128)(2,1)} %get-tuple-element.35), channel_id=1, source_target_pairs={{0,8},{4,12},{8,0},{12,4},{1,9},{5,13},{9,1},{13,5},{2,10},{6,14},... | collective-permute-start | bytes 4718600 | tf_op jit(solution)/shard_map/ppermute | solution.py:374
  125.5 35.3 %collective-permute-start.2 = (bf16[4,2,24,4096]{3,2,1,0:T(8,128)(2,1)}, bf16[4,2,24,4096]{3,2,1,0:T(8,128)(2,1)}, u32[]{:S(2)}, u32[]{:S(2)}) collective-permute-start(bf16[4,2,24,4096]{3,2,1,0:T(8,128)(2,1)} %get-tuple-element.36), channel_id=1, source_target_pairs={{0,12},{4,0},{8,4},{12,8},{1,13},{5,1},{9,5},{13,9},{2,14},{6,2},{... | collective-permute-start | bytes 4718600 | tf_op jit(solution)/shard_map/ppermute | solution.py:374
  126.6 19.1 %all-to-all-start.1 = ((bf16[16,72,384]{2,1,0:T(8,128)(2,1)}), bf16[16,72,384]{2,1,0:T(8,128)(2,1)}, u32[]{:S(2)}, u32[]{:S(2)}) async-start(bf16[16,72,384]{2,1,0:T(8,128)(2,1)} %get-tuple-element.37), calls=%async_computation.1 | async-start | bytes 1769472 | tf_op jit(solution)/shard_map/all_to_all | solution.py:325
  132.3 75.8 %reduce-scatter.2.cloned.1.call-start = ((), (), s32[]{:S(2)}) async-start(), calls=%async_computation.6 | async-start | bytes 2359296 | tf_op jit(solution)/shard_map/reduce_scatter | solution.py:381
  144.5 22.5 %copy-start = (bf16[4,2,24,4096]{3,2,1,0:T(8,128)(2,1)S(1)}, bf16[4,2,24,4096]{3,2,1,0:T(8,128)(2,1)}, u32[]{:S(2)}) copy-start(bf16[4,2,24,4096]{3,2,1,0:T(8,128)(2,1)} %get-tuple-element.41.refs_0_) | copy-start | bytes 4718596
  160.8 30.3 %all-to-all-start.3 = ((bf16[16,72,384]{2,1,0:T(8,128)(2,1)}), bf16[16,72,384]{2,1,0:T(8,128)(2,1)}, u32[]{:S(2)}, u32[]{:S(2)}) async-start(bf16[16,72,384]{2,1,0:T(8,128)(2,1)} %all-to-all-done.1), calls=%async_computation.4 | async-start | bytes 1769472 | tf_op jit(solution)/shard_map/all_to_all | solution.py:325
  167.0 8.7 %copy-start.1 = (s32[8,2]{0,1:T(2,128)S(1)}, s32[8,2]{0,1:T(2,128)}, u32[]{:S(2)}) copy-start(s32[8,2]{0,1:T(2,128)} %param.10) | copy-start | bytes 196
  170.8 13.9 %collective-permute-start.3 = (bf16[2,24,4096]{2,1,0:T(8,128)(2,1)S(1)}, bf16[2,24,4096]{2,1,0:T(8,128)(2,1)S(1)}, u32[]{:S(2)}, u32[]{:S(2)}) collective-permute-start(bf16[2,24,4096]{2,1,0:T(8,128)(2,1)S(1)} %get-tuple-element.46), channel_id=1, source_target_pairs={{0,1},{1,2},{2,3},{3,0},{4,5},{5,6},{6,7},{7,4},{8,9},{9,10},{10,1... | collective-permute-start | bytes 1179656 | tf_op jit(solution)/shard_map/ppermute | solution.py:374
  172.1 17.2 %collective-permute-start.4 = (bf16[2,24,4096]{2,1,0:T(8,128)(2,1)S(1)}, bf16[2,24,4096]{2,1,0:T(8,128)(2,1)S(1)}, u32[]{:S(2)}, u32[]{:S(2)}) collective-permute-start(bf16[2,24,4096]{2,1,0:T(8,128)(2,1)S(1)} %get-tuple-element.47), channel_id=1, source_target_pairs={{0,2},{1,3},{2,0},{3,1},{4,6},{5,7},{6,4},{7,5},{8,10},{9,11},{10,... | collective-permute-start | bytes 1179656 | tf_op jit(solution)/shard_map/ppermute | solution.py:374
  174.5 14.8 %collective-permute-start.5 = (bf16[2,24,4096]{2,1,0:T(8,128)(2,1)S(1)}, bf16[2,24,4096]{2,1,0:T(8,128)(2,1)S(1)}, u32[]{:S(2)}, u32[]{:S(2)}) collective-permute-start(bf16[2,24,4096]{2,1,0:T(8,128)(2,1)S(1)} %get-tuple-element.48), channel_id=1, source_target_pairs={{0,3},{1,0},{2,1},{3,2},{4,7},{5,4},{6,5},{7,6},{8,11},{9,8},{10,9... | collective-permute-start | bytes 1179656 | tf_op jit(solution)/shard_map/ppermute | solution.py:374
  191.1 15.5 %all-to-all-start.2 = ((bf16[8,8,4096]{2,1,0:T(8,128)(2,1)}), bf16[8,8,4096]{2,1,0:T(8,128)(2,1)S(1)}, u32[]{:S(2)}, u32[]{:S(2)}) async-start(bf16[8,8,4096]{2,1,0:T(8,128)(2,1)} %gather_blocks.1), calls=%async_computation.2 | async-start | bytes 1048576 | tf_op jit(solution)/shard_map/all_to_all | solution.py:325
Sparse Core Ops, SparseCore 0:
  11.7 85.3 all-gather.1
  160.9 31.7 reduce-scatter.1

commit v8 on v7

--- a/solution.py
+++ b/solution.py
@@ -379,8 +379,9 @@
     xe, ge = pick_rows(other_place, gathered)
     first, mine, scaled, xe, ge = lax.optimization_barrier((first, mine, scaled, xe, ge))
     merged_attn = lax.psum_scatter(scaled, "branch", scatter_dimension=0, tiled=True)
+    sums, mine = lax.optimization_barrier((first_sum(position_two, first), mine))
     relayed = exchange(mine, "wide")
-    second = deliver(first_sum(position_two, first), 1)
+    second = deliver(sums, 1)
     returned = gather_blocks(second, experts)
     grad_gate, grad_up, grad_down = weight_grads(relayed, xe, ge)
     got = exchange(returned, "branch")

time: 216 us -> 221 us (1.023)
  waiting for transfers between devices: 98.6 us -> 102 us
  local copies, waits for them, and re-layouts: 3.95 us -> 6.18 us
    ppermute x6, waiting for transfers between devices: 28.5 us -> 32.3 us  [deliver(): got.append(lax.ppermute(parts[distance], both, pairs))]
    unnamed x7 -> x15, local copies, waits for them, and re-layouts: 0.53 us -> 2.76 us
where the time goes in v8:
time: 221 us
  waiting for transfers between devices  102 us (46%)
  Pallas kernels  53.4 us (24%)
  starting transfers between devices  37.9 us (17%)
  between operations  14.2 us (6%)
  other arithmetic  6.56 us (3%)
  local copies, waits for them, and re-layouts  6.18 us (3%)
    all_gather x1, waiting for transfers between devices, on_device(): lax.all_gather(jnp.concatenate([x_tokens, out_grad], axis=0), both, axis=...  58.1 us
    ppermute x6, waiting for transfers between devices, deliver(): got.append(lax.ppermute(parts[distance], both, pairs))  32.3 us
    all_to_all x4, starting transfers between devices, exchange(): return lax.all_to_all(value, axis, split_axis=0, concat_axis=0, tiled=True)  28.4 us
    pallas_call x1, Pallas kernels, expert(): pl.pallas_call(functools.partial(expert_kernel, steps=steps), grid=(2 * s...  25 us
    all_to_all x4, waiting for transfers between devices, exchange(): return lax.all_to_all(value, axis, split_axis=0, concat_axis=0, tiled=True)  11.9 us
    pallas_call x1, Pallas kernels, pick_rows(): pl.pallas_call(pick_kernel, grid=(steps,), in_specs=[pl.BlockSpec((1, tok...  11.4 us
    pallas_call x1, Pallas kernels, weight_grads(): pl.pallas_call(weights_kernel, grid=(features // tile,), in_specs=[pl.Blo...  10.1 us
    ppermute x6, starting transfers between devices, deliver(): got.append(lax.ppermute(parts[distance], both, pairs))  9.46 us
  transfers between devices with their start and end apart: 12, of which 6 were waited for; matrix products, arithmetic and copies ran while one was open for 4% of the time, Pallas kernels for 13%

profile of v8, /device:TPU:1, one launch (start us, length us, event | category | flops | bytes accessed | tf_op | source)
XLA Modules:
  0.0 220.7 jit_solution(2027508360166432182)
XLA Ops:
  7.2 0.0 all-gather.2.cloned.1.call-start
  7.2 1.5 pad_maximum_fusion
  8.7 0.0 all-gather.2.cloned.1.call-update
  8.8 0.7 convert_element_type.32
  9.5 0.7 pad_maximum_fusion.1
  10.1 0.1 copy.46
  10.2 0.8 broadcast_in_dim.10
  11.1 11.5 %all-to-all-start = ((f32[128,8,128]{2,1,0:T(8,128)}), f32[128,8,128]{2,1,0:T(8,128)S(1)}, u32[]{:S(2)}, u32[]{:S(2)}) async-start(f32[128,8,128]{2,1,0:T(8,128)} %broadcast_in_dim.10), calls=%async_computation | async-start | bytes 1048576 | tf_op jit(solution)/shard_map/all_to_all | solution.py:325
  22.6 3.3 %fusion = bf16[4096,256]{1,0:T(8,128)(2,1)} fusion(bf16[1,4096,256]{2,1,0:T(8,128)(2,1)} %param.15), kind=kLoop, calls=%fused_computation.1 | loop fusion | flops 3145728 | bytes 4194304 | tf_op jit(solution)/shard_map/convert_element_type | solution.py:350
  25.9 10.7 %all-to-all-done = f32[128,8,128]{2,1,0:T(8,128)S(1)} async-done(((f32[128,8,128]{2,1,0:T(8,128)}), f32[128,8,128]{2,1,0:T(8,128)S(1)}, u32[]{:S(2)}, u32[]{:S(2)}) %all-to-all-start) | async-done | bytes 524320 | tf_op jit(solution)/shard_map/all_to_all | solution.py:325
  36.6 0.2 fusion.13
  36.8 0.2 copy.44
  37.0 0.2 copy.45
  37.3 0.1 convert_reduce_fusion
  37.4 0.1 copy.40
  37.5 0.7 select_n.159.place_ref
  38.2 0.1 copy.42
  38.3 0.7 reshape.181.prob_ref
  39.0 58.1 %all-gather.2.cloned.1.call-done = bf16[2048,4096]{1,0:T(8,128)(2,1)} async-done(((bf16[16,4096]{1,0:T(8,128)(2,1)}), bf16[2048,4096]{1,0:T(8,128)(2,1)}) %all-gather.2.cloned.1.call-update) | async-done | bytes 16777232 | tf_op jit(solution)/shard_map/all_gather | solution.py:337
  97.1 25.0 %expert.1 = (bf16[16,72,384]{2,1,0:T(8,128)(2,1)}, bf16[4,2,24,4096]{3,2,1,0:T(8,128)(2,1)}, bf16[4,2,24,4096]{3,2,1,0:T(8,128)(2,1)}, bf16[4,2,24,4096]{3,2,1,0:T(8,128)(2,1)}, bf16[4,2,24,4096]{3,2,1,0:T(8,128)(2,1)}) custom-call(s32[1]{0:T(128)} %bitcast.1.position_ref, s32[1,1024]{1,0:T(1,128)} %select_n.159.place_ref, f32[1,1024]{1,0:T(1,128)} %reshape.181.prob_ref, ...), custom_call_target="tpu_custom_call" | custom-call | flops 9663676416 | bytes 34603008 | tf_op jit(solution)/shard_map/expert/pallas_call | solution.py:109
  122.1 0.8 collective-permute-start
  122.9 2.6 %collective-permute-start.1 = (bf16[4,2,24,4096]{3,2,1,0:T(8,128)(2,1)}, bf16[4,2,24,4096]{3,2,1,0:T(8,128)(2,1)}, u32[]{:S(2)}, u32[]{:S(2)}) collective-permute-start(bf16[4,2,24,4096]{3,2,1,0:T(8,128)(2,1)} %get-tuple-element.40), channel_id=1, source_target_pairs={{0,8},{4,12},{8,0},{12,4},{1,9},{5,13},{9,1},{13,5},{2,10},{6,14},... | collective-permute-start | bytes 4718600 | tf_op jit(solution)/shard_map/ppermute | solution.py:374
  125.5 1.1 collective-permute-start.2
  126.6 5.7 %all-to-all-start.1 = ((bf16[16,72,384]{2,1,0:T(8,128)(2,1)}), bf16[16,72,384]{2,1,0:T(8,128)(2,1)}, u32[]{:S(2)}, u32[]{:S(2)}) async-start(bf16[16,72,384]{2,1,0:T(8,128)(2,1)} %get-tuple-element.42), calls=%async_computation.1 | async-start | bytes 1769472 | tf_op jit(solution)/shard_map/all_to_all | solution.py:325
  132.3 0.1 copy.43
  132.4 0.7 select_n.166.place_ref
  133.1 11.4 %pick_rows.1 = (bf16[384,4096]{1,0:T(8,128)(2,1)}, bf16[384,4096]{1,0:T(8,128)(2,1)}) custom-call(s32[1,1024]{1,0:T(1,128)} %select_n.166.place_ref, bf16[128,16,4096]{2,1,0:T(8,128)(2,1)} %bitcast.12), custom_call_target="tpu_custom_call" | custom-call | flops 6442450944 | bytes 25165824 | tf_op jit(solution)/shard_map/pick_rows/pallas_call | solution.py:162
  144.5 1.3 all-to-all-done.1
  145.7 15.0 %collective-permute-done.1.refs_2_ = bf16[4,2,24,4096]{3,2,1,0:T(8,128)(2,1)} collective-permute-done((bf16[4,2,24,4096]{3,2,1,0:T(8,128)(2,1)}, bf16[4,2,24,4096]{3,2,1,0:T(8,128)(2,1)}, u32[]{:S(2)}, u32[]{:S(2)}) %collective-permute-start.1) | collective-permute-done | bytes 1572896 | tf_op jit(solution)/shard_map/ppermute | solution.py:374
  160.8 0.0 reduce-scatter.2.cloned.1.call-update
  160.8 0.0 copy-start.5
  160.8 3.7 %first_sum.1 = (bf16[2,24,4096]{2,1,0:T(8,128)(2,1)S(1)}, bf16[2,24,4096]{2,1,0:T(8,128)(2,1)S(1)}, bf16[2,24,4096]{2,1,0:T(8,128)(2,1)S(1)}, bf16[2,24,4096]{2,1,0:T(8,128)(2,1)S(1)}) custom-call(s32[1]{0:T(128)} %bitcast.position_ref, bf16[4,2,24,4096]{3,2,1,0:T(8,128)(2,1)S(1)} %copy-done, bf16[4,2,24,4096]{3,2,1,0:T(8,128)(2,1)S(1)} %collective-permute-done.refs_1_, ...), custom_call_target="tpu_custom_call" | custom-call | tf_op jit(solution)/shard_map/first_sum/pallas_call | solution.py:191
  164.5 0.0 copy-start.1
  164.5 0.7 copy-done.1
  165.3 0.7 copy-done.2
  166.0 0.7 copy-done.3
  166.8 6.2 %all-to-all-start.3 = ((bf16[16,72,384]{2,1,0:T(8,128)(2,1)}), bf16[16,72,384]{2,1,0:T(8,128)(2,1)S(1)}, u32[]{:S(2)}, u32[]{:S(2)}) async-start(bf16[16,72,384]{2,1,0:T(8,128)(2,1)} %all-to-all-done.1), calls=%async_computation.4 | async-start | bytes 1769472 | tf_op jit(solution)/shard_map/all_to_all | solution.py:325
  172.9 1.4 collective-permute-start.3
  174.3 2.4 %collective-permute-start.4 = (bf16[2,24,4096]{2,1,0:T(8,128)(2,1)}, bf16[2,24,4096]{2,1,0:T(8,128)(2,1)S(1)}, u32[]{:S(2)}, u32[]{:S(2)}) collective-permute-start(bf16[2,24,4096]{2,1,0:T(8,128)(2,1)} %copy-done.2), channel_id=1, source_target_pairs={{0,2},{1,3},{2,0},{3,1},{4,6},{5,7},{6,4},{7,5},{8,10},{9,11},{10,... | collective-permute-start | bytes 1179656 | tf_op jit(solution)/shard_map/ppermute | solution.py:374
  176.7 1.2 collective-permute-start.5
  177.9 0.1 convert_reduce_fusion.2
  178.0 12.7 %collective-permute-done.3.refs_1_ = bf16[2,24,4096]{2,1,0:T(8,128)(2,1)S(1)} collective-permute-done((bf16[2,24,4096]{2,1,0:T(8,128)(2,1)}, bf16[2,24,4096]{2,1,0:T(8,128)(2,1)S(1)}, u32[]{:S(2)}, u32[]{:S(2)}) %collective-permute-start.3) | collective-permute-done | bytes 393248 | tf_op jit(solution)/shard_map/ppermute | solution.py:374
  190.6 4.6 %collective-permute-done.4.refs_2_ = bf16[2,24,4096]{2,1,0:T(8,128)(2,1)S(1)} collective-permute-done((bf16[2,24,4096]{2,1,0:T(8,128)(2,1)}, bf16[2,24,4096]{2,1,0:T(8,128)(2,1)S(1)}, u32[]{:S(2)}, u32[]{:S(2)}) %collective-permute-start.4) | collective-permute-done | bytes 393248 | tf_op jit(solution)/shard_map/ppermute | solution.py:374
  195.2 1.8 gather_blocks.1
  197.0 5.1 %all-to-all-start.2 = ((bf16[8,8,4096]{2,1,0:T(8,128)(2,1)}), bf16[8,8,4096]{2,1,0:T(8,128)(2,1)S(1)}, u32[]{:S(2)}, u32[]{:S(2)}) async-start(bf16[8,8,4096]{2,1,0:T(8,128)(2,1)} %gather_blocks.1), calls=%async_computation.2 | async-start | bytes 1048576 | tf_op jit(solution)/shard_map/all_to_all | solution.py:325
  202.1 0.1 fusion.2.chosen_ref
  202.2 10.1 %weight_grads.1 = (bf16[384,4096]{1,0:T(8,128)(2,1)}, bf16[384,4096]{1,0:T(8,128)(2,1)}, bf16[384,4096]{1,0:T(8,128)(2,1)}) custom-call(bf16[16,72,384]{2,1,0:T(8,128)(2,1)} %copy-done.4, bf16[384,4096]{1,0:T(8,128)(2,1)} %get-tuple-element.63.x_ref, bf16[384,4096]{1,0:T(8,128)(2,1)} %get-tuple-element.64.g_ref), custom_call_target="tpu_custom_call" | custom-call | flops 3623878656 | bytes 16777216 | tf_op jit(solution)/shard_map/weight_grads/pallas_call | solution.py:282
  212.3 1.5 combine.1
  (23 shorter events, 0.1 us)
Async XLA Ops:
  7.2 90.0 %all-gather.2.cloned.1.call-start = ((), (), s32[]{:S(2)}) async-start(), calls=%async_computation.5 | async-start | bytes 16908288 | tf_op jit(solution)/shard_map/all_gather | solution.py:337
  11.1 25.6 %all-to-all-start = ((f32[128,8,128]{2,1,0:T(8,128)}), f32[128,8,128]{2,1,0:T(8,128)S(1)}, u32[]{:S(2)}, u32[]{:S(2)}) async-start(f32[128,8,128]{2,1,0:T(8,128)} %broadcast_in_dim.10), calls=%async_computation | async-start | bytes 1048576 | tf_op jit(solution)/shard_map/all_to_all | solution.py:325
  122.1 23.6 %collective-permute-start = (bf16[4,2,24,4096]{3,2,1,0:T(8,128)(2,1)}, bf16[4,2,24,4096]{3,2,1,0:T(8,128)(2,1)S(1)}, u32[]{:S(2)}, u32[]{:S(2)}) collective-permute-start(bf16[4,2,24,4096]{3,2,1,0:T(8,128)(2,1)} %get-tuple-element.39), channel_id=1, source_target_pairs={{0,4},{4,8},{8,12},{12,0},{1,5},{5,9},{9,13},{13,1},{2,6},{6,10},{... | collective-permute-start | bytes 4718600 | tf_op jit(solution)/shard_map/ppermute | solution.py:374
  122.9 37.8 %collective-permute-start.1 = (bf16[4,2,24,4096]{3,2,1,0:T(8,128)(2,1)}, bf16[4,2,24,4096]{3,2,1,0:T(8,128)(2,1)}, u32[]{:S(2)}, u32[]{:S(2)}) collective-permute-start(bf16[4,2,24,4096]{3,2,1,0:T(8,128)(2,1)} %get-tuple-element.40), channel_id=1, source_target_pairs={{0,8},{4,12},{8,0},{12,4},{1,9},{5,13},{9,1},{13,5},{2,10},{6,14},... | collective-permute-start | bytes 4718600 | tf_op jit(solution)/shard_map/ppermute | solution.py:374
  125.5 35.3 %collective-permute-start.2 = (bf16[4,2,24,4096]{3,2,1,0:T(8,128)(2,1)}, bf16[4,2,24,4096]{3,2,1,0:T(8,128)(2,1)}, u32[]{:S(2)}, u32[]{:S(2)}) collective-permute-start(bf16[4,2,24,4096]{3,2,1,0:T(8,128)(2,1)} %get-tuple-element.41), channel_id=1, source_target_pairs={{0,12},{4,0},{8,4},{12,8},{1,13},{5,1},{9,5},{13,9},{2,14},{6,2},{... | collective-permute-start | bytes 4718600 | tf_op jit(solution)/shard_map/ppermute | solution.py:374
  126.6 19.1 %all-to-all-start.1 = ((bf16[16,72,384]{2,1,0:T(8,128)(2,1)}), bf16[16,72,384]{2,1,0:T(8,128)(2,1)}, u32[]{:S(2)}, u32[]{:S(2)}) async-start(bf16[16,72,384]{2,1,0:T(8,128)(2,1)} %get-tuple-element.42), calls=%async_computation.1 | async-start | bytes 1769472 | tf_op jit(solution)/shard_map/all_to_all | solution.py:325
  132.3 81.5 %reduce-scatter.2.cloned.1.call-start = ((), (), s32[]{:S(2)}) async-start(), calls=%async_computation.6 | async-start | bytes 2359296 | tf_op jit(solution)/shard_map/reduce_scatter | solution.py:381
  144.5 16.3 %copy-start = (bf16[4,2,24,4096]{3,2,1,0:T(8,128)(2,1)S(1)}, bf16[4,2,24,4096]{3,2,1,0:T(8,128)(2,1)}, u32[]{:S(2)}) copy-start(bf16[4,2,24,4096]{3,2,1,0:T(8,128)(2,1)} %get-tuple-element.46.refs_0_) | copy-start | bytes 4718596
  160.8 17.1 %copy-start.5 = (s32[8,2]{0,1:T(2,128)S(1)}, s32[8,2]{0,1:T(2,128)}, u32[]{:S(2)}) copy-start(s32[8,2]{0,1:T(2,128)} %param.10) | copy-start | bytes 196
  164.5 0.7 copy-start.1
  165.3 0.7 copy-start.2
  166.0 0.7 copy-start.3
  166.8 30.3 %all-to-all-start.3 = ((bf16[16,72,384]{2,1,0:T(8,128)(2,1)}), bf16[16,72,384]{2,1,0:T(8,128)(2,1)S(1)}, u32[]{:S(2)}, u32[]{:S(2)}) async-start(bf16[16,72,384]{2,1,0:T(8,128)(2,1)} %all-to-all-done.1), calls=%async_computation.4 | async-start | bytes 1769472 | tf_op jit(solution)/shard_map/all_to_all | solution.py:325
  172.9 17.7 %collective-permute-start.3 = (bf16[2,24,4096]{2,1,0:T(8,128)(2,1)}, bf16[2,24,4096]{2,1,0:T(8,128)(2,1)S(1)}, u32[]{:S(2)}, u32[]{:S(2)}) collective-permute-start(bf16[2,24,4096]{2,1,0:T(8,128)(2,1)} %copy-done.3), channel_id=1, source_target_pairs={{0,1},{1,2},{2,3},{3,0},{4,5},{5,6},{6,7},{7,4},{8,9},{9,10},{10,1... | collective-permute-start | bytes 1179656 | tf_op jit(solution)/shard_map/ppermute | solution.py:374
  174.3 20.9 %collective-permute-start.4 = (bf16[2,24,4096]{2,1,0:T(8,128)(2,1)}, bf16[2,24,4096]{2,1,0:T(8,128)(2,1)S(1)}, u32[]{:S(2)}, u32[]{:S(2)}) collective-permute-start(bf16[2,24,4096]{2,1,0:T(8,128)(2,1)} %copy-done.2), channel_id=1, source_target_pairs={{0,2},{1,3},{2,0},{3,1},{4,6},{5,7},{6,4},{7,5},{8,10},{9,11},{10,... | collective-permute-start | bytes 1179656 | tf_op jit(solution)/shard_map/ppermute | solution.py:374
  176.7 18.6 %collective-permute-start.5 = (bf16[2,24,4096]{2,1,0:T(8,128)(2,1)}, bf16[2,24,4096]{2,1,0:T(8,128)(2,1)S(1)}, u32[]{:S(2)}, u32[]{:S(2)}) collective-permute-start(bf16[2,24,4096]{2,1,0:T(8,128)(2,1)} %copy-done.1), channel_id=1, source_target_pairs={{0,3},{1,0},{2,1},{3,2},{4,7},{5,4},{6,5},{7,6},{8,11},{9,8},{10,9... | collective-permute-start | bytes 1179656 | tf_op jit(solution)/shard_map/ppermute | solution.py:374
  197.0 5.2 %copy-start.4 = (bf16[16,72,384]{2,1,0:T(8,128)(2,1)}, bf16[16,72,384]{2,1,0:T(8,128)(2,1)S(1)}, u32[]{:S(2)}) copy-start(bf16[16,72,384]{2,1,0:T(8,128)(2,1)S(1)} %all-to-all-done.3.lhs_ref) | copy-start | bytes 2654212
  197.0 15.3 %all-to-all-start.2 = ((bf16[8,8,4096]{2,1,0:T(8,128)(2,1)}), bf16[8,8,4096]{2,1,0:T(8,128)(2,1)S(1)}, u32[]{:S(2)}, u32[]{:S(2)}) async-start(bf16[8,8,4096]{2,1,0:T(8,128)(2,1)} %gather_blocks.1), calls=%async_computation.2 | async-start | bytes 1048576 | tf_op jit(solution)/shard_map/all_to_all | solution.py:325
Sparse Core Ops, SparseCore 0:
  11.7 85.3 all-gather.1
  160.9 31.3 reduce-scatter.1
